TPU v7x, 32 devices: a whole 2x2x4 slice. The times are simulated.
32 devices in a mesh: cls: 4 (over y, x), rows: 8 (over z, core).
Axes of the slice: x: 2, y: 2, z: 4, core: 2. Of those that a mesh axis runs over, the one named last changes fastest.
Arguments:
- prior: bfloat16 [16384, 1000], P('rows', 'cls'), may hold values from -6 to 6
- blocks: bfloat16 [64, 24, 256, 256], P('rows'), may hold values from -0.078125 to 0.078125
- links: int32 [64, 24], P('rows'), may hold values from 0 to 15, as said below
- counts: int32 [64], P('rows'), may hold values from 1 to 24
- fetch: int32 [8, 8, 1], P('rows'), may hold values from 0 to 7
- seeds: int32 [16384], P('rows'), may hold values from -1000 to 999
- inv_temp: float32 [16384], P('rows'), may hold values from 1 to 300
Outputs:
- pseudo: bfloat16 [16384, 1000], P('rows', 'cls')
- certainty: float32 [16384], P('rows')
Inputs may be any that keep to these rules, and one draw needn't show every extreme that they name: links index a slot list of 8 own tiles followed by one tile from each index of rows in order; every one of these slots is named by some link of its index of rows. `seeds`: a negative seed marks an image without a label.
All inputs are finite; a program needn't handle non-finite values.
Results may differ from a plain program's by a relative error of at most 0.0075.
The roundings to bfloat16 on the way count: a program that leaves them out, or rounds other values in their place, can miss the bound.
Values may be sent and summed in bfloat16 or wider, within the bound.
No kernel may reach another device: no remote copies, remote signals or barrier semaphores. Data moves between devices by JAX's collectives and lax.ppermute only.
A program may use at most 192 MiB of HBM per device.

v0:
```python
import jax
import jax.numpy as jnp
from jax import lax
from jax.sharding import PartitionSpec as P

CLS = 1000


blend = 0.8


def combined_all(value, axis, combine):
    everything = jax.tree.map(lambda part: lax.all_gather(part, axis), value)
    first = jax.tree.map(lambda part: part[0], everything)

    def lap(k, so_far):
        return combine(so_far, jax.tree.map(lambda part: part[k], everything))

    return lax.fori_loop(1, lax.axis_size(axis), lap, first)


def propagate_local(column_set, blocks, slot_tiles, counts, targets):
    adjacent_blocks = column_set[slot_tiles]
    live_slots = jnp.arange(blocks.shape[1], dtype=jnp.int32)[None, :] < counts[:, None]
    adjacent_blocks = jnp.where(
        live_slots[:, :, None, None], adjacent_blocks, jnp.zeros((), jnp.bfloat16)
    )
    accumulated_sum = jnp.einsum(
        "mvfg,mvgx->mfx", blocks, adjacent_blocks, preferred_element_type=jnp.float32
    )
    return blend * accumulated_sum.reshape(targets.shape) + (1.0 - blend) * targets


def combine_stats(earlier, later):
    first_max, first_total, first_moment = earlier
    second_max, second_total, squared_moment = later
    top = jnp.maximum(first_max, second_max)
    first_scale = jnp.exp(first_max - top)
    second_scale = jnp.exp(second_max - top)
    totals = first_total * first_scale + second_total * second_scale
    moments = first_scale * (first_moment + (first_max - top) * first_total) + second_scale * (
        squared_moment + (second_max - top) * second_total
    )
    return (top, totals, moments)


def local(prior, blocks, links, counts, fetch, seeds, inv_temp):
    col_width = prior.shape[1]
    tile_rows = blocks.shape[2]
    own_tiles = blocks.shape[0]
    col_start = lax.axis_index("cls") * col_width
    targets = (
        seeds[:, None] == col_start + jnp.arange(col_width, dtype=jnp.int32)[None, :]
    ).astype(jnp.float32)
    wanted = lax.all_to_all(fetch, "rows", split_axis=1, concat_axis=0, tiled=True).reshape(-1)
    field = prior
    for rounds in range(2):
        tiled = field.reshape(own_tiles, tile_rows, col_width)
        outgoing = tiled[wanted].reshape(lax.axis_size("rows"), -1, tile_rows, col_width)
        arrived = lax.all_to_all(outgoing, "rows", split_axis=0, concat_axis=0, tiled=True)
        column_set = jnp.concatenate([tiled, arrived.reshape(-1, tile_rows, col_width)], axis=0)
        mixed = propagate_local(column_set, blocks, links, counts, targets)
        field = mixed.astype(jnp.bfloat16) if rounds == 0 else mixed
    logits = inv_temp[:, None] * field
    local_max = jnp.max(logits, axis=1)
    local_shift = logits - local_max[:, None]
    local_exponent = jnp.exp(local_shift)
    local_summary = (
        local_max,
        jnp.sum(local_exponent, axis=1),
        jnp.sum(local_exponent * local_shift, axis=1),
    )
    top, totals, moments = combined_all(local_summary, "cls", combine_stats)
    shifted = logits - top[:, None]
    expo = jnp.exp(shifted)
    pseudo = (expo / totals[:, None]).astype(jnp.bfloat16)
    certainty = 1.0 - (jnp.log(totals) - moments / totals) / jnp.log(jnp.float32(CLS))
    return (pseudo, certainty)


def solution(mesh):
    return jax.shard_map(
        local,
        mesh=mesh,
        in_specs=(
            P("rows", "cls"),
            P("rows", None, None, None),
            P("rows", None),
            P("rows"),
            P("rows", None, None),
            P("rows"),
            P("rows"),
        ),
        out_specs=(P("rows", "cls"), P("rows")),
        check_vma=False,
    )
```

profile of v0, /device:TPU:0, one launch (start us, length us, event | category | flops | bytes accessed | tf_op | source)
XLA Modules:
  0.0 203.7 jit_solution(3738892849442728917)
XLA Ops:
  0.6 0.7 copy.16
  1.4 11.7 %all_to_all.19 = s32[1,8,1]{2,0,1:T(1,128)S(1)} all-to-all(s32[1,8,1]{2,0,1:T(1,128)S(1)} %copy.16), channel_id=1, replica_groups=mesh['cls'=4,'rows'=8] {'rows'}, dimensions={1} | all-to-all | bytes 64 | tf_op jit(solution)/shard_map/all_to_all | solution.py:55
  13.3 2.9 %gather_fusion = bf16[8,256,250]{2,1,0:T(8,128)(2,1)} fusion(bf16[8,256,250]{2,1,0:T(8,128)(2,1)} %bitcast.64, s32[1024]{0:T(1024)S(1)} %pad_clamp_fusion.1), kind=kCustom, calls=%fused_computation | custom fusion | bytes 2048032 | tf_op jit(solution)/shard_map/gather | solution.py:59
  16.2 3.6 %all-to-all-start.1 = ((bf16[8,1,256,250]{3,2,1,0:T(8,128)(2,1)}), bf16[8,1,256,250]{3,2,1,0:T(8,128)(2,1)S(1)}, u32[]{:S(2)}, u32[]{:S(2)}) async-start(bf16[8,1,256,250]{3,2,1,0:T(8,128)(2,1)} %bitcast.5), calls=%async_computation.1 | async-start | bytes 2097152 | tf_op jit(solution)/shard_map/all_to_all | solution.py:60
  20.0 26.3 %all-to-all-done.1 = bf16[8,1,256,250]{3,2,1,0:T(8,128)(2,1)S(1)} async-done(((bf16[8,1,256,250]{3,2,1,0:T(8,128)(2,1)}), bf16[8,1,256,250]{3,2,1,0:T(8,128)(2,1)S(1)}, u32[]{:S(2)}, u32[]{:S(2)}) %all-to-all-start.1) | async-done | bytes 1024032 | tf_op jit(solution)/shard_map/all_to_all | solution.py:60
  46.3 1.0 copy-done.2
  47.3 1.6 pad_maximum_fusion
  48.9 11.1 %gather_fusion.1 = bf16[192,256,250]{2,1,0:T(8,128)(2,1)} fusion(bf16[16,256,250]{2,1,0:T(8,128)(2,1)S(1)} %pad_maximum_fusion, s32[1024]{0:T(1024)S(1)} %pad_clamp_fusion), kind=kCustom, calls=%fused_computation.1 | custom fusion | bytes 49152768 | tf_op jit(solution)/shard_map/gather | solution.py:23
  59.9 32.6 %copy.17 = bf16[8,24,256,250]{2,3,1,0:T(8,128)(2,1)} copy(bf16[8,24,256,250]{3,2,1,0:T(8,128)(2,1)} %bitcast.62) | data formatting | bytes 49152000 | tf_op jit(solution)/shard_map/gather | solution.py:23
  92.5 18.3 %fusion.8 = bf16[8,256,250]{1,2,0:T(8,128)(2,1)S(1)} fusion(bf16[8,24,256,256]{3,2,1,0:T(8,128)(2,1)} %param.10, bf16[8,24,256,250]{2,3,1,0:T(8,128)(2,1)} %copy.17, pred[8,24]{1,0:T(8,128)(4,1)S(1)} %iota_compare_fusion, s32[8,256]{1,0:T(8,128)S(1)} %eq.25, s32[250]{0:T(256)S(1)} %iota_add_fusion), kind=kOutput, calls=%fused_computation.21 | convolution fusion | flops 6306304000 | bytes 50775208 | tf_op jit(solution)/shard_map/mvfg,mvgx->mfx/dot_general | solution.py:28
  110.9 1.6 gather_fusion.2
  112.4 3.6 %all-to-all-start.2 = ((bf16[8,1,256,250]{2,3,1,0:T(8,128)(2,1)}), bf16[8,1,256,250]{2,3,1,0:T(8,128)(2,1)S(1)}, u32[]{:S(2)}, u32[]{:S(2)}) async-start(bf16[8,1,256,250]{2,3,1,0:T(8,128)(2,1)} %bitcast.12), calls=%async_computation.2 | async-start | bytes 2097152 | tf_op jit(solution)/shard_map/all_to_all | solution.py:60
  116.0 26.5 %all-to-all-done.2 = bf16[8,1,256,250]{2,3,1,0:T(8,128)(2,1)S(1)} async-done(((bf16[8,1,256,250]{2,3,1,0:T(8,128)(2,1)}), bf16[8,1,256,250]{2,3,1,0:T(8,128)(2,1)S(1)}, u32[]{:S(2)}, u32[]{:S(2)}) %all-to-all-start.2) | async-done | bytes 1024032 | tf_op jit(solution)/shard_map/all_to_all | solution.py:60
  142.5 1.0 copy-done.3
  143.5 1.4 pad_maximum_fusion.1
  144.9 11.1 %gather_fusion.3 = bf16[192,256,250]{1,2,0:T(8,128)(2,1)} fusion(bf16[16,256,250]{1,2,0:T(8,128)(2,1)S(1)} %pad_maximum_fusion.1, s32[1024]{0:T(1024)S(1)} %pad_clamp_fusion), kind=kCustom, calls=%fused_computation.3 | custom fusion | bytes 49152768 | tf_op jit(solution)/shard_map/gather | solution.py:23
  156.0 17.5 %fusion.21 = (f32[8,256]{1,0:T(8,128)S(1)}, f32[8,256,250]{1,2,0:T(8,128)S(1)}) fusion(f32[8,256]{1,0:T(8,128)S(1)} %mul.120, s32[8,256]{1,0:T(8,128)S(1)} %eq.25, s32[250]{0:T(256)S(1)} %iota_add_fusion, bf16[8,24,256,256]{3,2,1,0:T(8,128)(2,1)} %param.10, bf16[8,24,256,250]{2,3,1,0:T(8,128)(2,1)} %bitcast.63, pred[8,24]{1,0:T(8,128)(4,1)S(1)} %iota_compare_fusion), kind=kOutput, calls=%fused_computation.35 | convolution fusion | flops 6306813952 | bytes 51815592 | tf_op jit(solution)/shard_map/mvfg,mvgx->mfx/dot_general | solution.py:28
  173.4 0.8 fusion.10
  174.3 8.2 %all-gather.1 = f32[4,1,2048]{2,1,0:T(1,128)S(1)} all-gather(f32[1,1,2048]{2,1,0:T(1,128)S(1)} %reshape.200), channel_id=1, replica_groups=mesh['cls'=4,'rows'=8] {'cls'}, dimensions={0}, use_global_device_ids=true | all-gather | bytes 40960 | tf_op jit(solution)/shard_map/all_gather | solution.py:13
  182.5 8.2 %all-gather.2 = f32[4,1,2048]{2,1,0:T(1,128)S(1)} all-gather(f32[1,1,2048]{2,1,0:T(1,128)S(1)} %reshape.202), channel_id=1, replica_groups=mesh['cls'=4,'rows'=8] {'cls'}, dimensions={0}, use_global_device_ids=true | all-gather | bytes 40960 | tf_op jit(solution)/shard_map/all_gather | solution.py:13
  190.7 7.2 %all-gather = f32[4,1,2048]{2,1,0:T(1,128)S(1)} all-gather(f32[1,1,2048]{2,1,0:T(1,128)S(1)} %reshape.198), channel_id=1, replica_groups=mesh['cls'=4,'rows'=8] {'cls'}, dimensions={0}, use_global_device_ids=true | all-gather | bytes 40960 | tf_op jit(solution)/shard_map/all_gather | solution.py:13
  197.9 1.9 copy.19
  200.2 0.6 multiply_subtract_fusion
  200.8 2.9 %fusion.16 = bf16[2048,250]{1,0:T(8,128)(2,1)} fusion(f32[8,256,250]{2,1,0:T(8,128)S(1)} %copy.19, f32[2048]{0:T(1024)S(1)} %get-tuple-element.181, f32[2048]{0:T(1024)S(1)} %get-tuple-element.180, s32[250]{0:T(256)S(1)} %iota_add_fusion, f32[2048]{0:T(1024)S(1)} %copy-done.4, s32[2048]{0:T(1024)S(1)} %copy-done.5), kind=kLoop, calls=%fused_computation.34 | loop fusion | flops 3584000 | bytes 3105768 | tf_op jit(solution)/shard_map/convert_element_type | solution.py:76
  (49 shorter events, 1.1 us)
Async XLA Ops:
  13.3 6.5 %copy-start.6 = (s32[8,24]{1,0:T(8,128)S(1)}, s32[8,24]{1,0:T(8,128)}, u32[]{:S(2)}) copy-start(s32[8,24]{1,0:T(8,128)} %param.11) | copy-start | bytes 2308
  13.3 6.6 %copy-start.5 = (s32[2048]{0:T(1024)S(1)}, s32[2048]{0:T(1024)}, u32[]{:S(2)}) copy-start(s32[2048]{0:T(1024)} %param.14) | copy-start | bytes 24580
  13.3 6.6 %copy-start.7 = (s32[8]{0:T(128)S(1)}, s32[8]{0:T(128)}, u32[]{:S(2)}) copy-start(s32[8]{0:T(128)} %param.12) | copy-start | bytes 100
  13.3 34.0 %copy-start.1 = (bf16[2048,250]{1,0:T(8,128)(2,1)S(1)}, bf16[2048,250]{1,0:T(8,128)(2,1)}, u32[]{:S(2)}) copy-start(bf16[2048,250]{1,0:T(8,128)(2,1)} %param.9) | copy-start | bytes 3072004
  16.2 30.1 %all-to-all-start.1 = ((bf16[8,1,256,250]{3,2,1,0:T(8,128)(2,1)}), bf16[8,1,256,250]{3,2,1,0:T(8,128)(2,1)S(1)}, u32[]{:S(2)}, u32[]{:S(2)}) async-start(bf16[8,1,256,250]{3,2,1,0:T(8,128)(2,1)} %bitcast.5), calls=%async_computation.1 | async-start | bytes 2097152 | tf_op jit(solution)/shard_map/all_to_all | solution.py:60
  46.3 1.0 copy-start.2
  110.8 5.2 %copy-start.4 = (f32[2048]{0:T(1024)S(1)}, f32[2048]{0:T(1024)}, u32[]{:S(2)}) copy-start(f32[2048]{0:T(1024)} %param.15) | copy-start | bytes 24580
  112.4 30.1 %all-to-all-start.2 = ((bf16[8,1,256,250]{2,3,1,0:T(8,128)(2,1)}), bf16[8,1,256,250]{2,3,1,0:T(8,128)(2,1)S(1)}, u32[]{:S(2)}, u32[]{:S(2)}) async-start(bf16[8,1,256,250]{2,3,1,0:T(8,128)(2,1)} %bitcast.12), calls=%async_computation.2 | async-start | bytes 2097152 | tf_op jit(solution)/shard_map/all_to_all | solution.py:60
  142.5 1.0 copy-start.3
  173.4 24.4 %copy-start = (f32[8,256,250]{1,2,0:T(8,128)}, f32[8,256,250]{1,2,0:T(8,128)S(1)}, u32[]{:S(2)}) copy-start(f32[8,256,250]{1,2,0:T(8,128)S(1)} %get-tuple-element.204) | copy-start | bytes 6144004
where the time goes:
time: 205 us; the launch traced here: 204 us
  local copies, waits for them, and re-layouts  64.1 us (31%)
  waiting for transfers between devices  52.8 us (26%)
  matrix products  35.8 us (17%)
  blocking collectives  35.2 us (17%)
  other arithmetic  7.67 us (4%)
  starting transfers between devices  7.12 us (3%)
    gather x3, local copies, waits for them, and re-layouts, propagate_local(): adjacent_blocks = column_set[slot_tiles]  54.7 us
    all_to_all x2, waiting for transfers between devices, local(): lax.all_to_all(outgoing, 'rows', split_axis=0, concat_axis=0, tiled=True)  52.8 us
    dot_general x2, matrix products, propagate_local(): jnp.einsum('mvfg,mvgx->mfx', blocks, adjacent_blocks, preferred_element_t...  35.8 us
    all_gather x3, blocking collectives, combined_all(): everything = jax.tree.map(lambda part: lax.all_gather(part, axis), value)  23.5 us
    all_to_all x1, blocking collectives, local(): lax.all_to_all(fetch, 'rows', split_axis=1, concat_axis=0, tiled=True)  11.7 us
    all_to_all x2, starting transfers between devices, local(): lax.all_to_all(outgoing, 'rows', split_axis=0, concat_axis=0, tiled=True)  7.12 us
    gather x2, local copies, waits for them, and re-layouts, local(): tiled[wanted].reshape(lax.axis_size('rows'), -1, tile_rows, col_width)  4.48 us
  transfers between devices with their start and end apart: 2, of which 2 were waited for; matrix products, arithmetic and copies ran while one was open for 0% of the time, Pallas kernels for 0%

commit v1 on v0

v1 whole, which is shorter than its diff:
```python
import functools

import jax
import jax.numpy as jnp
from jax import lax
from jax.experimental import pallas as pl
from jax.experimental.pallas import tpu as pltpu
from jax.sharding import PartitionSpec as P

CLS = 1000
LANES = 128
blend = 0.8

SMEM = pl.BlockSpec(memory_space=pltpu.SMEM)
VMEM = pl.BlockSpec(memory_space=pltpu.VMEM)
ANY = pl.BlockSpec(memory_space=pl.ANY)


def params(mib):
    return pltpu.CompilerParams(vmem_limit_bytes=mib << 20)


def sds(shape, dtype):
    return jax.ShapeDtypeStruct(shape, dtype)


def group_of(slots):
    return next(g for g in (4, 3, 2, 1) if slots % g == 0)


def split_kernel(prior_ref, *outs):
    width = prior_ref.shape[-1]
    for c, out in enumerate(outs):
        start = c * LANES
        live = min(LANES, width - start)
        out[:, :, :live] = prior_ref[:, :, start : start + live]
        if live < LANES:
            out[:, :, live:] = jnp.zeros(out.shape[:2] + (LANES - live,), out.dtype)


def split(prior, tile_rows):
    tiles = prior.reshape(-1, tile_rows, prior.shape[1])
    chunks = pl.cdiv(prior.shape[1], LANES)
    shape = sds((tiles.shape[0], tile_rows, LANES), prior.dtype)
    return pl.pallas_call(
        split_kernel,
        out_shape=[shape] * chunks,
        in_specs=[VMEM],
        out_specs=[VMEM] * chunks,
        compiler_params=params(16),
        name="split",
    )(tiles)


def pick_kernel(chunks, me_ref, wanted_ref, *refs):
    tabs, outs, sems = refs[:chunks], refs[chunks : 3 * chunks], refs[-1]
    n = wanted_ref.shape[0]
    copies = []
    for c in range(chunks):
        for x in range(n):
            tile = wanted_ref[me_ref[0] ^ x]
            copies.append(
                pltpu.make_async_copy(tabs[c].at[tile], outs[2 * c + x % 2].at[x // 2], sems.at[c, x])
            )
            copies[-1].start()
    for copy in copies:
        copy.wait()


def pick(me, wanted, tabs):
    n = wanted.shape[0]
    chunks = len(tabs)
    shape = sds((n // 2,) + tabs[0].shape[1:], tabs[0].dtype)
    outs = pl.pallas_call(
        functools.partial(pick_kernel, chunks),
        out_shape=[shape] * (2 * chunks),
        in_specs=[SMEM, SMEM] + [ANY] * chunks,
        out_specs=[ANY] * (2 * chunks),
        scratch_shapes=[pltpu.SemaphoreType.DMA((chunks, n))],
        compiler_params=params(16),
        name="pick",
    )(me, wanted, *tabs)
    return [outs[2 * c : 2 * c + 2] for c in range(chunks)]


def exchange(straight, across, n):
    got = lax.ppermute(across, "rows", [(i, i ^ 1) for i in range(n)])
    arrived = []
    for k in range(n // 2 - 1, 0, -1):
        message = jnp.stack([straight[k], got[k]])
        arrived.append(lax.ppermute(message, "rows", [(i, i ^ (2 * k)) for i in range(n)]))
    return got, arrived[::-1]


def load_field(tab, got, arrived, field, sems):
    own = tab.shape[0]
    copies = [pltpu.make_async_copy(tab, field.at[pl.ds(0, own)], sems.at[0])]
    copies.append(pltpu.make_async_copy(got.at[0], field.at[own + 1], sems.at[1]))
    for k, one in enumerate(arrived):
        copies.append(
            pltpu.make_async_copy(one, field.at[pl.ds(own + 2 * (k + 1), 2)], sems.at[2 + k])
        )
    for copy in copies:
        copy.start()
    field[own] = jnp.zeros(field.shape[1:], field.dtype)
    return copies


def block_copy(blocks, held, sems, t, g):
    size = held.shape[1] // sems.shape[1]
    span = pl.ds(g * size, size)
    return pltpu.make_async_copy(blocks.at[t, span], held.at[t, span], sems.at[t, g])


def start_blocks(groups_of, blocks, held, sems):
    for t in range(held.shape[0]):
        groups = groups_of(t)
        for g in range(sems.shape[1]):

            @pl.when(g < groups)
            def _():
                block_copy(blocks, held, sems, t, g).start()


def tile_sum(t, groups, slots_ref, blocks, held, field, sems):
    slots = held.shape[1]
    size = slots // sems.shape[1]

    def step(g, total):
        block_copy(blocks, held, sems, t, g).wait()
        for i in range(size):
            at = g * size + i
            total = total + jnp.dot(
                held[t, at], field[slots_ref[t * slots + at]], preferred_element_type=jnp.float32
            )
        return total

    return lax.fori_loop(0, groups, step, jnp.zeros(field.shape[1:], jnp.float32))


def with_targets(total, seeds, first_col):
    cols = first_col + lax.broadcasted_iota(jnp.int32, total.shape, 1)
    return blend * total + (1.0 - blend) * (seeds == cols).astype(jnp.float32)


def step1_kernel(
    links, chunk, me_ref, slots_ref, counts_ref, wanted_ref, tab, got, *refs
):
    arrived = refs[:links]
    (blocks, seeds_ref, out, straight, across, field, held, field_sems, sems) = refs[links:]
    own, tile_rows = tab.shape[:2]
    size = held.shape[1] // sems.shape[1]
    groups_of = lambda t: (counts_ref[t] + size - 1) // size
    copies = load_field(tab, got, arrived, field, field_sems)
    start_blocks(groups_of, blocks, held, sems)
    for copy in copies:
        copy.wait()
    first_col = me_ref[1] + chunk * LANES

    def tile(t, carry):
        total = tile_sum(t, groups_of(t), slots_ref, blocks, held, field, sems)
        seeds = seeds_ref[pl.ds(t * tile_rows, tile_rows), :]
        out[t] = with_targets(total, seeds, first_col).astype(out.dtype)
        return carry

    lax.fori_loop(0, own, tile, 0)
    for x in range(wanted_ref.shape[0]):
        (across if x % 2 else straight)[x // 2] = out[wanted_ref[me_ref[0] ^ x]]


def scratch(own, n, tile_rows, dtype, blocks, links):
    slots = blocks.shape[1]
    return [
        pltpu.VMEM((own + n, tile_rows, LANES), dtype),
        pltpu.VMEM(blocks.shape, blocks.dtype),
        pltpu.SemaphoreType.DMA((2 + links,)),
        pltpu.SemaphoreType.DMA((own, slots // group_of(slots))),
    ]


def cost(blocks):
    own, slots, rows, depth = blocks.shape
    return pl.CostEstimate(
        flops=2 * own * slots * rows * depth * LANES,
        bytes_accessed=blocks.size * blocks.dtype.itemsize * 2 // 3,
        transcendentals=0,
    )


def step1(chunk, me, slots, counts, wanted, tab, got, arrived, blocks, seeds):
    own, tile_rows = tab.shape[:2]
    n = wanted.shape[0]
    half = sds((n // 2, tile_rows, LANES), tab.dtype)
    return pl.pallas_call(
        functools.partial(step1_kernel, len(arrived), chunk),
        out_shape=[sds(tab.shape, tab.dtype), half, half],
        in_specs=[SMEM] * 4 + [ANY] * (3 + len(arrived)) + [VMEM],
        out_specs=[VMEM] * 3,
        scratch_shapes=scratch(own, n, tile_rows, tab.dtype, blocks, len(arrived)),
        compiler_params=params(44),
        cost_estimate=cost(blocks),
        name="step1",
    )(me, slots, counts, wanted, tab, got, *arrived, blocks, seeds)


def step2_kernel(links, chunk, width, me_ref, slots_ref, counts_ref, tab, got, *refs):
    arrived = refs[:links]
    (blocks, seeds_ref, temp_ref, expo_ref, stats_ref, field, held, field_sems, sems) = refs[links:]
    own, tile_rows = tab.shape[:2]
    size = held.shape[1] // sems.shape[1]
    groups_of = lambda t: (counts_ref[t] + size - 1) // size
    copies = load_field(tab, got, arrived, field, field_sems)
    start_blocks(groups_of, blocks, held, sems)
    for copy in copies:
        copy.wait()
    first_col = me_ref[1] + chunk * LANES
    live = min(LANES, width - chunk * LANES)

    def tile(t, carry):
        total = tile_sum(t, groups_of(t), slots_ref, blocks, held, field, sems)
        span = pl.ds(pl.multiple_of(t * tile_rows, tile_rows), tile_rows)
        logits = temp_ref[span, :] * with_targets(total, seeds_ref[span, :], first_col)
        lane = lax.broadcasted_iota(jnp.int32, logits.shape, 1)
        if live < LANES:
            top = jnp.max(jnp.where(lane < live, logits, -jnp.inf), axis=1, keepdims=True)
            shifted = jnp.where(lane < live, logits - top, 0.0)
            expo = jnp.where(lane < live, jnp.exp(shifted), 0.0)
        else:
            top = jnp.max(logits, axis=1, keepdims=True)
            shifted = logits - top
            expo = jnp.exp(shifted)
        totals = jnp.sum(expo, axis=1, keepdims=True)
        moments = jnp.sum(expo * shifted, axis=1, keepdims=True)
        expo_ref[span, :] = expo
        summary = jnp.where(lane == 0, top, jnp.where(lane == 1, totals, moments))
        stats_ref[:, span] = summary.T[:8]
        return carry

    lax.fori_loop(0, own, tile, 0)


def step2(chunk, width, me, slots, counts, tab, got, arrived, blocks, seeds, temp):
    own, tile_rows = tab.shape[:2]
    n = 2 * (len(arrived) + 1)
    rows = own * tile_rows
    return pl.pallas_call(
        functools.partial(step2_kernel, len(arrived), chunk, width),
        out_shape=[sds((rows, LANES), jnp.float32), sds((8, rows), jnp.float32)],
        in_specs=[SMEM] * 3 + [ANY] * (3 + len(arrived)) + [VMEM] * 2,
        out_specs=[VMEM] * 2,
        scratch_shapes=scratch(own, n, tile_rows, tab.dtype, blocks, len(arrived)),
        compiler_params=params(44),
        cost_estimate=cost(blocks),
        name="step2",
    )(me, slots, counts, tab, got, *arrived, blocks, seeds, temp)


def finish_kernel(chunks, parts, tile_rows, *refs):
    expos, stats = refs[:chunks], refs[chunks : chunks + chunks * parts]
    pseudo_ref, certainty_ref = refs[chunks + chunks * parts :]
    rows, width = pseudo_ref.shape
    tops = [s[0:1, :] for s in stats]
    top = functools.reduce(jnp.maximum, tops)
    totals = jnp.zeros((1, rows), jnp.float32)
    moments = jnp.zeros((1, rows), jnp.float32)
    scales = []
    for s, one in zip(stats, tops):
        delta = one - top
        scale = jnp.exp(delta)
        scales.append(scale)
        totals += scale * s[1:2, :]
        moments += scale * (s[2:3, :] + delta * s[1:2, :])
    certainty_ref[...] = 1.0 - (jnp.log(totals) - moments / totals) / jnp.log(jnp.float32(CLS))
    inverse = 1.0 / totals
    mine = [scales[c * parts] * inverse for c in range(chunks)]
    mine = jnp.concatenate(mine + [jnp.zeros((LANES - chunks, rows), jnp.float32)], axis=0)
    for t in range(rows // tile_rows):
        span = slice(t * tile_rows, (t + 1) * tile_rows)
        columns = mine[:, span].T
        for c in range(chunks):
            start = c * LANES
            live = min(LANES, width - start)
            value = expos[c][span, :] * columns[:, c : c + 1]
            pseudo_ref[span, start : start + live] = value[:, :live].astype(pseudo_ref.dtype)


def finish(expos, stats, tile_rows, width):
    rows = expos[0].shape[0]
    chunks, parts = len(expos), len(stats[0])
    flat = [s for part in stats for s in part]
    return pl.pallas_call(
        functools.partial(finish_kernel, chunks, parts, tile_rows),
        out_shape=[sds((rows, width), jnp.bfloat16), sds((1, rows), jnp.float32)],
        in_specs=[VMEM] * (len(expos) + len(flat)),
        out_specs=[VMEM] * 2,
        compiler_params=params(24),
        name="finish",
    )(*expos, *flat)


def local(prior, blocks, links, counts, fetch, seeds, inv_temp):
    width = prior.shape[1]
    own, slots, tile_rows = blocks.shape[:3]
    n = lax.axis_size("rows")
    parts = lax.axis_size("cls")
    chunks = pl.cdiv(width, LANES)
    index = lax.axis_index("rows")
    me = jnp.stack([index, lax.axis_index("cls") * width]).astype(jnp.int32)
    wanted = lax.all_to_all(fetch, "rows", split_axis=1, concat_axis=0, tiled=True).reshape(-1)
    tabs = split(prior, tile_rows)

    offset = (links - own) ^ index
    mine = fetch.reshape(n)[index]
    table = jnp.where(links < own, links, jnp.where(offset == 0, mine, own + offset))
    live = jnp.arange(slots, dtype=jnp.int32)[None, :] < counts[:, None]
    table = jnp.where(live, table, own).astype(jnp.int32).reshape(-1)
    seeds = seeds[:, None]
    temp = inv_temp[:, None]

    sent = pick(me, wanted, tabs)
    here = [exchange(*sent[c], n) for c in range(chunks)]
    fields = []
    for c in range(chunks):
        out, straight, across = step1(
            c, me, table, counts, wanted, tabs[c], *here[c], blocks, seeds
        )
        fields.append((out, *exchange(straight, across, n)))
    expos, stats = [], []
    for c in range(chunks):
        expo, summary = step2(c, width, me, table, counts, *fields[c], blocks, seeds, temp)
        expos.append(expo)
        stats.append(
            [summary]
            + [
                lax.ppermute(summary, "cls", [(i, (i + k) % parts) for i in range(parts)])
                for k in range(1, parts)
            ]
        )
    pseudo, certainty = finish(expos, stats, tile_rows, width)
    return pseudo, certainty.reshape(-1)


def solution(mesh):
    return jax.shard_map(
        local,
        mesh=mesh,
        in_specs=(
            P("rows", "cls"),
            P("rows", None, None, None),
            P("rows", None),
            P("rows"),
            P("rows", None, None),
            P("rows"),
            P("rows"),
        ),
        out_specs=(P("rows", "cls"), P("rows")),
        check_vma=False,
    )
```

time: 205 us -> 138 us (0.67)
  the two profiles are of different devices: /device:TPU:0 before, /device:TPU:18 now
where the time goes in v1:
time: 138 us; the launch traced here: 137 us
  Pallas kernels  62.6 us (45%)
  waiting for transfers between devices  33.9 us (25%)
  starting transfers between devices  27.8 us (20%)
  local copies, waits for them, and re-layouts  9.91 us (7%)
  other arithmetic  1.87 us (1%)
    pallas_call x2, Pallas kernels, step2(): pl.pallas_call(functools.partial(step2_kernel, len(arrived), chunk, width...  31.3 us
    ppermute x12, waiting for transfers between devices, exchange(): lax.ppermute(message, 'rows', [(i, i ^ 2 * k) for i in range(n)])  28.4 us
    pallas_call x2, Pallas kernels, step1(): pl.pallas_call(functools.partial(step1_kernel, len(arrived), chunk), out_...  27.2 us
    ppermute x12, starting transfers between devices, exchange(): lax.ppermute(message, 'rows', [(i, i ^ 2 * k) for i in range(n)])  15.3 us
    ppermute x6, starting transfers between devices, local(): lax.ppermute(summary, 'cls', [(i, (i + k) % parts) for i in range(parts)])  6.55 us
    unnamed x13, local copies, waits for them, and re-layouts  5.31 us
    all_to_all x1, starting transfers between devices, local(): lax.all_to_all(fetch, 'rows', split_axis=1, concat_axis=0, tiled=True)  5.21 us
    ppermute x6, waiting for transfers between devices, local(): lax.ppermute(summary, 'cls', [(i, (i + k) % parts) for i in range(parts)])  5.15 us
  transfers between devices with their start and end apart: 23, of which 8 were waited for; matrix products, arithmetic and copies ran while one was open for 5% of the time, Pallas kernels for 43%

profile of v1, /device:TPU:18, one launch (start us, length us, event | category | flops | bytes accessed | tf_op | source)
XLA Modules:
  0.0 137.0 jit_solution(16779760988038941322)
XLA Ops:
  0.6 1.3 copy.22
  2.0 5.2 %all-to-all-start = ((s32[1,8,1]{2,0,1:T(1,128)}), s32[1,8,1]{2,0,1:T(1,128)S(1)}, u32[]{:S(2)}, u32[]{:S(2)}) async-start(s32[1,8,1]{2,0,1:T(1,128)} %copy.22), calls=%async_computation | async-start | bytes 8192 | tf_op jit(solution)/shard_map/all_to_all | solution.py:309
  10.5 1.8 %pick.1 = (bf16[4,256,128]{2,1,0:T(8,128)(2,1)S(1)}, bf16[4,256,128]{2,1,0:T(8,128)(2,1)}, bf16[4,256,128]{2,1,0:T(8,128)(2,1)S(1)}, bf16[4,256,128]{2,1,0:T(8,128)(2,1)S(1)}) custom-call(s32[2]{0:T(128)S(1)} %pad_add_fusion.me_ref, s32[8]{0:T(128)S(1)} %reduce.wanted_ref, bf16[8,256,128]{2,1,0:T(8,128)(2,1)S(1)} %get-tuple-element.20.refs_0_.tab, ...), custom_call_target="tpu_custom_call" | custom-call | tf_op jit(solution)/shard_map/pick/pallas_call | solution.py:74
  14.5 1.4 %fusion = s32[8,24]{1,0:T(8,128)S(1)} fusion(s32[8,24]{1,0:T(8,128)} %param.9, s32[]{:T(128)} %bitcast.2, s32[]{:T(128)} %axis_index.22, s32[8]{0:T(128)} %counts_ref.7), kind=kLoop, calls=%fused_computation.13 | loop fusion | flops 1728 | bytes 1576 | tf_op jit(solution)/shard_map/jit(_where)/select_n | solution.py:316
  21.0 1.8 %collective-permute-start.2 = (bf16[2,256,128]{2,1,0:T(8,128)(2,1)S(1)}, bf16[2,256,128]{2,1,0:T(8,128)(2,1)S(1)}, u32[]{:S(2)}, u32[]{:S(2)}) collective-permute-start(bf16[2,256,128]{2,1,0:T(8,128)(2,1)S(1)} %pad_maximum_fusion.1), channel_id=1, source_target_pairs={{0,4},{1,5},{2,6},{3,7},{4,0},{5,1},{6,2},{7,3},{8,12},{9,13},{10,... | collective-permute-start | bytes 393224 | tf_op jit(solution)/shard_map/ppermute | solution.py:91
  23.5 2.2 %collective-permute-start.9 = (bf16[2,256,128]{2,1,0:T(8,128)(2,1)S(1)}, bf16[2,256,128]{2,1,0:T(8,128)(2,1)S(1)}, u32[]{:S(2)}, u32[]{:S(2)}) collective-permute-start(bf16[2,256,128]{2,1,0:T(8,128)(2,1)S(1)} %pad_maximum_fusion.6), channel_id=1, source_target_pairs={{0,2},{1,3},{2,0},{3,1},{4,6},{5,7},{6,4},{7,5},{8,10},{9,11},{10,... | collective-permute-start | bytes 393224 | tf_op jit(solution)/shard_map/ppermute | solution.py:91
  27.8 4.4 %collective-permute-done.2.refs_1_ = bf16[2,256,128]{2,1,0:T(8,128)(2,1)S(1)} collective-permute-done((bf16[2,256,128]{2,1,0:T(8,128)(2,1)S(1)}, bf16[2,256,128]{2,1,0:T(8,128)(2,1)S(1)}, u32[]{:S(2)}, u32[]{:S(2)}) %collective-permute-start.2) | collective-permute-done | bytes 131104 | tf_op jit(solution)/shard_map/ppermute | solution.py:91
  32.3 9.6 %collective-permute-done.3.refs_2_ = bf16[2,256,128]{2,1,0:T(8,128)(2,1)S(1)} collective-permute-done((bf16[2,256,128]{2,1,0:T(8,128)(2,1)S(1)}, bf16[2,256,128]{2,1,0:T(8,128)(2,1)S(1)}, u32[]{:S(2)}, u32[]{:S(2)}) %collective-permute-start.3) | collective-permute-done | bytes 131104 | tf_op jit(solution)/shard_map/ppermute | solution.py:91
  42.5 13.6 %step1.2 = (bf16[8,256,128]{2,1,0:T(8,128)(2,1)S(1)}, bf16[4,256,128]{2,1,0:T(8,128)(2,1)S(1)}, bf16[4,256,128]{2,1,0:T(8,128)(2,1)S(1)}) custom-call(s32[2]{0:T(128)S(1)} %pad_add_fusion.me_ref, s32[192]{0:T(256)S(1)} %reshape.24.slots_ref, s32[8]{0:T(128)S(1)} %copy-done.3, s32[8]{0:T(128)S(1)} %reduce.wanted_ref, ...), custom_call_target="tpu_custom_call" | custom-call | flops 3221225472 | bytes 16777216 | tf_op jit(solution)/shard_map/step1/pallas_call | solution.py:194
  56.2 13.6 %step1.3 = (bf16[8,256,128]{2,1,0:T(8,128)(2,1)S(1)}, bf16[4,256,128]{2,1,0:T(8,128)(2,1)S(1)}, bf16[4,256,128]{2,1,0:T(8,128)(2,1)S(1)}) custom-call(s32[2]{0:T(128)S(1)} %pad_add_fusion.me_ref, s32[192]{0:T(256)S(1)} %reshape.24.slots_ref, s32[8]{0:T(128)S(1)} %copy-done.4, s32[8]{0:T(128)S(1)} %reduce.wanted_ref, ...), custom_call_target="tpu_custom_call" | custom-call | flops 3221225472 | bytes 16777216 | tf_op jit(solution)/shard_map/step1/pallas_call | solution.py:194
  70.1 2.5 %collective-permute-start.6 = (bf16[2,256,128]{2,1,0:T(8,128)(2,1)S(1)}, bf16[2,256,128]{2,1,0:T(8,128)(2,1)S(1)}, u32[]{:S(2)}, u32[]{:S(2)}) collective-permute-start(bf16[2,256,128]{2,1,0:T(8,128)(2,1)S(1)} %pad_maximum_fusion.4), channel_id=1, source_target_pairs={{0,4},{1,5},{2,6},{3,7},{4,0},{5,1},{6,2},{7,3},{8,12},{9,13},{10,... | collective-permute-start | bytes 393224 | tf_op jit(solution)/shard_map/ppermute | solution.py:91
  74.8 1.6 %collective-permute-start.14 = (bf16[2,256,128]{2,1,0:T(8,128)(2,1)S(1)}, bf16[2,256,128]{2,1,0:T(8,128)(2,1)S(1)}, u32[]{:S(2)}, u32[]{:S(2)}) collective-permute-start(bf16[2,256,128]{2,1,0:T(8,128)(2,1)S(1)} %pad_maximum_fusion.10), channel_id=1, source_target_pairs={{0,4},{1,5},{2,6},{3,7},{4,0},{5,1},{6,2},{7,3},{8,12},{9,13},{10,... | collective-permute-start | bytes 393224 | tf_op jit(solution)/shard_map/ppermute | solution.py:91
  77.5 4.6 %collective-permute-done.6.refs_1_ = bf16[2,256,128]{2,1,0:T(8,128)(2,1)S(1)} collective-permute-done((bf16[2,256,128]{2,1,0:T(8,128)(2,1)S(1)}, bf16[2,256,128]{2,1,0:T(8,128)(2,1)S(1)}, u32[]{:S(2)}, u32[]{:S(2)}) %collective-permute-start.6) | collective-permute-done | bytes 131104 | tf_op jit(solution)/shard_map/ppermute | solution.py:91
  82.1 9.8 %collective-permute-done.7.refs_2_ = bf16[2,256,128]{2,1,0:T(8,128)(2,1)S(1)} collective-permute-done((bf16[2,256,128]{2,1,0:T(8,128)(2,1)S(1)}, bf16[2,256,128]{2,1,0:T(8,128)(2,1)S(1)}, u32[]{:S(2)}, u32[]{:S(2)}) %collective-permute-start.7) | collective-permute-done | bytes 131104 | tf_op jit(solution)/shard_map/ppermute | solution.py:91
  91.9 15.7 %step2.2 = (f32[2048,128]{1,0:T(8,128)S(1)}, f32[8,2048]{1,0:T(8,128)S(1)}) custom-call(s32[2]{0:T(128)S(1)} %pad_add_fusion.me_ref, s32[192]{0:T(256)S(1)} %reshape.24.slots_ref, s32[8]{0:T(128)S(1)} %copy-done.4, bf16[8,256,128]{2,1,0:T(8,128)(2,1)S(1)} %get-tuple-element.24.tab, bf16[4,256,128]{2,1,0:T(8,128)(2,1)S(1)} %collective-permute-done.4.got, ...), custom_call_target="tpu_custom_call" | custom-call | flops 3221225472 | bytes 16777216 | tf_op jit(solution)/shard_map/step2/pallas_call | solution.py:246
  107.6 1.5 %collective-permute-start.16 = (f32[8,2048]{1,0:T(8,128)S(1)}, f32[8,2048]{1,0:T(8,128)S(1)}, u32[]{:S(2)}, u32[]{:S(2)}) collective-permute-start(f32[8,2048]{1,0:T(8,128)S(1)} %get-tuple-element.34.refs_2_), channel_id=1, source_target_pairs={{0,8},{8,16},{16,24},{24,0},{1,9},{9,17},{17,25},{25,1},{2,10},{10... | collective-permute-start | bytes 196616 | tf_op jit(solution)/shard_map/ppermute | solution.py:335
  109.6 1.5 %collective-permute-start.18 = (f32[8,2048]{1,0:T(8,128)S(1)}, f32[8,2048]{1,0:T(8,128)S(1)}, u32[]{:S(2)}, u32[]{:S(2)}) collective-permute-start(f32[8,2048]{1,0:T(8,128)S(1)} %get-tuple-element.34.refs_2_), channel_id=1, source_target_pairs={{0,24},{8,0},{16,8},{24,16},{1,25},{9,1},{17,9},{25,17},{2,26},{10... | collective-permute-start | bytes 196616 | tf_op jit(solution)/shard_map/ppermute | solution.py:335
  111.2 15.7 %step2.3 = (f32[2048,128]{1,0:T(8,128)S(1)}, f32[8,2048]{1,0:T(8,128)S(1)}) custom-call(s32[2]{0:T(128)S(1)} %pad_add_fusion.me_ref, s32[192]{0:T(256)S(1)} %reshape.24.slots_ref, s32[8]{0:T(128)S(1)} %copy-done.4, bf16[8,256,128]{2,1,0:T(8,128)(2,1)S(1)} %get-tuple-element.30.tab, bf16[4,256,128]{2,1,0:T(8,128)(2,1)S(1)} %collective-permute-done.12.got, ...), custom_call_target="tpu_custom_call" | custom-call | flops 3221225472 | bytes 16777216 | tf_op jit(solution)/shard_map/step2/pallas_call | solution.py:246
  126.9 1.4 %collective-permute-start.19 = (f32[8,2048]{1,0:T(8,128)S(1)}, f32[8,2048]{1,0:T(8,128)S(1)}, u32[]{:S(2)}, u32[]{:S(2)}) collective-permute-start(f32[8,2048]{1,0:T(8,128)S(1)} %get-tuple-element.35.refs_6_), channel_id=1, source_target_pairs={{0,8},{8,16},{16,24},{24,0},{1,9},{9,17},{17,25},{25,1},{2,10},{10... | collective-permute-start | bytes 196616 | tf_op jit(solution)/shard_map/ppermute | solution.py:335
  128.3 1.5 %collective-permute-start.20 = (f32[8,2048]{1,0:T(8,128)S(1)}, f32[8,2048]{1,0:T(8,128)S(1)}, u32[]{:S(2)}, u32[]{:S(2)}) collective-permute-start(f32[8,2048]{1,0:T(8,128)S(1)} %get-tuple-element.35.refs_6_), channel_id=1, source_target_pairs={{0,16},{8,24},{16,0},{24,8},{1,17},{9,25},{17,1},{25,9},{2,18},{10... | collective-permute-start | bytes 196616 | tf_op jit(solution)/shard_map/ppermute | solution.py:335
  129.9 1.3 collective-permute-done.19.refs_7_
  131.2 1.4 %collective-permute-done.20.refs_8_ = f32[8,2048]{1,0:T(8,128)S(1)} collective-permute-done((f32[8,2048]{1,0:T(8,128)S(1)}, f32[8,2048]{1,0:T(8,128)S(1)}, u32[]{:S(2)}, u32[]{:S(2)}) %collective-permute-start.20) | collective-permute-done | bytes 65568 | tf_op jit(solution)/shard_map/ppermute | solution.py:335
  132.6 2.4 %collective-permute-done.21.refs_9_ = f32[8,2048]{1,0:T(8,128)S(1)} collective-permute-done((f32[8,2048]{1,0:T(8,128)S(1)}, f32[8,2048]{1,0:T(8,128)S(1)}, u32[]{:S(2)}, u32[]{:S(2)}) %collective-permute-start.21) | collective-permute-done | bytes 65568 | tf_op jit(solution)/shard_map/ppermute | solution.py:335
  135.0 2.0 %finish.1 = (bf16[2048,250]{1,0:T(8,128)(2,1)}, f32[1,2048]{1,0:T(1,128)}) custom-call(f32[2048,128]{1,0:T(8,128)S(1)} %get-tuple-element.27.refs_0_, f32[2048,128]{1,0:T(8,128)S(1)} %get-tuple-element.33.refs_1_, f32[8,2048]{1,0:T(8,128)S(1)} %get-tuple-element.34.refs_2_, f32[8,2048]{1,0:T(8,128)S(1)} %collective-permute-done.16.refs_3_, ...), custom_call_target="tpu_custom_call" | custom-call | tf_op jit(solution)/shard_map/finish/pallas_call | solution.py:291
  (68 shorter events, 18.2 us)
Async XLA Ops:
  0.6 55.6 %copy-start.4 = (s32[8]{0:T(128)S(1)}, s32[8]{0:T(128)}, u32[]{:S(2)}) copy-start(s32[8]{0:T(128)} %counts_ref.7) | copy-start | bytes 100
  2.0 8.3 %all-to-all-start = ((s32[1,8,1]{2,0,1:T(1,128)}), s32[1,8,1]{2,0,1:T(1,128)S(1)}, u32[]{:S(2)}, u32[]{:S(2)}) async-start(s32[1,8,1]{2,0,1:T(1,128)} %copy.22), calls=%async_computation | async-start | bytes 8192 | tf_op jit(solution)/shard_map/all_to_all | solution.py:309
  14.5 5.2 %collective-permute-start = (bf16[4,256,128]{2,1,0:T(8,128)(2,1)}, bf16[4,256,128]{2,1,0:T(8,128)(2,1)S(1)}, u32[]{:S(2)}, u32[]{:S(2)}) collective-permute-start(bf16[4,256,128]{2,1,0:T(8,128)(2,1)} %get-tuple-element.22), channel_id=1, source_target_pairs={{0,1},{1,0},{2,3},{3,2},{4,5},{5,4},{6,7},{7,6},{8,9},{9,8},{10,11... | collective-permute-start | bytes 786440 | tf_op jit(solution)/shard_map/ppermute | solution.py:87
  18.1 5.4 %collective-permute-start.8 = (bf16[4,256,128]{2,1,0:T(8,128)(2,1)}, bf16[4,256,128]{2,1,0:T(8,128)(2,1)S(1)}, u32[]{:S(2)}, u32[]{:S(2)}) collective-permute-start(bf16[4,256,128]{2,1,0:T(8,128)(2,1)} %copy-done.5), channel_id=1, source_target_pairs={{0,1},{1,0},{2,3},{3,2},{4,5},{5,4},{6,7},{7,6},{8,9},{9,8},{10,11... | collective-permute-start | bytes 786440 | tf_op jit(solution)/shard_map/ppermute | solution.py:87
  19.7 7.2 %collective-permute-start.1 = (bf16[2,256,128]{2,1,0:T(8,128)(2,1)S(1)}, bf16[2,256,128]{2,1,0:T(8,128)(2,1)S(1)}, u32[]{:S(2)}, u32[]{:S(2)}) collective-permute-start(bf16[2,256,128]{2,1,0:T(8,128)(2,1)S(1)} %pad_maximum_fusion), channel_id=1, source_target_pairs={{0,2},{1,3},{2,0},{3,1},{4,6},{5,7},{6,4},{7,5},{8,10},{9,11},{10,... | collective-permute-start | bytes 393224 | tf_op jit(solution)/shard_map/ppermute | solution.py:91
  21.0 11.3 %collective-permute-start.2 = (bf16[2,256,128]{2,1,0:T(8,128)(2,1)S(1)}, bf16[2,256,128]{2,1,0:T(8,128)(2,1)S(1)}, u32[]{:S(2)}, u32[]{:S(2)}) collective-permute-start(bf16[2,256,128]{2,1,0:T(8,128)(2,1)S(1)} %pad_maximum_fusion.1), channel_id=1, source_target_pairs={{0,4},{1,5},{2,6},{3,7},{4,0},{5,1},{6,2},{7,3},{8,12},{9,13},{10,... | collective-permute-start | bytes 393224 | tf_op jit(solution)/shard_map/ppermute | solution.py:91
  22.8 19.0 %collective-permute-start.3 = (bf16[2,256,128]{2,1,0:T(8,128)(2,1)S(1)}, bf16[2,256,128]{2,1,0:T(8,128)(2,1)S(1)}, u32[]{:S(2)}, u32[]{:S(2)}) collective-permute-start(bf16[2,256,128]{2,1,0:T(8,128)(2,1)S(1)} %pad_maximum_fusion.2), channel_id=1, source_target_pairs={{0,6},{1,7},{2,4},{3,5},{4,2},{5,3},{6,0},{7,1},{8,14},{9,15},{10,... | collective-permute-start | bytes 393224 | tf_op jit(solution)/shard_map/ppermute | solution.py:91
  23.5 32.7 %collective-permute-start.9 = (bf16[2,256,128]{2,1,0:T(8,128)(2,1)S(1)}, bf16[2,256,128]{2,1,0:T(8,128)(2,1)S(1)}, u32[]{:S(2)}, u32[]{:S(2)}) collective-permute-start(bf16[2,256,128]{2,1,0:T(8,128)(2,1)S(1)} %pad_maximum_fusion.6), channel_id=1, source_target_pairs={{0,2},{1,3},{2,0},{3,1},{4,6},{5,7},{6,4},{7,5},{8,10},{9,11},{10,... | collective-permute-start | bytes 393224 | tf_op jit(solution)/shard_map/ppermute | solution.py:91
  25.7 30.5 %collective-permute-start.10 = (bf16[2,256,128]{2,1,0:T(8,128)(2,1)S(1)}, bf16[2,256,128]{2,1,0:T(8,128)(2,1)S(1)}, u32[]{:S(2)}, u32[]{:S(2)}) collective-permute-start(bf16[2,256,128]{2,1,0:T(8,128)(2,1)S(1)} %pad_maximum_fusion.7), channel_id=1, source_target_pairs={{0,4},{1,5},{2,6},{3,7},{4,0},{5,1},{6,2},{7,3},{8,12},{9,13},{10,... | collective-permute-start | bytes 393224 | tf_op jit(solution)/shard_map/ppermute | solution.py:91
  26.9 29.2 %collective-permute-start.11 = (bf16[2,256,128]{2,1,0:T(8,128)(2,1)S(1)}, bf16[2,256,128]{2,1,0:T(8,128)(2,1)S(1)}, u32[]{:S(2)}, u32[]{:S(2)}) collective-permute-start(bf16[2,256,128]{2,1,0:T(8,128)(2,1)S(1)} %pad_maximum_fusion.8), channel_id=1, source_target_pairs={{0,6},{1,7},{2,4},{3,5},{4,2},{5,3},{6,0},{7,1},{8,14},{9,15},{10,... | collective-permute-start | bytes 393224 | tf_op jit(solution)/shard_map/ppermute | solution.py:91
  56.1 13.9 %collective-permute-start.4 = (bf16[4,256,128]{2,1,0:T(8,128)(2,1)S(1)}, bf16[4,256,128]{2,1,0:T(8,128)(2,1)S(1)}, u32[]{:S(2)}, u32[]{:S(2)}) collective-permute-start(bf16[4,256,128]{2,1,0:T(8,128)(2,1)S(1)} %get-tuple-element.25), channel_id=1, source_target_pairs={{0,1},{1,0},{2,3},{3,2},{4,5},{5,4},{6,7},{7,6},{8,9},{9,8},{10,11... | collective-permute-start | bytes 786440 | tf_op jit(solution)/shard_map/ppermute | solution.py:87
  69.9 3.9 %collective-permute-start.12 = (bf16[4,256,128]{2,1,0:T(8,128)(2,1)S(1)}, bf16[4,256,128]{2,1,0:T(8,128)(2,1)S(1)}, u32[]{:S(2)}, u32[]{:S(2)}) collective-permute-start(bf16[4,256,128]{2,1,0:T(8,128)(2,1)S(1)} %get-tuple-element.31), channel_id=1, source_target_pairs={{0,1},{1,0},{2,3},{3,2},{4,5},{5,4},{6,7},{7,6},{8,9},{9,8},{10,11... | collective-permute-start | bytes 786440 | tf_op jit(solution)/shard_map/ppermute | solution.py:87
  70.0 6.4 %collective-permute-start.5 = (bf16[2,256,128]{2,1,0:T(8,128)(2,1)S(1)}, bf16[2,256,128]{2,1,0:T(8,128)(2,1)S(1)}, u32[]{:S(2)}, u32[]{:S(2)}) collective-permute-start(bf16[2,256,128]{2,1,0:T(8,128)(2,1)S(1)} %pad_maximum_fusion.3), channel_id=1, source_target_pairs={{0,2},{1,3},{2,0},{3,1},{4,6},{5,7},{6,4},{7,5},{8,10},{9,11},{10,... | collective-permute-start | bytes 393224 | tf_op jit(solution)/shard_map/ppermute | solution.py:91
  70.1 12.0 %collective-permute-start.6 = (bf16[2,256,128]{2,1,0:T(8,128)(2,1)S(1)}, bf16[2,256,128]{2,1,0:T(8,128)(2,1)S(1)}, u32[]{:S(2)}, u32[]{:S(2)}) collective-permute-start(bf16[2,256,128]{2,1,0:T(8,128)(2,1)S(1)} %pad_maximum_fusion.4), channel_id=1, source_target_pairs={{0,4},{1,5},{2,6},{3,7},{4,0},{5,1},{6,2},{7,3},{8,12},{9,13},{10,... | collective-permute-start | bytes 393224 | tf_op jit(solution)/shard_map/ppermute | solution.py:91
  72.6 19.3 %collective-permute-start.7 = (bf16[2,256,128]{2,1,0:T(8,128)(2,1)S(1)}, bf16[2,256,128]{2,1,0:T(8,128)(2,1)S(1)}, u32[]{:S(2)}, u32[]{:S(2)}) collective-permute-start(bf16[2,256,128]{2,1,0:T(8,128)(2,1)S(1)} %pad_maximum_fusion.5), channel_id=1, source_target_pairs={{0,6},{1,7},{2,4},{3,5},{4,2},{5,3},{6,0},{7,1},{8,14},{9,15},{10,... | collective-permute-start | bytes 393224 | tf_op jit(solution)/shard_map/ppermute | solution.py:91
  73.8 35.9 %collective-permute-start.13 = (bf16[2,256,128]{2,1,0:T(8,128)(2,1)S(1)}, bf16[2,256,128]{2,1,0:T(8,128)(2,1)S(1)}, u32[]{:S(2)}, u32[]{:S(2)}) collective-permute-start(bf16[2,256,128]{2,1,0:T(8,128)(2,1)S(1)} %pad_maximum_fusion.9), channel_id=1, source_target_pairs={{0,2},{1,3},{2,0},{3,1},{4,6},{5,7},{6,4},{7,5},{8,10},{9,11},{10,... | collective-permute-start | bytes 393224 | tf_op jit(solution)/shard_map/ppermute | solution.py:91
  74.8 36.4 %collective-permute-start.14 = (bf16[2,256,128]{2,1,0:T(8,128)(2,1)S(1)}, bf16[2,256,128]{2,1,0:T(8,128)(2,1)S(1)}, u32[]{:S(2)}, u32[]{:S(2)}) collective-permute-start(bf16[2,256,128]{2,1,0:T(8,128)(2,1)S(1)} %pad_maximum_fusion.10), channel_id=1, source_target_pairs={{0,4},{1,5},{2,6},{3,7},{4,0},{5,1},{6,2},{7,3},{8,12},{9,13},{10,... | collective-permute-start | bytes 393224 | tf_op jit(solution)/shard_map/ppermute | solution.py:91
  76.4 34.8 %collective-permute-start.15 = (bf16[2,256,128]{2,1,0:T(8,128)(2,1)S(1)}, bf16[2,256,128]{2,1,0:T(8,128)(2,1)S(1)}, u32[]{:S(2)}, u32[]{:S(2)}) collective-permute-start(bf16[2,256,128]{2,1,0:T(8,128)(2,1)S(1)} %pad_maximum_fusion.11), channel_id=1, source_target_pairs={{0,6},{1,7},{2,4},{3,5},{4,2},{5,3},{6,0},{7,1},{8,14},{9,15},{10,... | collective-permute-start | bytes 393224 | tf_op jit(solution)/shard_map/ppermute | solution.py:91
  107.6 22.3 %collective-permute-start.16 = (f32[8,2048]{1,0:T(8,128)S(1)}, f32[8,2048]{1,0:T(8,128)S(1)}, u32[]{:S(2)}, u32[]{:S(2)}) collective-permute-start(f32[8,2048]{1,0:T(8,128)S(1)} %get-tuple-element.34.refs_2_), channel_id=1, source_target_pairs={{0,8},{8,16},{16,24},{24,0},{1,9},{9,17},{17,25},{25,1},{2,10},{10... | collective-permute-start | bytes 196616 | tf_op jit(solution)/shard_map/ppermute | solution.py:335
  109.1 20.7 %collective-permute-start.17 = (f32[8,2048]{1,0:T(8,128)S(1)}, f32[8,2048]{1,0:T(8,128)S(1)}, u32[]{:S(2)}, u32[]{:S(2)}) collective-permute-start(f32[8,2048]{1,0:T(8,128)S(1)} %get-tuple-element.34.refs_2_), channel_id=1, source_target_pairs={{0,16},{8,24},{16,0},{24,8},{1,17},{9,25},{17,1},{25,9},{2,18},{10... | collective-permute-start | bytes 196616 | tf_op jit(solution)/shard_map/ppermute | solution.py:335
  109.6 20.2 %collective-permute-start.18 = (f32[8,2048]{1,0:T(8,128)S(1)}, f32[8,2048]{1,0:T(8,128)S(1)}, u32[]{:S(2)}, u32[]{:S(2)}) collective-permute-start(f32[8,2048]{1,0:T(8,128)S(1)} %get-tuple-element.34.refs_2_), channel_id=1, source_target_pairs={{0,24},{8,0},{16,8},{24,16},{1,25},{9,1},{17,9},{25,17},{2,26},{10... | collective-permute-start | bytes 196616 | tf_op jit(solution)/shard_map/ppermute | solution.py:335
  126.9 4.3 %collective-permute-start.19 = (f32[8,2048]{1,0:T(8,128)S(1)}, f32[8,2048]{1,0:T(8,128)S(1)}, u32[]{:S(2)}, u32[]{:S(2)}) collective-permute-start(f32[8,2048]{1,0:T(8,128)S(1)} %get-tuple-element.35.refs_6_), channel_id=1, source_target_pairs={{0,8},{8,16},{16,24},{24,0},{1,9},{9,17},{17,25},{25,1},{2,10},{10... | collective-permute-start | bytes 196616 | tf_op jit(solution)/shard_map/ppermute | solution.py:335
  128.3 4.3 %collective-permute-start.20 = (f32[8,2048]{1,0:T(8,128)S(1)}, f32[8,2048]{1,0:T(8,128)S(1)}, u32[]{:S(2)}, u32[]{:S(2)}) collective-permute-start(f32[8,2048]{1,0:T(8,128)S(1)} %get-tuple-element.35.refs_6_), channel_id=1, source_target_pairs={{0,16},{8,24},{16,0},{24,8},{1,17},{9,25},{17,1},{25,9},{2,18},{10... | collective-permute-start | bytes 196616 | tf_op jit(solution)/shard_map/ppermute | solution.py:335
  129.8 5.2 %collective-permute-start.21 = (f32[8,2048]{1,0:T(8,128)S(1)}, f32[8,2048]{1,0:T(8,128)S(1)}, u32[]{:S(2)}, u32[]{:S(2)}) collective-permute-start(f32[8,2048]{1,0:T(8,128)S(1)} %get-tuple-element.35.refs_6_), channel_id=1, source_target_pairs={{0,24},{8,0},{16,8},{24,16},{1,25},{9,1},{17,9},{25,17},{2,26},{10... | collective-permute-start | bytes 196616 | tf_op jit(solution)/shard_map/ppermute | solution.py:335
  (5 other events, 4.0 us)

commit v2 on v0

v2 whole, which is shorter than its diff:
```python
import functools

import jax
import jax.numpy as jnp
from jax import lax
from jax.experimental import pallas as pl
from jax.experimental.pallas import tpu as pltpu
from jax.sharding import PartitionSpec as P

CLS = 1000
LANES = 128
GROUP = 16
blend = 0.8

SMEM = pl.BlockSpec(memory_space=pltpu.SMEM)
VMEM = pl.BlockSpec(memory_space=pltpu.VMEM)
ANY = pl.BlockSpec(memory_space=pl.ANY)
T_SHIFT, B_SHIFT = 20, 8


def params(mib):
    return pltpu.CompilerParams(vmem_limit_bytes=mib << 20)


def held(shape, dtype):
    return pltpu.VMEM(shape, dtype)


def sds(shape, dtype):
    return jax.ShapeDtypeStruct(shape, dtype)


def split_kernel(prior_ref, *outs):
    width = prior_ref.shape[-1]
    for c, out in enumerate(outs):
        start = c * LANES
        live = min(LANES, width - start)
        out[:, :, :live] = prior_ref[:, :, start : start + live]
        if live < LANES:
            out[:, :, live:] = jnp.zeros(out.shape[:2] + (LANES - live,), out.dtype)


def split(prior, tile_rows):
    tiles = prior.reshape(-1, tile_rows, prior.shape[1])
    chunks = pl.cdiv(prior.shape[1], LANES)
    return pl.pallas_call(
        split_kernel,
        out_shape=[held((tiles.shape[0], tile_rows, LANES), prior.dtype)] * chunks,
        in_specs=[VMEM],
        out_specs=[VMEM] * chunks,
        compiler_params=params(8),
        name="split",
    )(tiles)


def fill_lists(room, index, links_ref, counts_ref, fetch_ref, items_ref, sizes_ref):
    own, slots = links_ref.shape
    n = fetch_ref.shape[1]
    mine = fetch_ref[0, index, 0]

    def tile(t, sizes):
        def slot(j, sizes):
            v = links_ref[t, j]
            x = (v - own) ^ index
            is_own = jnp.logical_or(v < own, x == 0)
            kind = jnp.where(is_own, 0, jnp.where(x < n // 2, 1, 2))
            field = jnp.where(is_own, jnp.where(v < own, v, mine), x)
            place = jnp.where(kind == 0, sizes[0], jnp.where(kind == 1, sizes[1], sizes[2]))
            items_ref[kind * room + place] = (t << T_SHIFT) + ((t * slots + j) << B_SHIFT) + field
            return tuple(s + (kind == i).astype(jnp.int32) for i, s in enumerate(sizes))

        return lax.fori_loop(0, counts_ref[t], slot, sizes)

    sizes = lax.fori_loop(0, own, tile, (jnp.int32(0),) * 3)
    for kind in range(3):
        sizes_ref[kind] = sizes[kind]

        def fill(i, carry):
            items_ref[kind * room + sizes[kind] + i] = own << T_SHIFT
            return carry

        lax.fori_loop(0, GROUP, fill, 0)


def pick_kernel(chunks, me_ref, wanted_ref, *refs):
    tabs, outs = refs[:chunks], refs[chunks:]
    for c in range(chunks):
        for x in range(wanted_ref.shape[0]):
            outs[2 * c + x % 2][x // 2] = tabs[c][wanted_ref[me_ref[0] ^ x, 0, 0]]


def pick(me, wanted, tabs):
    n = wanted.shape[0]
    chunks = len(tabs)
    outs = pl.pallas_call(
        functools.partial(pick_kernel, chunks),
        out_shape=[held((n // 2,) + tabs[0].shape[1:], tabs[0].dtype)] * (2 * chunks),
        in_specs=[SMEM, SMEM] + [VMEM] * chunks,
        out_specs=[VMEM] * (2 * chunks),
        compiler_params=params(8),
        name="pick",
    )(me, wanted, *tabs)
    return [outs[2 * c : 2 * c + 2] for c in range(chunks)]


def after(value, *others):
    return lax.optimization_barrier((value, others))[0]


def across_core(across, n):
    pairs = [(i, i ^ 1) for i in range(n)]
    return [lax.ppermute(across[k], "rows", pairs) for k in range(across.shape[0])]


def messages(straight, got):
    return [jnp.stack([straight[k], got[k]]) for k in range(1, len(got))]


def send(parts, n):
    order = range(len(parts) - 1, -1, -1)
    arrived = [
        lax.ppermute(parts[k], "rows", [(i, i ^ (2 * k + 2)) for i in range(n)]) for k in order
    ]
    return arrived[::-1]


def run_list(kind, items_ref, sizes_ref, room, blocks, rhs, totals, ready=None):
    own = totals[0].shape[0] - 1
    low, high = (1 << B_SHIFT) - 1, (1 << (T_SHIFT - B_SHIFT)) - 1

    def step(g, waited):
        at = kind * room + g * GROUP
        if ready is not None:
            last = jnp.minimum(items_ref[at + GROUP - 1] >> T_SHIFT, own - 1) + 1
            lax.fori_loop(waited, last, ready, 0)
            waited = jnp.maximum(waited, last)
        for i in range(GROUP):
            word = items_ref[at + i]
            t = word >> T_SHIFT
            value = jnp.dot(
                blocks[(word >> B_SHIFT) & high],
                rhs(word & low),
                preferred_element_type=jnp.float32,
            )
            for c, total in enumerate(totals):
                total[t] += value[:, c * LANES : (c + 1) * LANES]
        return waited

    groups = (sizes_ref[kind] + GROUP - 1) // GROUP
    waited = lax.fori_loop(0, groups, step, jnp.int32(0))
    if ready is not None:
        lax.fori_loop(waited, own, ready, 0)


def column(ref, t, tile_rows):
    parts = tile_rows // LANES
    rows = [ref[pl.ds(t * parts + i, 1), :] for i in range(parts)]
    return jnp.concatenate(
        [jnp.broadcast_to(row, (LANES, LANES)).T for row in rows], axis=0
    )


def start_totals(me_ref, seeds_ref, totals):
    own, tile_rows = totals[0].shape[0] - 1, totals[0].shape[1]
    share = (1.0 - blend) / blend
    lane = lax.broadcasted_iota(jnp.int32, totals[0].shape[1:], 1)
    for t in range(own):
        seeds = column(seeds_ref, t, tile_rows) - me_ref[1]
        for c, total in enumerate(totals):
            total[t] = jnp.where(seeds == lane + c * LANES, share, 0.0)


def side_by_side(tabs):
    return lambda f: jnp.concatenate([tab[f] for tab in tabs], axis=1)


def begin_kernel(
    chunks, room, me_ref, links_ref, counts_ref, fetch_ref, blocks_hbm, seeds_ref, temp_ref, *refs
):
    tabs = refs[:chunks]
    items_ref, sizes_ref, blocks, wide_ref = refs[chunks : chunks + 4]
    totals, sems = refs[chunks + 4 : -1], refs[-1]
    own, slots = links_ref.shape
    tile_rows = blocks.shape[1]
    groups = sems.shape[1]
    size = slots // groups

    def copy(t, g):
        return pltpu.make_async_copy(
            blocks_hbm.at[pl.ds(t * slots + g * size, size)],
            blocks.at[pl.ds(t * slots + g * size, size)],
            sems.at[t, g],
        )

    def used(t):
        return (counts_ref[t] + size - 1) // size

    def begin(t, carry):
        return lax.fori_loop(0, used(t), lambda g, c: (copy(t, g).start(), c)[1], carry)

    def ready(t, carry):
        return lax.fori_loop(0, used(t), lambda g, c: (copy(t, g).wait(), c)[1], carry)

    lax.fori_loop(0, own, begin, 0)
    fill_lists(room, me_ref[0], links_ref, counts_ref, fetch_ref, items_ref, sizes_ref)
    for t in range(own):
        wide_ref[t] = blend * column(temp_ref, t, tile_rows)
    start_totals(me_ref, seeds_ref, totals)
    run_list(0, items_ref, sizes_ref, room, blocks, side_by_side(tabs), totals, ready)


def begin(me, links, counts, fetch, blocks, seeds, temp, tabs):
    own, tile_rows = tabs[0].shape[:2]
    slots = links.shape[1]
    room = links.size + GROUP
    chunks = len(tabs)
    size = next(g for g in (4, 3, 2, 1) if slots % g == 0)
    out = pl.pallas_call(
        functools.partial(begin_kernel, chunks, room),
        out_shape=[
            sds((3 * room,), jnp.int32),
            sds((3,), jnp.int32),
            held(blocks.shape, blocks.dtype),
            held(tabs[0].shape, jnp.float32),
        ]
        + [held((own + 1, tile_rows, LANES), jnp.float32)] * chunks,
        in_specs=[SMEM] * 4 + [ANY] + [VMEM] * (2 + chunks),
        out_specs=[SMEM] * 2 + [VMEM] * (2 + chunks),
        scratch_shapes=[pltpu.SemaphoreType.DMA((own, slots // size))],
        compiler_params=params(8),
        cost_estimate=COST,
        name="begin",
    )(me, links, counts, fetch, blocks, seeds, temp, *tabs)
    return out[:2], out[2], out[3], out[4:]


def own_kernel(chunks, room, me_ref, items_ref, sizes_ref, blocks, seeds_ref, *refs):
    tabs, totals = refs[:chunks], refs[chunks:]
    start_totals(me_ref, seeds_ref, totals)
    run_list(0, items_ref, sizes_ref, room, blocks, side_by_side(tabs), totals)


COST = pl.CostEstimate(flops=1, bytes_accessed=1, transcendentals=0)


def own_part(me, items, sizes, blocks, seeds, tabs):
    own, tile_rows = tabs[0].shape[:2]
    chunks = len(tabs)
    return pl.pallas_call(
        functools.partial(own_kernel, chunks, items.shape[0] // 3),
        out_shape=[held((own + 1, tile_rows, LANES), jnp.float32)] * chunks,
        in_specs=[SMEM] * 3 + [VMEM] * (2 + chunks),
        out_specs=[VMEM] * chunks,
        compiler_params=params(8),
        cost_estimate=COST,
        name="own_part",
    )(me, items, sizes, blocks, seeds, *tabs)


def gather_field(kinds, got, arrived, field):
    half = field.shape[0] // 2
    if 1 in kinds:
        field[1] = got[...]
    for k, one in enumerate(arrived):
        x = 2 * (k + 1)
        if (1 if x < half else 2) in kinds:
            field[x] = one[0]
            field[x + 1] = one[1]


def step1_kernel(links, room, me_ref, items_ref, sizes_ref, wanted_ref, blocks, got, *refs):
    arrived = refs[:links]
    begun, out, straight, across, field, total = refs[links:]
    own = out.shape[0]
    gather_field((1, 2), got, arrived, field)
    total[...] = begun[...]
    for kind in (1, 2):
        run_list(kind, items_ref, sizes_ref, room, blocks, lambda f: field[f], [total])
    for t in range(own):
        out[t] = (blend * total[t]).astype(out.dtype)
    for x in range(wanted_ref.shape[0]):
        (across if x % 2 else straight)[x // 2] = out[wanted_ref[me_ref[0] ^ x, 0, 0]]


def step1(me, items, sizes, wanted, blocks, got, arrived, begun):
    own, tile_rows = begun.shape[0] - 1, begun.shape[1]
    n = wanted.shape[0]
    half = held((n // 2, tile_rows, LANES), got.dtype)
    return pl.pallas_call(
        functools.partial(step1_kernel, len(arrived), items.shape[0] // 3),
        out_shape=[held((own, tile_rows, LANES), got.dtype), half, half],
        in_specs=[SMEM] * 4 + [VMEM] * (3 + len(arrived)),
        out_specs=[VMEM] * 3,
        scratch_shapes=[
            pltpu.VMEM((n, tile_rows, LANES), got.dtype),
            pltpu.VMEM(begun.shape, begun.dtype),
        ],
        compiler_params=params(12),
        cost_estimate=COST,
        name="step1",
    )(me, items, sizes, wanted, blocks, got, *arrived, begun)


def near_kernel(links, room, items_ref, sizes_ref, blocks, got, *refs):
    arrived = refs[:links]
    begun, total, field = refs[links:]
    gather_field((1,), got, arrived, field)
    total[...] = begun[...]
    run_list(1, items_ref, sizes_ref, room, blocks, lambda f: field[f], [total])


def near_part(items, sizes, blocks, got, arrived, begun, n):
    tile_rows = begun.shape[1]
    return pl.pallas_call(
        functools.partial(near_kernel, len(arrived), items.shape[0] // 3),
        out_shape=held(begun.shape, begun.dtype),
        in_specs=[SMEM] * 2 + [VMEM] * (3 + len(arrived)),
        out_specs=VMEM,
        scratch_shapes=[pltpu.VMEM((n, tile_rows, LANES), got.dtype)],
        compiler_params=params(8),
        cost_estimate=COST,
        name="near_part",
    )(items, sizes, blocks, got, *arrived, begun)


def step2_kernel(links, live, room, items_ref, sizes_ref, blocks, got, *refs):
    arrived = refs[:links]
    begun, wide_ref, expo_ref, stats_ref, field, total = refs[links:]
    own, tile_rows = expo_ref.shape[:2]
    gather_field((2,), got, arrived, field)
    total[...] = begun[...]
    run_list(2, items_ref, sizes_ref, room, blocks, lambda f: field[f], [total])
    parts = tile_rows // LANES
    for t in range(own):
        logits = wide_ref[t] * total[t]
        lane = lax.broadcasted_iota(jnp.int32, logits.shape, 1)
        if live < LANES:
            top = jnp.max(jnp.where(lane < live, logits, -jnp.inf), axis=1, keepdims=True)
            shifted = jnp.where(lane < live, logits - top, 0.0)
            expo = jnp.where(lane < live, jnp.exp(shifted), 0.0)
        else:
            top = jnp.max(logits, axis=1, keepdims=True)
            shifted = logits - top
            expo = jnp.exp(shifted)
        sums = jnp.sum(expo, axis=1, keepdims=True)
        moments = jnp.sum(expo * shifted, axis=1, keepdims=True)
        expo_ref[t] = expo
        summary = jnp.where(lane == 0, top, jnp.where(lane == 1, sums, moments))
        for i in range(parts):
            flat = summary[i * LANES : (i + 1) * LANES, :].T
            for q in range(3):
                stats_ref[q, t * parts + i : t * parts + i + 1, :] = flat[q : q + 1]


def step2(live, items, sizes, blocks, got, arrived, begun, wide):
    own, tile_rows = begun.shape[0] - 1, begun.shape[1]
    n = 2 * (len(arrived) + 1)
    return pl.pallas_call(
        functools.partial(step2_kernel, len(arrived), live, items.shape[0] // 3),
        out_shape=[
            held((own, tile_rows, LANES), jnp.float32),
            held((3, own * tile_rows // LANES, LANES), jnp.float32),
        ],
        in_specs=[SMEM] * 2 + [VMEM] * (4 + len(arrived)),
        out_specs=[VMEM] * 2,
        scratch_shapes=[
            pltpu.VMEM((n, tile_rows, LANES), got.dtype),
            pltpu.VMEM(begun.shape, begun.dtype),
        ],
        compiler_params=params(12),
        cost_estimate=COST,
        name="step2",
    )(items, sizes, blocks, got, *arrived, begun, wide)


def finish_kernel(chunks, parts, *refs):
    expos, stats = refs[:chunks], refs[chunks : chunks + chunks * parts]
    pseudo_ref, certainty_ref, scale_ref = refs[chunks + chunks * parts :]
    own, tile_rows = expos[0].shape[:2]
    width = pseudo_ref.shape[1]
    top = functools.reduce(jnp.maximum, [s[0] for s in stats])
    totals, moments, scales = 0.0, 0.0, []
    for s in stats:
        delta = s[0] - top
        scale = jnp.exp(delta)
        scales.append(scale)
        totals += scale * s[1]
        moments += scale * (s[2] + delta * s[1])
    certainty_ref[...] = 1.0 - (jnp.log(totals) - moments / totals) / jnp.log(jnp.float32(CLS))
    inverse = 1.0 / totals
    for c in range(chunks):
        scale_ref[c] = scales[c * parts] * inverse
    for t in range(own):
        span = slice(t * tile_rows, (t + 1) * tile_rows)
        for c in range(chunks):
            start = c * LANES
            live = min(LANES, width - start)
            value = expos[c][t] * column(scale_ref.at[c], t, tile_rows)
            pseudo_ref[span, start : start + live] = value[:, :live].astype(pseudo_ref.dtype)


def finish(expos, stats, width):
    own, tile_rows = expos[0].shape[:2]
    rows = own * tile_rows
    chunks, parts = len(expos), len(stats[0])
    flat = [s for part in stats for s in part]
    return pl.pallas_call(
        functools.partial(finish_kernel, chunks, parts),
        out_shape=[sds((rows, width), jnp.bfloat16), sds((rows // LANES, LANES), jnp.float32)],
        in_specs=[VMEM] * (len(expos) + len(flat)),
        out_specs=[VMEM] * 2,
        scratch_shapes=[pltpu.VMEM((chunks, rows // LANES, LANES), jnp.float32)],
        compiler_params=params(12),
        name="finish",
    )(*expos, *flat)


def local(prior, blocks, links, counts, fetch, seeds, inv_temp):
    width = prior.shape[1]
    tile_rows = blocks.shape[2]
    n = lax.axis_size("rows")
    parts = lax.axis_size("cls")
    chunks = pl.cdiv(width, LANES)
    me = jnp.stack([lax.axis_index("rows"), lax.axis_index("cls") * width]).astype(jnp.int32)
    wanted = lax.all_to_all(fetch, "rows", split_axis=1, concat_axis=0, tiled=True)
    tabs = split(prior, tile_rows)
    blocks = blocks.reshape((-1,) + blocks.shape[2:])
    seeds = seeds.reshape(-1, LANES)
    temp = inv_temp.reshape(-1, LANES)

    sent = pick(me, wanted, tabs)
    gots = [across_core(sent[c][1], n) for c in range(chunks)]
    parcels = messages(sent[0][0], gots[0])
    arrived = [send(parcels, n)]
    (items, sizes), blocks, wide, begun = begin(
        me, links, counts, fetch, after(blocks, parcels, gots[1:]), seeds, temp, tabs
    )
    for c in range(1, chunks):
        parcels = [after(part, begun) for part in messages(sent[c][0], gots[c])]
        arrived.append(send(parcels, n))
    firsts, there = [], []
    for c in range(chunks):
        out, straight, across = step1(
            me, items, sizes, wanted, blocks, gots[c][0], arrived[c], after(begun[c], parcels)
        )
        got = across_core(across, n)
        parcels = messages(straight, got)
        firsts.append(out)
        there.append((got[0], send(parcels, n)))
    begun = own_part(me, items, sizes, blocks, after(seeds, parcels), firsts)
    expos, stats = [], []
    for c in range(chunks):
        near = near_part(items, sizes, blocks, *there[c], begun[c], n)
        live = min(LANES, width - c * LANES)
        expo, summary = step2(live, items, sizes, blocks, *there[c], near, wide)
        expos.append(expo)
        stats.append(
            [summary]
            + [
                lax.ppermute(summary, "cls", [(i, (i + k) % parts) for i in range(parts)])
                for k in range(1, parts)
            ]
        )
    pseudo, certainty = finish(expos, stats, width)
    return pseudo, certainty.reshape(-1)


def solution(mesh):
    return jax.shard_map(
        local,
        mesh=mesh,
        in_specs=(
            P("rows", "cls"),
            P("rows", None, None, None),
            P("rows", None),
            P("rows"),
            P("rows", None, None),
            P("rows"),
            P("rows"),
        ),
        out_specs=(P("rows", "cls"), P("rows")),
        check_vma=False,
    )
```

time: 205 us -> 90.9 us (0.44)
  local copies, waits for them, and re-layouts: 64.1 us -> 3.46 us
  waiting for transfers between devices: 52.8 us -> 13.9 us
  Pallas kernels: 0 us -> 37.4 us
  matrix products: 35.8 us -> 0 us
  blocking collectives: 35.2 us -> 0 us
  starting transfers between devices: 7.12 us -> 34.4 us
  other arithmetic: 7.67 us -> 0.25 us
    gather x5 -> x0, local copies, waits for them, and re-layouts: 59.2 us -> none  [the longest x3 54.7 us: propagate_local(): adjacent_blocks = column_set[slot_tiles]]
    all_to_all x2 -> x1, waiting for transfers between devices: 52.8 us -> 3.18 us  [local(): lax.all_to_all(fetch, 'rows', split_axis=1, concat_axis=0, tiled=True)]
    pallas_call x0 -> x11, Pallas kernels: none -> 37.4 us  [the longest x1 10.2 us: begin(): pl.pallas_call(functools.partial(begin_kernel, chunks, room), out_shape=[...]
    dot_general x2 -> x0, matrix products: 35.8 us -> none  [propagate_local(): jnp.einsum('mvfg,mvgx->mfx', blocks, adjacent_blocks, preferred_element_t...]
    ppermute x0 -> x34, starting transfers between devices: none -> 28.1 us  [the longest x12 17.2 us: send(): lax.ppermute(parts[k], 'rows', [(i, i ^ 2 * k + 2) for i in range(n)])]
    all_gather x3 -> x0, blocking collectives: 23.5 us -> none  [combined_all(): everything = jax.tree.map(lambda part: lax.all_gather(part, axis), value)]
    all_to_all x1 -> x0, blocking collectives: 11.7 us -> none  [local(): lax.all_to_all(fetch, 'rows', split_axis=1, concat_axis=0, tiled=True)]
    ppermute x0 -> x34, waiting for transfers between devices: none -> 10.8 us  [the longest x16 5.21 us: across_core(): lax.ppermute(across[k], 'rows', pairs)]
  transfers between devices with their start and end apart: 2 -> 35, of which waited for: 2 -> 10; matrix products, arithmetic and copies ran while one was open for 0% -> 1% of each run, Pallas kernels for 0% -> 39%
where the time goes in v2:
time: 90.9 us; the launch traced here: 90.6 us
  Pallas kernels  37.4 us (41%)
  starting transfers between devices  34.4 us (38%)
  waiting for transfers between devices  13.9 us (15%)
  local copies, waits for them, and re-layouts  3.46 us (4%)
  between operations  1.1 us (1%)
    ppermute x12, starting transfers between devices, send(): lax.ppermute(parts[k], 'rows', [(i, i ^ 2 * k + 2) for i in range(n)])  17.2 us
    pallas_call x1, Pallas kernels, begin(): pl.pallas_call(functools.partial(begin_kernel, chunks, room), out_shape=[...  10.2 us
    ppermute x6, starting transfers between devices, local(): lax.ppermute(summary, 'cls', [(i, (i + k) % parts) for i in range(parts)])  7.71 us
    pallas_call x2, Pallas kernels, step1(): pl.pallas_call(functools.partial(step1_kernel, len(arrived), items.shape[...  7.48 us
    pallas_call x2, Pallas kernels, step2(): pl.pallas_call(functools.partial(step2_kernel, len(arrived), live, items....  7.29 us
    all_to_all x1, starting transfers between devices, local(): lax.all_to_all(fetch, 'rows', split_axis=1, concat_axis=0, tiled=True)  6.33 us
    pallas_call x1, Pallas kernels, own_part(): pl.pallas_call(functools.partial(own_kernel, chunks, items.shape[0] // 3)...  5.63 us
    ppermute x16, waiting for transfers between devices, across_core(): lax.ppermute(across[k], 'rows', pairs)  5.21 us
  transfers between devices with their start and end apart: 35, of which 10 were waited for; matrix products, arithmetic and copies ran while one was open for 1% of the time, Pallas kernels for 39%

profile of v2, /device:TPU:0, one launch (start us, length us, event | category | flops | bytes accessed | tf_op | source)
XLA Modules:
  0.0 90.6 jit_solution(3511898971326652777)
XLA Ops:
  0.6 1.3 %copy.18 = s32[1,8,1]{2,0,1:T(1,128)} copy(s32[1,8,1]{1,2,0:T(1,128)} %param.11) | data formatting | bytes 64 | tf_op args[4]
  2.0 6.3 %all-to-all-start = ((s32[1,8,1]{2,0,1:T(1,128)}), s32[1,8,1]{2,0,1:T(1,128)S(1)}, u32[]{:S(2)}, u32[]{:S(2)}) async-start(s32[1,8,1]{2,0,1:T(1,128)} %copy.18), calls=%async_computation | async-start | bytes 8192 | tf_op jit(solution)/shard_map/all_to_all | solution.py:425
  9.1 1.2 %copy-done.4 = bf16[2048,250]{1,0:T(8,128)(2,1)S(1)} copy-done((bf16[2048,250]{1,0:T(8,128)(2,1)S(1)}, bf16[2048,250]{1,0:T(8,128)(2,1)}, u32[]{:S(2)}) %copy-start.4) | copy-done | bytes 1024024
  10.6 3.2 %all-to-all-done = s32[1,8,1]{2,0,1:T(1,128)S(1)} async-done(((s32[1,8,1]{2,0,1:T(1,128)}), s32[1,8,1]{2,0,1:T(1,128)S(1)}, u32[]{:S(2)}, u32[]{:S(2)}) %all-to-all-start) | async-done | bytes 64 | tf_op jit(solution)/shard_map/all_to_all | solution.py:425
  18.0 3.1 %collective-permute-start.10 = (bf16[2,256,128]{2,1,0:T(8,128)(2,1)S(1)}, bf16[2,256,128]{2,1,0:T(8,128)(2,1)S(1)}, u32[]{:S(2)}, u32[]{:S(2)}) collective-permute-start(bf16[2,256,128]{2,1,0:T(8,128)(2,1)S(1)} %pad_maximum_fusion.2), channel_id=1, source_target_pairs={{0,6},{1,7},{2,4},{3,5},{4,2},{5,3},{6,0},{7,1},{8,14},{9,15},{10,... | collective-permute-start | bytes 393224 | tf_op jit(solution)/shard_map/ppermute | solution.py:122
  21.4 10.2 %begin.1 = (s32[624]{0:T(1024)S(1)}, s32[3]{0:T(128)S(1)}, bf16[192,256,256]{2,1,0:T(8,128)(2,1)S(1)}, f32[8,256,128]{2,1,0:T(8,128)S(1)}, f32[9,256,128]{2,1,0:T(8,128)S(1)}, /*index=5*/f32[9,256,128]{2,1,0:T(8,128)S(1)}) custom-call(s32[2]{0:T(128)S(1)} %pad_add_fusion.me_ref, s32[8,24]{1,0:T(8,128)S(1)} %copy-done.7, s32[8]{0:T(128)S(1)} %copy-done.8, ...), custom_call_target="tpu_custom_call" | custom-call | flops 1 | bytes 1 | tf_op jit(solution)/shard_map/begin/pallas_call | solution.py:218
  31.8 4.3 %collective-permute-start.20 = (bf16[2,256,128]{2,1,0:T(8,128)(2,1)S(1)}, bf16[2,256,128]{2,1,0:T(8,128)(2,1)S(1)}, u32[]{:S(2)}, u32[]{:S(2)}) collective-permute-start(bf16[2,256,128]{2,1,0:T(8,128)(2,1)S(1)} %pad_maximum_fusion.5), channel_id=1, source_target_pairs={{0,6},{1,7},{2,4},{3,5},{4,2},{5,3},{6,0},{7,1},{8,14},{9,15},{10,... | collective-permute-start | bytes 393224 | tf_op jit(solution)/shard_map/ppermute | solution.py:122
  36.1 3.7 %step1.2 = (bf16[8,256,128]{2,1,0:T(8,128)(2,1)S(1)}, bf16[4,256,128]{2,1,0:T(8,128)(2,1)S(1)}, bf16[4,256,128]{2,1,0:T(8,128)(2,1)S(1)}) custom-call(s32[2]{0:T(128)S(1)} %pad_add_fusion.me_ref, s32[624]{0:T(1024)S(1)} %get-tuple-element.41.items_ref, s32[3]{0:T(128)S(1)} %get-tuple-element.42.sizes_ref, s32[8,1,1]{2,1,0:T(1,128)S(1)} %bitcast.54, ...), custom_call_target="tpu_custom_call" | custom-call | flops 1 | bytes 1 | tf_op jit(solution)/shard_map/step1/pallas_call | solution.py:289
  44.2 3.0 %collective-permute-start.17 = (bf16[2,256,128]{2,1,0:T(8,128)(2,1)S(1)}, bf16[2,256,128]{2,1,0:T(8,128)(2,1)S(1)}, u32[]{:S(2)}, u32[]{:S(2)}) collective-permute-start(bf16[2,256,128]{2,1,0:T(8,128)(2,1)S(1)} %pad_maximum_fusion.8), channel_id=1, source_target_pairs={{0,6},{1,7},{2,4},{3,5},{4,2},{5,3},{6,0},{7,1},{8,14},{9,15},{10,... | collective-permute-start | bytes 393224 | tf_op jit(solution)/shard_map/ppermute | solution.py:122
  47.2 3.7 %step1.3 = (bf16[8,256,128]{2,1,0:T(8,128)(2,1)S(1)}, bf16[4,256,128]{2,1,0:T(8,128)(2,1)S(1)}, bf16[4,256,128]{2,1,0:T(8,128)(2,1)S(1)}) custom-call(s32[2]{0:T(128)S(1)} %pad_add_fusion.me_ref, s32[624]{0:T(1024)S(1)} %get-tuple-element.41.items_ref, s32[3]{0:T(128)S(1)} %get-tuple-element.42.sizes_ref, s32[8,1,1]{2,1,0:T(1,128)S(1)} %bitcast.55, ...), custom_call_target="tpu_custom_call" | custom-call | flops 1 | bytes 1 | tf_op jit(solution)/shard_map/step1/pallas_call | solution.py:289
  51.1 1.2 %collective-permute-done.23 = bf16[256,128]{1,0:T(8,128)(2,1)S(1)} collective-permute-done((bf16[256,128]{1,0:T(8,128)(2,1)S(1)}, bf16[256,128]{1,0:T(8,128)(2,1)S(1)}, u32[]{:S(2)}, u32[]{:S(2)}) %collective-permute-start.23) | collective-permute-done | bytes 65568 | tf_op jit(solution)/shard_map/ppermute | solution.py:112
  54.8 1.5 %collective-permute-start.26 = (bf16[2,256,128]{2,1,0:T(8,128)(2,1)S(1)}, bf16[2,256,128]{2,1,0:T(8,128)(2,1)S(1)}, u32[]{:S(2)}, u32[]{:S(2)}) collective-permute-start(bf16[2,256,128]{2,1,0:T(8,128)(2,1)S(1)} %pad_maximum_fusion.10), channel_id=1, source_target_pairs={{0,4},{1,5},{2,6},{3,7},{4,0},{5,1},{6,2},{7,3},{8,12},{9,13},{10,... | collective-permute-start | bytes 393224 | tf_op jit(solution)/shard_map/ppermute | solution.py:122
  56.3 3.0 %collective-permute-start.27 = (bf16[2,256,128]{2,1,0:T(8,128)(2,1)S(1)}, bf16[2,256,128]{2,1,0:T(8,128)(2,1)S(1)}, u32[]{:S(2)}, u32[]{:S(2)}) collective-permute-start(bf16[2,256,128]{2,1,0:T(8,128)(2,1)S(1)} %pad_maximum_fusion.11), channel_id=1, source_target_pairs={{0,6},{1,7},{2,4},{3,5},{4,2},{5,3},{6,0},{7,1},{8,14},{9,15},{10,... | collective-permute-start | bytes 393224 | tf_op jit(solution)/shard_map/ppermute | solution.py:122
  59.3 5.6 %own_part.1 = (f32[9,256,128]{2,1,0:T(8,128)S(1)}, f32[9,256,128]{2,1,0:T(8,128)S(1)}) custom-call(s32[2]{0:T(128)S(1)} %pad_add_fusion.me_ref, s32[624]{0:T(1024)S(1)} %get-tuple-element.41.items_ref, s32[3]{0:T(128)S(1)} %get-tuple-element.42.sizes_ref, bf16[192,256,256]{2,1,0:T(8,128)(2,1)S(1)} %get-tuple-element.43.blocks, s32[16,128]{1,0:T(8,128)S(1)} %bitcast.57, ...), custom_call_target="tpu_custom_call" | custom-call | flops 1 | bytes 1 | tf_op jit(solution)/shard_map/own_part/pallas_call | solution.py:249
  64.9 2.1 %near_part.2.refs_3_ = f32[9,256,128]{2,1,0:T(8,128)S(1)} custom-call(s32[624]{0:T(1024)S(1)} %get-tuple-element.41.items_ref, s32[3]{0:T(128)S(1)} %get-tuple-element.42.sizes_ref, bf16[192,256,256]{2,1,0:T(8,128)(2,1)S(1)} %get-tuple-element.43.blocks, bf16[256,128]{1,0:T(8,128)(2,1)S(1)} %collective-permute-done.11.got, ...), custom_call_target="tpu_custom_call" | custom-call | flops 1 | bytes 1 | tf_op jit(solution)/shard_map/near_part/pallas_call | solution.py:314
  67.1 3.6 %step2.2 = (f32[8,256,128]{2,1,0:T(8,128)S(1)}, f32[3,16,128]{2,1,0:T(8,128)S(1)}) custom-call(s32[624]{0:T(1024)S(1)} %get-tuple-element.41.items_ref, s32[3]{0:T(128)S(1)} %get-tuple-element.42.sizes_ref, bf16[192,256,256]{2,1,0:T(8,128)(2,1)S(1)} %get-tuple-element.43.blocks, bf16[256,128]{1,0:T(8,128)(2,1)S(1)} %collective-permute-done.11.got, ...), custom_call_target="tpu_custom_call" | custom-call | flops 1 | bytes 1 | tf_op jit(solution)/shard_map/step2/pallas_call | solution.py:358
  70.7 2.7 %collective-permute-start.30 = (f32[3,16,128]{2,1,0:T(8,128)S(1)}, f32[3,16,128]{2,1,0:T(8,128)S(1)}, u32[]{:S(2)}, u32[]{:S(2)}) collective-permute-start(f32[3,16,128]{2,1,0:T(8,128)S(1)} %get-tuple-element.64.refs_2_), channel_id=1, source_target_pairs={{0,24},{8,0},{16,8},{24,16},{1,25},{9,1},{17,9},{25,17},{2,26},{10... | collective-permute-start | bytes 73736 | tf_op jit(solution)/shard_map/ppermute | solution.py:460
  73.9 2.1 %near_part.3.refs_3_ = f32[9,256,128]{2,1,0:T(8,128)S(1)} custom-call(s32[624]{0:T(1024)S(1)} %get-tuple-element.41.items_ref, s32[3]{0:T(128)S(1)} %get-tuple-element.42.sizes_ref, bf16[192,256,256]{2,1,0:T(8,128)(2,1)S(1)} %get-tuple-element.43.blocks, bf16[256,128]{1,0:T(8,128)(2,1)S(1)} %collective-permute-done.24.got, ...), custom_call_target="tpu_custom_call" | custom-call | flops 1 | bytes 1 | tf_op jit(solution)/shard_map/near_part/pallas_call | solution.py:314
  76.7 3.7 %step2.3 = (f32[8,256,128]{2,1,0:T(8,128)S(1)}, f32[3,16,128]{2,1,0:T(8,128)S(1)}) custom-call(s32[624]{0:T(1024)S(1)} %get-tuple-element.41.items_ref, s32[3]{0:T(128)S(1)} %get-tuple-element.42.sizes_ref, bf16[192,256,256]{2,1,0:T(8,128)(2,1)S(1)} %get-tuple-element.43.blocks, bf16[256,128]{1,0:T(8,128)(2,1)S(1)} %collective-permute-done.24.got, ...), custom_call_target="tpu_custom_call" | custom-call | flops 1 | bytes 1 | tf_op jit(solution)/shard_map/step2/pallas_call | solution.py:358
  80.3 2.4 %collective-permute-start.33 = (f32[3,16,128]{2,1,0:T(8,128)S(1)}, f32[3,16,128]{2,1,0:T(8,128)S(1)}, u32[]{:S(2)}, u32[]{:S(2)}) collective-permute-start(f32[3,16,128]{2,1,0:T(8,128)S(1)} %get-tuple-element.65.refs_6_), channel_id=1, source_target_pairs={{0,24},{8,0},{16,8},{24,16},{1,25},{9,1},{17,9},{25,17},{2,26},{10... | collective-permute-start | bytes 73736 | tf_op jit(solution)/shard_map/ppermute | solution.py:460
  82.7 1.5 %collective-permute-start.32 = (f32[3,16,128]{2,1,0:T(8,128)S(1)}, f32[3,16,128]{2,1,0:T(8,128)S(1)}, u32[]{:S(2)}, u32[]{:S(2)}) collective-permute-start(f32[3,16,128]{2,1,0:T(8,128)S(1)} %get-tuple-element.65.refs_6_), channel_id=1, source_target_pairs={{0,16},{8,24},{16,0},{24,8},{1,17},{9,25},{17,1},{25,9},{2,18},{10... | collective-permute-start | bytes 73736 | tf_op jit(solution)/shard_map/ppermute | solution.py:460
  84.6 2.0 %collective-permute-done.32.refs_8_ = f32[3,16,128]{2,1,0:T(8,128)S(1)} collective-permute-done((f32[3,16,128]{2,1,0:T(8,128)S(1)}, f32[3,16,128]{2,1,0:T(8,128)S(1)}, u32[]{:S(2)}, u32[]{:S(2)}) %collective-permute-start.32) | collective-permute-done | bytes 24608 | tf_op jit(solution)/shard_map/ppermute | solution.py:460
  86.5 2.4 %collective-permute-done.31.refs_7_ = f32[3,16,128]{2,1,0:T(8,128)S(1)} collective-permute-done((f32[3,16,128]{2,1,0:T(8,128)S(1)}, f32[3,16,128]{2,1,0:T(8,128)S(1)}, u32[]{:S(2)}, u32[]{:S(2)}) %collective-permute-start.31) | collective-permute-done | bytes 24608 | tf_op jit(solution)/shard_map/ppermute | solution.py:460
  89.0 1.6 %finish.1 = (bf16[2048,250]{1,0:T(8,128)(2,1)}, f32[16,128]{1,0:T(8,128)}) custom-call(f32[8,256,128]{2,1,0:T(8,128)S(1)} %get-tuple-element.61.refs_0_, f32[8,256,128]{2,1,0:T(8,128)S(1)} %get-tuple-element.63.refs_1_, f32[3,16,128]{2,1,0:T(8,128)S(1)} %get-tuple-element.64.refs_2_, f32[3,16,128]{2,1,0:T(8,128)S(1)} %collective-permute-done.28.refs_3_, ...), custom_call_target="tpu_custom_call" | custom-call | tf_op jit(solution)/shard_map/finish/pallas_call | solution.py:407
  (97 shorter events, 13.9 us)
Async XLA Ops:
  2.0 11.8 %all-to-all-start = ((s32[1,8,1]{2,0,1:T(1,128)}), s32[1,8,1]{2,0,1:T(1,128)S(1)}, u32[]{:S(2)}, u32[]{:S(2)}) async-start(s32[1,8,1]{2,0,1:T(1,128)} %copy.18), calls=%async_computation | async-start | bytes 8192 | tf_op jit(solution)/shard_map/all_to_all | solution.py:425
  15.9 5.4 %collective-permute-start.4 = (bf16[256,128]{1,0:T(8,128)(2,1)S(1)}, bf16[256,128]{1,0:T(8,128)(2,1)S(1)}, u32[]{:S(2)}, u32[]{:S(2)}) collective-permute-start(bf16[256,128]{1,0:T(8,128)(2,1)S(1)} %get-tuple-element.91), channel_id=1, source_target_pairs={{0,1},{1,0},{2,3},{3,2},{4,5},{5,4},{6,7},{7,6},{8,9},{9,8},{10,11... | collective-permute-start | bytes 196616 | tf_op jit(solution)/shard_map/ppermute | solution.py:112
  16.4 4.9 %collective-permute-start.3 = (bf16[256,128]{1,0:T(8,128)(2,1)S(1)}, bf16[256,128]{1,0:T(8,128)(2,1)S(1)}, u32[]{:S(2)}, u32[]{:S(2)}) collective-permute-start(bf16[256,128]{1,0:T(8,128)(2,1)S(1)} %get-tuple-element.92), channel_id=1, source_target_pairs={{0,1},{1,0},{2,3},{3,2},{4,5},{5,4},{6,7},{7,6},{8,9},{9,8},{10,11... | collective-permute-start | bytes 196616 | tf_op jit(solution)/shard_map/ppermute | solution.py:112
  16.6 15.2 %collective-permute-start.8 = (bf16[2,256,128]{2,1,0:T(8,128)(2,1)S(1)}, bf16[2,256,128]{2,1,0:T(8,128)(2,1)S(1)}, u32[]{:S(2)}, u32[]{:S(2)}) collective-permute-start(bf16[2,256,128]{2,1,0:T(8,128)(2,1)S(1)} %pad_maximum_fusion), channel_id=1, source_target_pairs={{0,2},{1,3},{2,0},{3,1},{4,6},{5,7},{6,4},{7,5},{8,10},{9,11},{10,... | collective-permute-start | bytes 393224 | tf_op jit(solution)/shard_map/ppermute | solution.py:122
  17.2 18.9 %collective-permute-start.9 = (bf16[2,256,128]{2,1,0:T(8,128)(2,1)S(1)}, bf16[2,256,128]{2,1,0:T(8,128)(2,1)S(1)}, u32[]{:S(2)}, u32[]{:S(2)}) collective-permute-start(bf16[2,256,128]{2,1,0:T(8,128)(2,1)S(1)} %pad_maximum_fusion.1), channel_id=1, source_target_pairs={{0,4},{1,5},{2,6},{3,7},{4,0},{5,1},{6,2},{7,3},{8,12},{9,13},{10,... | collective-permute-start | bytes 393224 | tf_op jit(solution)/shard_map/ppermute | solution.py:122
  18.0 18.1 %collective-permute-start.10 = (bf16[2,256,128]{2,1,0:T(8,128)(2,1)S(1)}, bf16[2,256,128]{2,1,0:T(8,128)(2,1)S(1)}, u32[]{:S(2)}, u32[]{:S(2)}) collective-permute-start(bf16[2,256,128]{2,1,0:T(8,128)(2,1)S(1)} %pad_maximum_fusion.2), channel_id=1, source_target_pairs={{0,6},{1,7},{2,4},{3,5},{4,2},{5,3},{6,0},{7,1},{8,14},{9,15},{10,... | collective-permute-start | bytes 393224 | tf_op jit(solution)/shard_map/ppermute | solution.py:122
  21.2 10.5 %collective-permute-start.7 = (bf16[256,128]{1,0:T(8,128)(2,1)S(1)}, bf16[256,128]{1,0:T(8,128)(2,1)S(1)}, u32[]{:S(2)}, u32[]{:S(2)}) collective-permute-start(bf16[256,128]{1,0:T(8,128)(2,1)S(1)} %get-tuple-element.85), channel_id=1, source_target_pairs={{0,1},{1,0},{2,3},{3,2},{4,5},{5,4},{6,7},{7,6},{8,9},{9,8},{10,11... | collective-permute-start | bytes 196616 | tf_op jit(solution)/shard_map/ppermute | solution.py:112
  31.6 11.1 %collective-permute-start.18 = (bf16[2,256,128]{2,1,0:T(8,128)(2,1)S(1)}, bf16[2,256,128]{2,1,0:T(8,128)(2,1)S(1)}, u32[]{:S(2)}, u32[]{:S(2)}) collective-permute-start(bf16[2,256,128]{2,1,0:T(8,128)(2,1)S(1)} %pad_maximum_fusion.3), channel_id=1, source_target_pairs={{0,2},{1,3},{2,0},{3,1},{4,6},{5,7},{6,4},{7,5},{8,10},{9,11},{10,... | collective-permute-start | bytes 393224 | tf_op jit(solution)/shard_map/ppermute | solution.py:122
  31.7 12.5 %collective-permute-start.19 = (bf16[2,256,128]{2,1,0:T(8,128)(2,1)S(1)}, bf16[2,256,128]{2,1,0:T(8,128)(2,1)S(1)}, u32[]{:S(2)}, u32[]{:S(2)}) collective-permute-start(bf16[2,256,128]{2,1,0:T(8,128)(2,1)S(1)} %pad_maximum_fusion.4), channel_id=1, source_target_pairs={{0,4},{1,5},{2,6},{3,7},{4,0},{5,1},{6,2},{7,3},{8,12},{9,13},{10,... | collective-permute-start | bytes 393224 | tf_op jit(solution)/shard_map/ppermute | solution.py:122
  31.8 15.4 %collective-permute-start.20 = (bf16[2,256,128]{2,1,0:T(8,128)(2,1)S(1)}, bf16[2,256,128]{2,1,0:T(8,128)(2,1)S(1)}, u32[]{:S(2)}, u32[]{:S(2)}) collective-permute-start(bf16[2,256,128]{2,1,0:T(8,128)(2,1)S(1)} %pad_maximum_fusion.5), channel_id=1, source_target_pairs={{0,6},{1,7},{2,4},{3,5},{4,2},{5,3},{6,0},{7,1},{8,14},{9,15},{10,... | collective-permute-start | bytes 393224 | tf_op jit(solution)/shard_map/ppermute | solution.py:122
  42.4 12.4 %collective-permute-start.11 = (bf16[256,128]{1,0:T(8,128)(2,1)S(1)}, bf16[256,128]{1,0:T(8,128)(2,1)S(1)}, u32[]{:S(2)}, u32[]{:S(2)}) collective-permute-start(bf16[256,128]{1,0:T(8,128)(2,1)S(1)} %get-tuple-element.81), channel_id=1, source_target_pairs={{0,1},{1,0},{2,3},{3,2},{4,5},{5,4},{6,7},{7,6},{8,9},{9,8},{10,11... | collective-permute-start | bytes 196616 | tf_op jit(solution)/shard_map/ppermute | solution.py:112
  42.6 13.7 %collective-permute-start.13 = (bf16[2,256,128]{2,1,0:T(8,128)(2,1)S(1)}, bf16[2,256,128]{2,1,0:T(8,128)(2,1)S(1)}, u32[]{:S(2)}, u32[]{:S(2)}) collective-permute-start(bf16[2,256,128]{2,1,0:T(8,128)(2,1)S(1)} %pad_maximum_fusion.6), channel_id=1, source_target_pairs={{0,2},{1,3},{2,0},{3,1},{4,6},{5,7},{6,4},{7,5},{8,10},{9,11},{10,... | collective-permute-start | bytes 393224 | tf_op jit(solution)/shard_map/ppermute | solution.py:122
  42.7 16.5 %collective-permute-start.15 = (bf16[2,256,128]{2,1,0:T(8,128)(2,1)S(1)}, bf16[2,256,128]{2,1,0:T(8,128)(2,1)S(1)}, u32[]{:S(2)}, u32[]{:S(2)}) collective-permute-start(bf16[2,256,128]{2,1,0:T(8,128)(2,1)S(1)} %pad_maximum_fusion.7), channel_id=1, source_target_pairs={{0,4},{1,5},{2,6},{3,7},{4,0},{5,1},{6,2},{7,3},{8,12},{9,13},{10,... | collective-permute-start | bytes 393224 | tf_op jit(solution)/shard_map/ppermute | solution.py:122
  44.2 20.7 %collective-permute-start.17 = (bf16[2,256,128]{2,1,0:T(8,128)(2,1)S(1)}, bf16[2,256,128]{2,1,0:T(8,128)(2,1)S(1)}, u32[]{:S(2)}, u32[]{:S(2)}) collective-permute-start(bf16[2,256,128]{2,1,0:T(8,128)(2,1)S(1)} %pad_maximum_fusion.8), channel_id=1, source_target_pairs={{0,6},{1,7},{2,4},{3,5},{4,2},{5,3},{6,0},{7,1},{8,14},{9,15},{10,... | collective-permute-start | bytes 393224 | tf_op jit(solution)/shard_map/ppermute | solution.py:122
  54.8 19.1 %collective-permute-start.25 = (bf16[2,256,128]{2,1,0:T(8,128)(2,1)S(1)}, bf16[2,256,128]{2,1,0:T(8,128)(2,1)S(1)}, u32[]{:S(2)}, u32[]{:S(2)}) collective-permute-start(bf16[2,256,128]{2,1,0:T(8,128)(2,1)S(1)} %pad_maximum_fusion.9), channel_id=1, source_target_pairs={{0,2},{1,3},{2,0},{3,1},{4,6},{5,7},{6,4},{7,5},{8,10},{9,11},{10,... | collective-permute-start | bytes 393224 | tf_op jit(solution)/shard_map/ppermute | solution.py:122
  54.8 19.1 %collective-permute-start.26 = (bf16[2,256,128]{2,1,0:T(8,128)(2,1)S(1)}, bf16[2,256,128]{2,1,0:T(8,128)(2,1)S(1)}, u32[]{:S(2)}, u32[]{:S(2)}) collective-permute-start(bf16[2,256,128]{2,1,0:T(8,128)(2,1)S(1)} %pad_maximum_fusion.10), channel_id=1, source_target_pairs={{0,4},{1,5},{2,6},{3,7},{4,0},{5,1},{6,2},{7,3},{8,12},{9,13},{10,... | collective-permute-start | bytes 393224 | tf_op jit(solution)/shard_map/ppermute | solution.py:122
  56.3 17.6 %collective-permute-start.27 = (bf16[2,256,128]{2,1,0:T(8,128)(2,1)S(1)}, bf16[2,256,128]{2,1,0:T(8,128)(2,1)S(1)}, u32[]{:S(2)}, u32[]{:S(2)}) collective-permute-start(bf16[2,256,128]{2,1,0:T(8,128)(2,1)S(1)} %pad_maximum_fusion.11), channel_id=1, source_target_pairs={{0,6},{1,7},{2,4},{3,5},{4,2},{5,3},{6,0},{7,1},{8,14},{9,15},{10,... | collective-permute-start | bytes 393224 | tf_op jit(solution)/shard_map/ppermute | solution.py:122
  59.3 14.1 %collective-permute-start.24 = (bf16[256,128]{1,0:T(8,128)(2,1)S(1)}, bf16[256,128]{1,0:T(8,128)(2,1)S(1)}, u32[]{:S(2)}, u32[]{:S(2)}) collective-permute-start(bf16[256,128]{1,0:T(8,128)(2,1)S(1)} %get-tuple-element.68), channel_id=1, source_target_pairs={{0,1},{1,0},{2,3},{3,2},{4,5},{5,4},{6,7},{7,6},{8,9},{9,8},{10,11... | collective-permute-start | bytes 196616 | tf_op jit(solution)/shard_map/ppermute | solution.py:112
  70.7 13.5 %collective-permute-start.30 = (f32[3,16,128]{2,1,0:T(8,128)S(1)}, f32[3,16,128]{2,1,0:T(8,128)S(1)}, u32[]{:S(2)}, u32[]{:S(2)}) collective-permute-start(f32[3,16,128]{2,1,0:T(8,128)S(1)} %get-tuple-element.64.refs_2_), channel_id=1, source_target_pairs={{0,24},{8,0},{16,8},{24,16},{1,25},{9,1},{17,9},{25,17},{2,26},{10... | collective-permute-start | bytes 73736 | tf_op jit(solution)/shard_map/ppermute | solution.py:460
  73.4 10.9 %collective-permute-start.29 = (f32[3,16,128]{2,1,0:T(8,128)S(1)}, f32[3,16,128]{2,1,0:T(8,128)S(1)}, u32[]{:S(2)}, u32[]{:S(2)}) collective-permute-start(f32[3,16,128]{2,1,0:T(8,128)S(1)} %get-tuple-element.64.refs_2_), channel_id=1, source_target_pairs={{0,16},{8,24},{16,0},{24,8},{1,17},{9,25},{17,1},{25,9},{2,18},{10... | collective-permute-start | bytes 73736 | tf_op jit(solution)/shard_map/ppermute | solution.py:460
  76.0 8.2 %collective-permute-start.28 = (f32[3,16,128]{2,1,0:T(8,128)S(1)}, f32[3,16,128]{2,1,0:T(8,128)S(1)}, u32[]{:S(2)}, u32[]{:S(2)}) collective-permute-start(f32[3,16,128]{2,1,0:T(8,128)S(1)} %get-tuple-element.64.refs_2_), channel_id=1, source_target_pairs={{0,8},{8,16},{16,24},{24,0},{1,9},{9,17},{17,25},{25,1},{2,10},{10... | collective-permute-start | bytes 73736 | tf_op jit(solution)/shard_map/ppermute | solution.py:460
  80.3 4.2 %collective-permute-start.33 = (f32[3,16,128]{2,1,0:T(8,128)S(1)}, f32[3,16,128]{2,1,0:T(8,128)S(1)}, u32[]{:S(2)}, u32[]{:S(2)}) collective-permute-start(f32[3,16,128]{2,1,0:T(8,128)S(1)} %get-tuple-element.65.refs_6_), channel_id=1, source_target_pairs={{0,24},{8,0},{16,8},{24,16},{1,25},{9,1},{17,9},{25,17},{2,26},{10... | collective-permute-start | bytes 73736 | tf_op jit(solution)/shard_map/ppermute | solution.py:460
  82.7 3.8 %collective-permute-start.32 = (f32[3,16,128]{2,1,0:T(8,128)S(1)}, f32[3,16,128]{2,1,0:T(8,128)S(1)}, u32[]{:S(2)}, u32[]{:S(2)}) collective-permute-start(f32[3,16,128]{2,1,0:T(8,128)S(1)} %get-tuple-element.65.refs_6_), channel_id=1, source_target_pairs={{0,16},{8,24},{16,0},{24,8},{1,17},{9,25},{17,1},{25,9},{2,18},{10... | collective-permute-start | bytes 73736 | tf_op jit(solution)/shard_map/ppermute | solution.py:460
  84.2 4.7 %collective-permute-start.31 = (f32[3,16,128]{2,1,0:T(8,128)S(1)}, f32[3,16,128]{2,1,0:T(8,128)S(1)}, u32[]{:S(2)}, u32[]{:S(2)}) collective-permute-start(f32[3,16,128]{2,1,0:T(8,128)S(1)} %get-tuple-element.65.refs_6_), channel_id=1, source_target_pairs={{0,8},{8,16},{16,24},{24,0},{1,9},{9,17},{17,25},{25,1},{2,10},{10... | collective-permute-start | bytes 73736 | tf_op jit(solution)/shard_map/ppermute | solution.py:460
  (20 other events, 65.5 us)

commit v3 on v2

v3 whole, which is shorter than its diff:
```python
import functools

import jax
import jax.numpy as jnp
from jax import lax
from jax.experimental import pallas as pl
from jax.experimental.pallas import tpu as pltpu
from jax.sharding import PartitionSpec as P

CLS = 1000
LANES = 128
GROUP = 16
blend = 0.8

SMEM = pl.BlockSpec(memory_space=pltpu.SMEM)
VMEM = pl.BlockSpec(memory_space=pltpu.VMEM)
ANY = pl.BlockSpec(memory_space=pl.ANY)
T_SHIFT, B_SHIFT = 20, 8


COST = pl.CostEstimate(flops=1, bytes_accessed=1, transcendentals=0)


def params(mib):
    return pltpu.CompilerParams(vmem_limit_bytes=mib << 20)


def held(shape, dtype):
    return pltpu.VMEM(shape, dtype)


def sds(shape, dtype):
    return jax.ShapeDtypeStruct(shape, dtype)


def split_kernel(prior_ref, *outs):
    width = prior_ref.shape[-1]
    for c, out in enumerate(outs):
        start = c * LANES
        live = min(LANES, width - start)
        out[:, :, :live] = prior_ref[:, :, start : start + live]
        if live < LANES:
            out[:, :, live:] = jnp.zeros(out.shape[:2] + (LANES - live,), out.dtype)


def split(prior, tile_rows):
    tiles = prior.reshape(-1, tile_rows, prior.shape[1])
    chunks = pl.cdiv(prior.shape[1], LANES)
    return pl.pallas_call(
        split_kernel,
        out_shape=[held((tiles.shape[0], tile_rows, LANES), prior.dtype)] * chunks,
        in_specs=[VMEM],
        out_specs=[VMEM] * chunks,
        compiler_params=params(8),
        name="split",
    )(tiles)


def fill_lists(room, index, links_ref, counts_ref, fetch_ref, items_ref, sizes_ref):
    own, slots = links_ref.shape
    n = fetch_ref.shape[0]
    mine = fetch_ref[index]

    def tile(t, sizes):
        def slot(j, sizes):
            v = links_ref[t, j]
            x = (v - own) ^ index
            is_own = jnp.logical_or(v < own, x == 0)
            is_near = jnp.logical_and(jnp.logical_not(is_own), x < n // 2)
            field = jnp.where(is_own, jnp.where(v < own, v, mine), x)
            place = jnp.where(
                is_own, sizes[0], jnp.where(is_near, 2 * room + sizes[1], 2 * room - 1 - sizes[2])
            )
            items_ref[place] = (t << T_SHIFT) + ((t * slots + j) << B_SHIFT) + field
            is_far = jnp.logical_not(jnp.logical_or(is_own, is_near))
            return tuple(
                size + kind.astype(jnp.int32) for size, kind in zip(sizes, (is_own, is_near, is_far))
            )

        return lax.fori_loop(0, counts_ref[t], slot, sizes)

    sizes = lax.fori_loop(0, own, tile, (jnp.int32(0),) * 3)
    for kind in range(3):
        sizes_ref[kind] = sizes[kind]
    sizes_ref[3] = fetch_ref[index ^ 1]

    def fill(i, carry):
        items_ref[sizes[0] + i] = own << T_SHIFT
        items_ref[2 * room + sizes[1] + i] = own << T_SHIFT
        items_ref[2 * room - sizes[2] - 1 - i] = own << T_SHIFT
        return carry

    lax.fori_loop(0, GROUP, fill, 0)


def groups_of(count):
    return (count + GROUP - 1) // GROUP


def own_list(room, sizes_ref):
    return 0, groups_of(sizes_ref[0])


def near_list(room, sizes_ref):
    return 2 * room, groups_of(sizes_ref[1])


def far_list(room, sizes_ref):
    groups = groups_of(sizes_ref[2])
    return 2 * room - groups * GROUP, groups


def both_lists(room, sizes_ref):
    return 2 * room - sizes_ref[2], groups_of(sizes_ref[1] + sizes_ref[2])


def ask_kernel(fetch_ref, out_ref):
    for i in range(fetch_ref.shape[0]):
        for j in range(2):
            out_ref[i, 0, j] = fetch_ref[i // 2 * 2 + j]


def ask(fetch):
    return pl.pallas_call(
        ask_kernel,
        out_shape=sds((fetch.shape[0], 1, 2), fetch.dtype),
        in_specs=[SMEM],
        out_specs=SMEM,
        name="ask",
    )(fetch)


def pick_kernel(chunks, me_ref, wanted_ref, *refs):
    tabs, neighbours, outs = refs[:chunks], refs[chunks : 2 * chunks], refs[2 * chunks :]
    index = me_ref[0]
    low = index & 1
    count = len(outs) // chunks
    for c in range(chunks):
        for k in range(count):
            to = index ^ (2 * k + 2)
            outs[c * count + k][0] = tabs[c][wanted_ref[to, 0, low]]
            outs[c * count + k][1] = neighbours[c][wanted_ref[to, 0, 1 - low]]


def pick(me, wanted, tabs, neighbours):
    chunks = len(tabs)
    count = wanted.shape[0] // 2 - 1
    outs = pl.pallas_call(
        functools.partial(pick_kernel, chunks),
        out_shape=[held((2,) + tabs[0].shape[1:], tabs[0].dtype)] * (chunks * count),
        in_specs=[SMEM, SMEM] + [VMEM] * (2 * chunks),
        out_specs=[VMEM] * (chunks * count),
        compiler_params=params(8),
        name="pick",
    )(me, wanted, *tabs, *neighbours)
    return [outs[c * count : (c + 1) * count] for c in range(chunks)]


def stay(arrays):
    return [pltpu.with_memory_space_constraint(array, pltpu.VMEM) for array in arrays]


def after(value, *others):
    return lax.optimization_barrier((value, others))[0]


def swap(value, n):
    return lax.ppermute(value, "rows", [(i, i ^ 1) for i in range(n)])


def across_core(across, n):
    half = across.shape[0] // 2
    late, early = swap(across[:half], n), swap(across[half:], n)
    return [late[k] for k in range(half)] + [early[k] for k in range(half)]


def messages(straight, got):
    return [jnp.stack([straight[k], got[k]]) for k in range(1, len(got))]


def send(parts, n):
    order = range(len(parts) - 1, -1, -1)
    arrived = [
        lax.ppermute(parts[k], "rows", [(i, i ^ (2 * k + 2)) for i in range(n)]) for k in order
    ]
    return arrived[::-1]


def run_list(which, items_ref, blocks, rhs, totals):
    first, groups = which
    low, high = (1 << B_SHIFT) - 1, (1 << (T_SHIFT - B_SHIFT)) - 1

    def step(g, carry):
        for i in range(GROUP):
            word = items_ref[first + g * GROUP + i]
            t = word >> T_SHIFT
            value = jnp.dot(
                blocks[(word >> B_SHIFT) & high],
                rhs(word & low),
                preferred_element_type=jnp.float32,
            )
            for c, total in enumerate(totals):
                total[t] += value[:, c * LANES : (c + 1) * LANES]
        return carry

    lax.fori_loop(0, groups, step, 0)


def column(ref, t, tile_rows):
    parts = tile_rows // LANES
    rows = [ref[pl.ds(t * parts + i, 1), :] for i in range(parts)]
    return jnp.concatenate(
        [jnp.broadcast_to(row, (LANES, LANES)).T for row in rows], axis=0
    )


def target_parts(me_ref, seeds_ref, parts):
    own, tile_rows = parts[0].shape[:2]
    share = (1.0 - blend) / blend
    lane = lax.broadcasted_iota(jnp.int32, parts[0].shape[1:], 1)
    for t in range(own):
        seeds = column(seeds_ref, t, tile_rows) - me_ref[1]
        for c, part in enumerate(parts):
            part[t] = jnp.where(seeds == lane + c * LANES, share, 0.0)


def start_totals(parts, totals):
    for part, total in zip(parts, totals):
        total[: part.shape[0]] = part[...]


def side_by_side(tabs):
    return lambda f: jnp.concatenate([tab[f] for tab in tabs], axis=1)


def load_kernel(
    room, me_ref, links_ref, counts_ref, fetch_ref, blocks_hbm, seeds_ref, temp_ref, *refs
):
    items_ref, sizes_ref, blocks, wide_ref = refs[:4]
    targets, sems = refs[4:-1], refs[-1]
    own, slots = links_ref.shape
    tile_rows = blocks.shape[1]
    groups = sems.shape[1]
    size = slots // groups

    def copy(t, g):
        return pltpu.make_async_copy(
            blocks_hbm.at[pl.ds(t * slots + g * size, size)],
            blocks.at[pl.ds(t * slots + g * size, size)],
            sems.at[t, g],
        )

    def used(t):
        return (counts_ref[t] + size - 1) // size

    def begin(t, carry):
        return lax.fori_loop(0, used(t), lambda g, c: (copy(t, g).start(), c)[1], carry)

    def ready(t, carry):
        return lax.fori_loop(0, used(t), lambda g, c: (copy(t, g).wait(), c)[1], carry)

    lax.fori_loop(0, own, begin, 0)
    fill_lists(room, me_ref[0], links_ref, counts_ref, fetch_ref, items_ref, sizes_ref)
    for t in range(own):
        wide_ref[t] = blend * column(temp_ref, t, tile_rows)
    target_parts(me_ref, seeds_ref, targets)
    lax.fori_loop(0, own, ready, 0)


def load(me, links, counts, fetch, blocks, seeds, temp, chunks):
    own, slots = links.shape
    tile_rows = blocks.shape[1]
    room = links.size + GROUP
    size = next(g for g in (4, 3, 2, 1) if slots % g == 0)
    wide = held((own, tile_rows, LANES), jnp.float32)
    out = pl.pallas_call(
        functools.partial(load_kernel, room),
        out_shape=[
            sds((3 * room,), jnp.int32),
            sds((4,), jnp.int32),
            held(blocks.shape, blocks.dtype),
        ]
        + [wide] * (1 + chunks),
        in_specs=[SMEM] * 4 + [ANY] + [VMEM] * 2,
        out_specs=[SMEM] * 2 + [VMEM] * (2 + chunks),
        scratch_shapes=[pltpu.SemaphoreType.DMA((own, slots // size))],
        compiler_params=params(8),
        cost_estimate=COST,
        name="load",
    )(me, links, counts, fetch, blocks, seeds, temp)
    return out[:2], out[2], out[3], out[4:]


def own_kernel(chunks, room, items_ref, sizes_ref, blocks, *refs):
    targets, tabs, totals = refs[:chunks], refs[chunks : 2 * chunks], refs[2 * chunks :]
    start_totals(targets, totals)
    run_list(own_list(room, sizes_ref), items_ref, blocks, side_by_side(tabs), totals)


def own_part(items, sizes, blocks, targets, tabs):
    own, tile_rows = tabs[0].shape[:2]
    chunks = len(tabs)
    return pl.pallas_call(
        functools.partial(own_kernel, chunks, items.shape[0] // 3),
        out_shape=[held((own + 1, tile_rows, LANES), jnp.float32)] * chunks,
        in_specs=[SMEM] * 2 + [VMEM] * (1 + 2 * chunks),
        out_specs=[VMEM] * chunks,
        compiler_params=params(8),
        cost_estimate=COST,
        name="own_part",
    )(items, sizes, blocks, *targets, *tabs)


def gather_field(near, far, beside, arrived, field):
    half = field.shape[0] // 2
    if near:
        field[1] = beside
    for k, one in enumerate(arrived):
        x = 2 * (k + 1)
        if near if x < half else far:
            field[x] = one[0]
            field[x + 1] = one[1]


def step1_kernel(
    links, room, me_ref, items_ref, sizes_ref, wanted_ref, blocks, neighbour, *refs
):
    arrived = refs[:links]
    begun, out, straight, across, field, total = refs[links:]
    own = out.shape[0]
    gather_field(True, True, neighbour[sizes_ref[3]], arrived, field)
    total[...] = begun[...]
    run_list(both_lists(room, sizes_ref), items_ref, blocks, lambda f: field[f], [total])
    for t in range(own):
        out[t] = (blend * total[t]).astype(out.dtype)
    index = me_ref[0]
    low = index & 1
    for x in range(field.shape[0]):
        (across if x % 2 else straight)[x // 2] = out[wanted_ref[index ^ x, 0, low]]


def step1(me, items, sizes, wanted, blocks, neighbour, arrived, begun):
    own, tile_rows = begun.shape[0] - 1, begun.shape[1]
    n = wanted.shape[0]
    dtype = neighbour.dtype
    half = held((n // 2, tile_rows, LANES), dtype)
    return pl.pallas_call(
        functools.partial(step1_kernel, len(arrived), items.shape[0] // 3),
        out_shape=[held((own, tile_rows, LANES), dtype), half, half],
        in_specs=[SMEM] * 4 + [VMEM] * (3 + len(arrived)),
        out_specs=[VMEM] * 3,
        scratch_shapes=[
            pltpu.VMEM((n, tile_rows, LANES), dtype),
            pltpu.VMEM(begun.shape, begun.dtype),
        ],
        compiler_params=params(12),
        cost_estimate=COST,
        name="step1",
    )(me, items, sizes, wanted, blocks, neighbour, *arrived, begun)


def near_kernel(links, room, items_ref, sizes_ref, blocks, beside, *refs):
    arrived = refs[:links]
    begun, total, field = refs[links:]
    gather_field(True, False, beside[...], arrived, field)
    total[...] = begun[...]
    run_list(near_list(room, sizes_ref), items_ref, blocks, lambda f: field[f], [total])


def near_part(items, sizes, blocks, beside, arrived, begun, n):
    tile_rows = begun.shape[1]
    return pl.pallas_call(
        functools.partial(near_kernel, len(arrived), items.shape[0] // 3),
        out_shape=held(begun.shape, begun.dtype),
        in_specs=[SMEM] * 2 + [VMEM] * (3 + len(arrived)),
        out_specs=VMEM,
        scratch_shapes=[pltpu.VMEM((n, tile_rows, LANES), beside.dtype)],
        compiler_params=params(8),
        cost_estimate=COST,
        name="near_part",
    )(items, sizes, blocks, beside, *arrived, begun)


def step2_kernel(links, live, near, room, items_ref, sizes_ref, blocks, beside, *refs):
    arrived = refs[:links]
    begun, wide_ref = refs[links : links + 2]
    *earlier, expo_ref, stats_ref, field, total = refs[links + 2 :]
    own, tile_rows = expo_ref.shape[:2]
    gather_field(near, True, beside[...], arrived, field)
    total[...] = begun[...]
    which = (both_lists if near else far_list)(room, sizes_ref)
    run_list(which, items_ref, blocks, lambda f: field[f], [total])
    parts = tile_rows // LANES
    last = stats_ref.shape[0] - 1
    if earlier:
        stats_ref[:last] = earlier[0][...]
    for t in range(own):
        logits = wide_ref[t] * total[t]
        lane = lax.broadcasted_iota(jnp.int32, logits.shape, 1)
        if live < LANES:
            top = jnp.max(jnp.where(lane < live, logits, -jnp.inf), axis=1, keepdims=True)
            shifted = jnp.where(lane < live, logits - top, 0.0)
            expo = jnp.where(lane < live, jnp.exp(shifted), 0.0)
        else:
            top = jnp.max(logits, axis=1, keepdims=True)
            shifted = logits - top
            expo = jnp.exp(shifted)
        sums = jnp.sum(expo, axis=1, keepdims=True)
        moments = jnp.sum(expo * shifted, axis=1, keepdims=True)
        expo_ref[t] = expo
        summary = jnp.where(lane == 0, top, jnp.where(lane == 1, sums, moments))
        for i in range(parts):
            flat = summary[i * LANES : (i + 1) * LANES, :].T
            for q in range(3):
                stats_ref[last, q, t * parts + i : t * parts + i + 1, :] = flat[q : q + 1]


def step2(live, near, items, sizes, blocks, beside, arrived, begun, wide, earlier):
    own, tile_rows = begun.shape[0] - 1, begun.shape[1]
    n = 2 * (len(arrived) + 1)
    before = () if earlier is None else (earlier,)
    count = 1 + (earlier.shape[0] if before else 0)
    return pl.pallas_call(
        functools.partial(step2_kernel, len(arrived), live, near, items.shape[0] // 3),
        out_shape=[
            held((own, tile_rows, LANES), jnp.float32),
            held((count, 3, own * tile_rows // LANES, LANES), jnp.float32),
        ],
        in_specs=[SMEM] * 2 + [VMEM] * (4 + len(arrived) + len(before)),
        out_specs=[VMEM] * 2,
        scratch_shapes=[
            pltpu.VMEM((n, tile_rows, LANES), beside.dtype),
            pltpu.VMEM(begun.shape, begun.dtype),
        ],
        compiler_params=params(12),
        cost_estimate=COST,
        name="step2",
    )(items, sizes, blocks, beside, *arrived, begun, wide, *before)


def finish_kernel(chunks, parts, *refs):
    expos, stats = refs[:chunks], refs[chunks : chunks + parts]
    pseudo_ref, certainty_ref, scale_ref = refs[chunks + parts :]
    own, tile_rows = expos[0].shape[:2]
    width = pseudo_ref.shape[1]
    every = [(s, c) for s in stats for c in range(chunks)]
    top = functools.reduce(jnp.maximum, [s[c, 0] for s, c in every])
    totals, moments, scales = 0.0, 0.0, []
    for s, c in every:
        delta = s[c, 0] - top
        scale = jnp.exp(delta)
        scales.append(scale)
        totals += scale * s[c, 1]
        moments += scale * (s[c, 2] + delta * s[c, 1])
    certainty_ref[...] = 1.0 - (jnp.log(totals) - moments / totals) / jnp.log(jnp.float32(CLS))
    inverse = 1.0 / totals
    for c in range(chunks):
        scale_ref[c] = scales[c] * inverse
    for t in range(own):
        span = slice(t * tile_rows, (t + 1) * tile_rows)
        for c in range(chunks):
            start = c * LANES
            live = min(LANES, width - start)
            value = expos[c][t] * column(scale_ref.at[c], t, tile_rows)
            pseudo_ref[span, start : start + live] = value[:, :live].astype(pseudo_ref.dtype)


def finish(expos, stats, width):
    own, tile_rows = expos[0].shape[:2]
    rows = own * tile_rows
    chunks, parts = len(expos), len(stats)
    return pl.pallas_call(
        functools.partial(finish_kernel, chunks, parts),
        out_shape=[sds((rows, width), jnp.bfloat16), sds((rows // LANES, LANES), jnp.float32)],
        in_specs=[VMEM] * (chunks + parts),
        out_specs=[VMEM] * 2,
        scratch_shapes=[pltpu.VMEM((chunks, rows // LANES, LANES), jnp.float32)],
        compiler_params=params(12),
        name="finish",
    )(*expos, *stats)


def local(prior, blocks, links, counts, fetch, seeds, inv_temp):
    width = prior.shape[1]
    tile_rows = blocks.shape[2]
    n = lax.axis_size("rows")
    parts = lax.axis_size("cls")
    chunks = pl.cdiv(width, LANES)
    me = jnp.stack([lax.axis_index("rows"), lax.axis_index("cls") * width]).astype(jnp.int32)
    fetch = fetch.reshape(n)
    wanted = lax.all_to_all(ask(fetch), "rows", split_axis=0, concat_axis=0, tiled=True)
    tabs = stay(split(prior, tile_rows))
    neighbours = stay(split(swap(prior, n), tile_rows))
    blocks = blocks.reshape((-1,) + blocks.shape[2:])
    seeds = seeds.reshape(-1, LANES)
    temp = inv_temp.reshape(-1, LANES)

    sent = pick(me, wanted, tabs, neighbours)
    arrived = [send(sent[0], n)]
    (items, sizes), blocks, wide, targets = load(
        me, links, counts, fetch, after(blocks, sent), seeds, temp, chunks
    )
    parcels = []
    for c in range(1, chunks):
        parcels = [after(part, sizes) for part in sent[c]]
        arrived.append(send(parcels, n))
    begun = own_part(items, sizes, after(blocks, parcels), targets, tabs)
    firsts, there = [], []
    for c in range(chunks):
        out, straight, across = step1(
            me, items, sizes, wanted, blocks, neighbours[c], arrived[c], after(begun[c], parcels)
        )
        got = across_core(across, n)
        parcels = messages(straight, got)
        firsts.append(out)
        there.append((got[0], send(parcels, n)))
    begun = own_part(items, sizes, after(blocks, parcels), targets, firsts)
    expos, stats = [], None
    for c in range(chunks):
        near = c < chunks - 1
        total = begun[c]
        if not near:
            total = near_part(items, sizes, blocks, *there[c], total, n)
        live = min(LANES, width - c * LANES)
        expo, stats = step2(
            live, near, items, sizes, blocks, *there[c], total, wide, stats
        )
        expos.append(expo)
    stats = [stats] + [
        lax.ppermute(stats, "cls", [(i, (i + k) % parts) for i in range(parts)])
        for k in range(1, parts)
    ]
    pseudo, certainty = finish(expos, stats, width)
    return pseudo, certainty.reshape(-1)


def solution(mesh):
    return jax.shard_map(
        local,
        mesh=mesh,
        in_specs=(
            P("rows", "cls"),
            P("rows", None, None, None),
            P("rows", None),
            P("rows"),
            P("rows", None, None),
            P("rows"),
            P("rows"),
        ),
        out_specs=(P("rows", "cls"), P("rows")),
        check_vma=False,
    )
```

time: 90.9 us -> 80.5 us (0.89)
  starting transfers between devices: 34.4 us -> 29.5 us
  local copies, waits for them, and re-layouts: 3.46 us -> 1.4 us
  waiting for transfers between devices: 13.9 us -> 12 us
    ppermute x22 -> x8, waiting for transfers between devices: 9.93 us -> 4.3 us  [the longest x3 2.65 us: local(): lax.ppermute(stats, 'cls', [(i, (i + k) % parts) for i in range(parts)])]
    ppermute x22 -> x8, starting transfers between devices: 10.9 us -> 6.13 us  [the longest x3 4.47 us: local(): lax.ppermute(stats, 'cls', [(i, (i + k) % parts) for i in range(parts)])]
    pallas_call x1 -> x2, Pallas kernels: 5.63 us -> 9.14 us  [own_part(): pl.pallas_call(functools.partial(own_kernel, chunks, items.shape[0] // 3)...]
    ppermute x12, waiting for transfers between devices: 0.84 us -> 4.17 us  [send(): lax.ppermute(parts[k], 'rows', [(i, i ^ 2 * k + 2) for i in range(n)])]
    pallas_call x2 -> x1, Pallas kernels: 4.25 us -> 2.09 us  [near_part(): pl.pallas_call(functools.partial(near_kernel, len(arrived), items.shape[0...]
    unnamed x20 -> x28, local copies, waits for them, and re-layouts: 3.32 us -> 1.29 us
    pallas_call x2, Pallas kernels: 7.48 us -> 6.04 us  [step1(): pl.pallas_call(functools.partial(step1_kernel, len(arrived), items.shape[...]
    pallas_call x4 -> x5, Pallas kernels: 18.2 us -> 17.2 us  [the longest x2 8.02 us: step2(): pl.pallas_call(functools.partial(step2_kernel, len(arrived), live, near,...]
  transfers between devices with their start and end apart: 35 -> 21, of which waited for: 10 -> 8; matrix products, arithmetic and copies ran while one was open for 1% -> 0% of each run, Pallas kernels for 39% -> 35%
where the time goes in v3:
time: 80.5 us; the launch traced here: 80.6 us
  Pallas kernels  36.6 us (45%)
  starting transfers between devices  29.5 us (37%)
  waiting for transfers between devices  12 us (15%)
  local copies, waits for them, and re-layouts  1.4 us (2%)
  between operations  1.01 us (1%)
    ppermute x12, starting transfers between devices, send(): lax.ppermute(parts[k], 'rows', [(i, i ^ 2 * k + 2) for i in range(n)])  17.3 us
    pallas_call x2, Pallas kernels, own_part(): pl.pallas_call(functools.partial(own_kernel, chunks, items.shape[0] // 3)...  9.14 us
    pallas_call x2, Pallas kernels, step2(): pl.pallas_call(functools.partial(step2_kernel, len(arrived), live, near,...  8.02 us
    pallas_call x1, Pallas kernels, load(): pl.pallas_call(functools.partial(load_kernel, room), out_shape=[sds((3 *...  7.24 us
    pallas_call x2, Pallas kernels, step1(): pl.pallas_call(functools.partial(step1_kernel, len(arrived), items.shape[...  6.04 us
    all_to_all x1, starting transfers between devices, local(): lax.all_to_all(ask(fetch), 'rows', split_axis=0, concat_axis=0, tiled=True)  6 us
    ppermute x3, starting transfers between devices, local(): lax.ppermute(stats, 'cls', [(i, (i + k) % parts) for i in range(parts)])  4.47 us
    ppermute x12, waiting for transfers between devices, send(): lax.ppermute(parts[k], 'rows', [(i, i ^ 2 * k + 2) for i in range(n)])  4.17 us
  transfers between devices with their start and end apart: 21, of which 8 were waited for; matrix products, arithmetic and copies ran while one was open for 0% of the time, Pallas kernels for 35%

profile of v3, /device:TPU:0, one launch (start us, length us, event | category | flops | bytes accessed | tf_op | source)
XLA Modules:
  0.0 80.6 jit_solution(7610941551501515176)
XLA Ops:
  1.1 1.3 %ask.1 = s32[8,1,2]{2,1,0:T(1,128)} custom-call(s32[8]{0:T(128)} %bitcast.17), custom_call_target="tpu_custom_call" | custom-call | tf_op jit(solution)/shard_map/ask/pallas_call | solution.py:124
  2.4 6.0 %all-to-all-start = ((s32[8,1,2]{2,1,0:T(1,128)}), s32[8,1,2]{2,1,0:T(1,128)S(1)}, u32[]{:S(2)}, u32[]{:S(2)}) async-start(s32[8,1,2]{2,1,0:T(1,128)} %ask.1), calls=%async_computation | async-start | bytes 8192 | tf_op jit(solution)/shard_map/all_to_all | solution.py:491
  8.4 1.2 %copy-done.8 = bf16[2048,250]{1,0:T(8,128)(2,1)S(1)} copy-done((bf16[2048,250]{1,0:T(8,128)(2,1)S(1)}, bf16[2048,250]{1,0:T(8,128)(2,1)}, u32[]{:S(2)}) %copy-start.8) | copy-done | bytes 1024024
  10.3 3.6 %all-to-all-done.wanted_ref = s32[8,1,2]{2,1,0:T(1,128)S(1)} async-done(((s32[8,1,2]{2,1,0:T(1,128)}), s32[8,1,2]{2,1,0:T(1,128)S(1)}, u32[]{:S(2)}, u32[]{:S(2)}) %all-to-all-start) | async-done | bytes 96 | tf_op jit(solution)/shard_map/all_to_all | solution.py:491
  15.8 3.3 %collective-permute-start.3 = (bf16[2,256,128]{2,1,0:T(8,128)(2,1)S(1)}, bf16[2,256,128]{2,1,0:T(8,128)(2,1)S(1)}, u32[]{:S(2)}, u32[]{:S(2)}) collective-permute-start(bf16[2,256,128]{2,1,0:T(8,128)(2,1)S(1)} %get-tuple-element.48), channel_id=1, source_target_pairs={{0,6},{1,7},{2,4},{3,5},{4,2},{5,3},{6,0},{7,1},{8,14},{9,15},{10,... | collective-permute-start | bytes 393224 | tf_op jit(solution)/shard_map/ppermute | solution.py:184
  19.1 7.2 %load.1 = (s32[624]{0:T(1024)S(1)}, s32[4]{0:T(128)S(1)}, bf16[192,256,256]{2,1,0:T(8,128)(2,1)S(1)}, f32[8,256,128]{2,1,0:T(8,128)S(1)}, f32[8,256,128]{2,1,0:T(8,128)S(1)}, /*index=5*/f32[8,256,128]{2,1,0:T(8,128)S(1)}) custom-call(s32[2]{0:T(128)S(1)} %pad_add_fusion.me_ref, s32[8,24]{1,0:T(8,128)S(1)} %copy-done.11, s32[8]{0:T(128)S(1)} %copy-done.13, ...), custom_call_target="tpu_custom_call" | custom-call | flops 1 | bytes 1 | tf_op jit(solution)/shard_map/load/pallas_call | solution.py:276
  26.6 4.6 %own_part.2 = (f32[9,256,128]{2,1,0:T(8,128)S(1)}, f32[9,256,128]{2,1,0:T(8,128)S(1)}) custom-call(s32[624]{0:T(1024)S(1)} %get-tuple-element.53.items_ref, s32[4]{0:T(128)S(1)} %get-tuple-element.54.sizes_ref, bf16[192,256,256]{2,1,0:T(8,128)(2,1)S(1)} %get-tuple-element.70.blocks, f32[8,256,128]{2,1,0:T(8,128)S(1)} %get-tuple-element.60.refs_0_, ...), custom_call_target="tpu_custom_call" | custom-call | flops 1 | bytes 1 | tf_op jit(solution)/shard_map/own_part/pallas_call | solution.py:303
  31.2 3.4 %collective-permute-start.9 = (bf16[2,256,128]{2,1,0:T(8,128)(2,1)S(1)}, bf16[2,256,128]{2,1,0:T(8,128)(2,1)S(1)}, u32[]{:S(2)}, u32[]{:S(2)}) collective-permute-start(bf16[2,256,128]{2,1,0:T(8,128)(2,1)S(1)} %get-tuple-element.56), channel_id=1, source_target_pairs={{0,2},{1,3},{2,0},{3,1},{4,6},{5,7},{6,4},{7,5},{8,10},{9,11},{10,... | collective-permute-start | bytes 393224 | tf_op jit(solution)/shard_map/ppermute | solution.py:184
  34.5 3.0 %step1.2 = (bf16[8,256,128]{2,1,0:T(8,128)(2,1)S(1)}, bf16[4,256,128]{2,1,0:T(8,128)(2,1)S(1)}, bf16[4,256,128]{2,1,0:T(8,128)(2,1)S(1)}) custom-call(s32[2]{0:T(128)S(1)} %pad_add_fusion.me_ref, s32[624]{0:T(1024)S(1)} %get-tuple-element.53.items_ref, s32[4]{0:T(128)S(1)} %get-tuple-element.54.sizes_ref, s32[8,1,2]{2,1,0:T(1,128)S(1)} %all-to-all-done.wanted_ref, ...), custom_call_target="tpu_custom_call" | custom-call | flops 1 | bytes 1 | tf_op jit(solution)/shard_map/step1/pallas_call | solution.py:347
  39.1 3.3 %collective-permute-start.8 = (bf16[2,256,128]{2,1,0:T(8,128)(2,1)S(1)}, bf16[2,256,128]{2,1,0:T(8,128)(2,1)S(1)}, u32[]{:S(2)}, u32[]{:S(2)}) collective-permute-start(bf16[2,256,128]{2,1,0:T(8,128)(2,1)S(1)} %pad_maximum_fusion.2), channel_id=1, source_target_pairs={{0,6},{1,7},{2,4},{3,5},{4,2},{5,3},{6,0},{7,1},{8,14},{9,15},{10,... | collective-permute-start | bytes 393224 | tf_op jit(solution)/shard_map/ppermute | solution.py:184
  43.7 3.0 %step1.3 = (bf16[8,256,128]{2,1,0:T(8,128)(2,1)S(1)}, bf16[4,256,128]{2,1,0:T(8,128)(2,1)S(1)}, bf16[4,256,128]{2,1,0:T(8,128)(2,1)S(1)}) custom-call(s32[2]{0:T(128)S(1)} %pad_add_fusion.me_ref, s32[624]{0:T(1024)S(1)} %get-tuple-element.53.items_ref, s32[4]{0:T(128)S(1)} %get-tuple-element.54.sizes_ref, s32[8,1,2]{2,1,0:T(1,128)S(1)} %all-to-all-done.wanted_ref, ...), custom_call_target="tpu_custom_call" | custom-call | flops 1 | bytes 1 | tf_op jit(solution)/shard_map/step1/pallas_call | solution.py:347
  47.4 0.8 %collective-permute-done.13 = bf16[2,256,128]{2,1,0:T(8,128)(2,1)S(1)} collective-permute-done((bf16[2,256,128]{2,1,0:T(8,128)(2,1)S(1)}, bf16[2,256,128]{2,1,0:T(8,128)(2,1)S(1)}, u32[]{:S(2)}, u32[]{:S(2)}) %collective-permute-start.13) | collective-permute-done | bytes 131104 | tf_op jit(solution)/shard_map/ppermute | solution.py:168
  48.2 3.9 %collective-permute-start.16 = (bf16[2,256,128]{2,1,0:T(8,128)(2,1)S(1)}, bf16[2,256,128]{2,1,0:T(8,128)(2,1)S(1)}, u32[]{:S(2)}, u32[]{:S(2)}) collective-permute-start(bf16[2,256,128]{2,1,0:T(8,128)(2,1)S(1)} %pad_maximum_fusion.5), channel_id=1, source_target_pairs={{0,6},{1,7},{2,4},{3,5},{4,2},{5,3},{6,0},{7,1},{8,14},{9,15},{10,... | collective-permute-start | bytes 393224 | tf_op jit(solution)/shard_map/ppermute | solution.py:184
  53.1 4.6 %own_part.3 = (f32[9,256,128]{2,1,0:T(8,128)S(1)}, f32[9,256,128]{2,1,0:T(8,128)S(1)}) custom-call(s32[624]{0:T(1024)S(1)} %get-tuple-element.53.items_ref, s32[4]{0:T(128)S(1)} %get-tuple-element.54.sizes_ref, bf16[192,256,256]{2,1,0:T(8,128)(2,1)S(1)} %get-tuple-element.70.blocks, f32[8,256,128]{2,1,0:T(8,128)S(1)} %get-tuple-element.60.refs_0_, ...), custom_call_target="tpu_custom_call" | custom-call | flops 1 | bytes 1 | tf_op jit(solution)/shard_map/own_part/pallas_call | solution.py:303
  57.6 3.0 %collective-permute-done.7.refs_1_ = bf16[2,256,128]{2,1,0:T(8,128)(2,1)S(1)} collective-permute-done((bf16[2,256,128]{2,1,0:T(8,128)(2,1)S(1)}, bf16[2,256,128]{2,1,0:T(8,128)(2,1)S(1)}, u32[]{:S(2)}, u32[]{:S(2)}) %collective-permute-start.7) | collective-permute-done | bytes 131104 | tf_op jit(solution)/shard_map/ppermute | solution.py:184
  60.6 4.3 %step2.2 = (f32[8,256,128]{2,1,0:T(8,128)S(1)}, f32[1,3,16,128]{3,2,1,0:T(8,128)S(1)}) custom-call(s32[624]{0:T(1024)S(1)} %get-tuple-element.53.items_ref, s32[4]{0:T(128)S(1)} %get-tuple-element.54.sizes_ref, bf16[192,256,256]{2,1,0:T(8,128)(2,1)S(1)} %get-tuple-element.70.blocks, bf16[256,128]{1,0:T(8,128)(2,1)S(1)} %get-tuple-element.99.beside, ...), custom_call_target="tpu_custom_call" | custom-call | flops 1 | bytes 1 | tf_op jit(solution)/shard_map/step2/pallas_call | solution.py:423
  65.0 1.2 %collective-permute-done.15.refs_1_ = bf16[2,256,128]{2,1,0:T(8,128)(2,1)S(1)} collective-permute-done((bf16[2,256,128]{2,1,0:T(8,128)(2,1)S(1)}, bf16[2,256,128]{2,1,0:T(8,128)(2,1)S(1)}, u32[]{:S(2)}, u32[]{:S(2)}) %collective-permute-start.15) | collective-permute-done | bytes 131104 | tf_op jit(solution)/shard_map/ppermute | solution.py:184
  66.1 2.1 %near_part.1.refs_3_ = f32[9,256,128]{2,1,0:T(8,128)S(1)} custom-call(s32[624]{0:T(1024)S(1)} %get-tuple-element.53.items_ref, s32[4]{0:T(128)S(1)} %get-tuple-element.54.sizes_ref, bf16[192,256,256]{2,1,0:T(8,128)(2,1)S(1)} %get-tuple-element.70.blocks, bf16[256,128]{1,0:T(8,128)(2,1)S(1)} %get-tuple-element.92.beside, ...), custom_call_target="tpu_custom_call" | custom-call | flops 1 | bytes 1 | tf_op jit(solution)/shard_map/near_part/pallas_call | solution.py:372
  68.2 3.7 %step2.3 = (f32[8,256,128]{2,1,0:T(8,128)S(1)}, f32[2,3,16,128]{3,2,1,0:T(8,128)S(1)}) custom-call(s32[624]{0:T(1024)S(1)} %get-tuple-element.53.items_ref, s32[4]{0:T(128)S(1)} %get-tuple-element.54.sizes_ref, bf16[192,256,256]{2,1,0:T(8,128)(2,1)S(1)} %get-tuple-element.70.blocks, bf16[256,128]{1,0:T(8,128)(2,1)S(1)} %get-tuple-element.92.beside, ...), custom_call_target="tpu_custom_call" | custom-call | flops 1 | bytes 1 | tf_op jit(solution)/shard_map/step2/pallas_call | solution.py:423
  71.9 1.5 %collective-permute-start.17 = (f32[2,3,16,128]{3,2,1,0:T(8,128)S(1)}, f32[2,3,16,128]{3,2,1,0:T(8,128)S(1)}, u32[]{:S(2)}, u32[]{:S(2)}) collective-permute-start(f32[2,3,16,128]{3,2,1,0:T(8,128)S(1)} %get-tuple-element.79.refs_2_), channel_id=1, source_target_pairs={{0,8},{8,16},{16,24},{24,0},{1,9},{9,17},{17,25},{25,1},{2,10},{10... | collective-permute-start | bytes 147464 | tf_op jit(solution)/shard_map/ppermute | solution.py:530
  73.4 1.5 %collective-permute-start.18 = (f32[2,3,16,128]{3,2,1,0:T(8,128)S(1)}, f32[2,3,16,128]{3,2,1,0:T(8,128)S(1)}, u32[]{:S(2)}, u32[]{:S(2)}) collective-permute-start(f32[2,3,16,128]{3,2,1,0:T(8,128)S(1)} %get-tuple-element.79.refs_2_), channel_id=1, source_target_pairs={{0,16},{8,24},{16,0},{24,8},{1,17},{9,25},{17,1},{25,9},{2,18},{10... | collective-permute-start | bytes 147464 | tf_op jit(solution)/shard_map/ppermute | solution.py:530
  74.9 1.4 %collective-permute-start.19 = (f32[2,3,16,128]{3,2,1,0:T(8,128)S(1)}, f32[2,3,16,128]{3,2,1,0:T(8,128)S(1)}, u32[]{:S(2)}, u32[]{:S(2)}) collective-permute-start(f32[2,3,16,128]{3,2,1,0:T(8,128)S(1)} %get-tuple-element.79.refs_2_), channel_id=1, source_target_pairs={{0,24},{8,0},{16,8},{24,16},{1,25},{9,1},{17,9},{25,17},{2,26},{10... | collective-permute-start | bytes 147464 | tf_op jit(solution)/shard_map/ppermute | solution.py:530
  77.5 1.5 %collective-permute-done.19.refs_5_ = f32[2,3,16,128]{3,2,1,0:T(8,128)S(1)} collective-permute-done((f32[2,3,16,128]{3,2,1,0:T(8,128)S(1)}, f32[2,3,16,128]{3,2,1,0:T(8,128)S(1)}, u32[]{:S(2)}, u32[]{:S(2)}) %collective-permute-start.19) | collective-permute-done | bytes 49184 | tf_op jit(solution)/shard_map/ppermute | solution.py:530
  79.0 1.6 %finish.1 = (bf16[2048,250]{1,0:T(8,128)(2,1)}, f32[16,128]{1,0:T(8,128)}) custom-call(f32[8,256,128]{2,1,0:T(8,128)S(1)} %get-tuple-element.75.refs_0_, f32[8,256,128]{2,1,0:T(8,128)S(1)} %get-tuple-element.78.refs_1_, f32[2,3,16,128]{3,2,1,0:T(8,128)S(1)} %get-tuple-element.79.refs_2_, f32[2,3,16,128]{3,2,1,0:T(8,128)S(1)} %collective-permute-done.17.refs_3_, ...), custom_call_target="tpu_custom_call" | custom-call | tf_op jit(solution)/shard_map/finish/pallas_call | solution.py:472
  (74 shorter events, 8.6 us)
Async XLA Ops:
  0.6 9.4 %collective-permute-start = (bf16[2048,250]{1,0:T(8,128)(2,1)}, bf16[2048,250]{1,0:T(8,128)(2,1)S(1)}, u32[]{:S(2)}, u32[]{:S(2)}) collective-permute-start(bf16[2048,250]{1,0:T(8,128)(2,1)} %param.7), channel_id=1, source_target_pairs={{0,1},{1,0},{2,3},{3,2},{4,5},{5,4},{6,7},{7,6},{8,9},{9,8},{10,11... | collective-permute-start | bytes 3072008 | tf_op jit(solution)/shard_map/ppermute | solution.py:168
  2.4 11.5 %all-to-all-start = ((s32[8,1,2]{2,1,0:T(1,128)}), s32[8,1,2]{2,1,0:T(1,128)S(1)}, u32[]{:S(2)}, u32[]{:S(2)}) async-start(s32[8,1,2]{2,1,0:T(1,128)} %ask.1), calls=%async_computation | async-start | bytes 8192 | tf_op jit(solution)/shard_map/all_to_all | solution.py:491
  10.3 8.8 %copy-start = (bf16[8,256,128]{2,1,0:T(8,128)(2,1)}, bf16[8,256,128]{2,1,0:T(8,128)(2,1)S(1)}, u32[]{:S(2)}) copy-start(bf16[8,256,128]{2,1,0:T(8,128)(2,1)S(1)} %get-tuple-element.45.refs_3_.neighbour) | copy-start | bytes 1572868
  10.3 8.8 %copy-start.2 = (bf16[8,256,128]{2,1,0:T(8,128)(2,1)}, bf16[8,256,128]{2,1,0:T(8,128)(2,1)S(1)}, u32[]{:S(2)}) copy-start(bf16[8,256,128]{2,1,0:T(8,128)(2,1)S(1)} %get-tuple-element.44.refs_2_.neighbour) | copy-start | bytes 1572868
  10.3 8.8 %copy-start.9 = (s32[2048]{0:T(1024)S(1)}, s32[2048]{0:T(1024)}, u32[]{:S(2)}) copy-start(s32[2048]{0:T(1024)} %param.12) | copy-start | bytes 24580
  14.6 16.6 %collective-permute-start.1 = (bf16[2,256,128]{2,1,0:T(8,128)(2,1)S(1)}, bf16[2,256,128]{2,1,0:T(8,128)(2,1)S(1)}, u32[]{:S(2)}, u32[]{:S(2)}) collective-permute-start(bf16[2,256,128]{2,1,0:T(8,128)(2,1)S(1)} %get-tuple-element.46), channel_id=1, source_target_pairs={{0,2},{1,3},{2,0},{3,1},{4,6},{5,7},{6,4},{7,5},{8,10},{9,11},{10,... | collective-permute-start | bytes 393224 | tf_op jit(solution)/shard_map/ppermute | solution.py:184
  15.2 19.3 %collective-permute-start.2 = (bf16[2,256,128]{2,1,0:T(8,128)(2,1)S(1)}, bf16[2,256,128]{2,1,0:T(8,128)(2,1)S(1)}, u32[]{:S(2)}, u32[]{:S(2)}) collective-permute-start(bf16[2,256,128]{2,1,0:T(8,128)(2,1)S(1)} %get-tuple-element.47), channel_id=1, source_target_pairs={{0,4},{1,5},{2,6},{3,7},{4,0},{5,1},{6,2},{7,3},{8,12},{9,13},{10,... | collective-permute-start | bytes 393224 | tf_op jit(solution)/shard_map/ppermute | solution.py:184
  15.8 18.7 %collective-permute-start.3 = (bf16[2,256,128]{2,1,0:T(8,128)(2,1)S(1)}, bf16[2,256,128]{2,1,0:T(8,128)(2,1)S(1)}, u32[]{:S(2)}, u32[]{:S(2)}) collective-permute-start(bf16[2,256,128]{2,1,0:T(8,128)(2,1)S(1)} %get-tuple-element.48), channel_id=1, source_target_pairs={{0,6},{1,7},{2,4},{3,5},{4,2},{5,3},{6,0},{7,1},{8,14},{9,15},{10,... | collective-permute-start | bytes 393224 | tf_op jit(solution)/shard_map/ppermute | solution.py:184
  26.4 16.7 %collective-permute-start.11 = (bf16[2,256,128]{2,1,0:T(8,128)(2,1)S(1)}, bf16[2,256,128]{2,1,0:T(8,128)(2,1)S(1)}, u32[]{:S(2)}, u32[]{:S(2)}) collective-permute-start(bf16[2,256,128]{2,1,0:T(8,128)(2,1)S(1)} %get-tuple-element.58), channel_id=1, source_target_pairs={{0,6},{1,7},{2,4},{3,5},{4,2},{5,3},{6,0},{7,1},{8,14},{9,15},{10,... | collective-permute-start | bytes 393224 | tf_op jit(solution)/shard_map/ppermute | solution.py:184
  26.5 17.2 %collective-permute-start.10 = (bf16[2,256,128]{2,1,0:T(8,128)(2,1)S(1)}, bf16[2,256,128]{2,1,0:T(8,128)(2,1)S(1)}, u32[]{:S(2)}, u32[]{:S(2)}) collective-permute-start(bf16[2,256,128]{2,1,0:T(8,128)(2,1)S(1)} %get-tuple-element.57), channel_id=1, source_target_pairs={{0,4},{1,5},{2,6},{3,7},{4,0},{5,1},{6,2},{7,3},{8,12},{9,13},{10,... | collective-permute-start | bytes 393224 | tf_op jit(solution)/shard_map/ppermute | solution.py:184
  31.2 12.6 %collective-permute-start.9 = (bf16[2,256,128]{2,1,0:T(8,128)(2,1)S(1)}, bf16[2,256,128]{2,1,0:T(8,128)(2,1)S(1)}, u32[]{:S(2)}, u32[]{:S(2)}) collective-permute-start(bf16[2,256,128]{2,1,0:T(8,128)(2,1)S(1)} %get-tuple-element.56), channel_id=1, source_target_pairs={{0,2},{1,3},{2,0},{3,1},{4,6},{5,7},{6,4},{7,5},{8,10},{9,11},{10,... | collective-permute-start | bytes 393224 | tf_op jit(solution)/shard_map/ppermute | solution.py:184
  37.6 1.4 %collective-permute-start.6 = (bf16[2,256,128]{2,1,0:T(8,128)(2,1)S(1)}, bf16[2,256,128]{2,1,0:T(8,128)(2,1)S(1)}, u32[]{:S(2)}, u32[]{:S(2)}) collective-permute-start(bf16[2,256,128]{2,1,0:T(8,128)(2,1)S(1)} %get-tuple-element.90), channel_id=1, source_target_pairs={{0,1},{1,0},{2,3},{3,2},{4,5},{5,4},{6,7},{7,6},{8,9},{9,8},{10,11... | collective-permute-start | bytes 393224 | tf_op jit(solution)/shard_map/ppermute | solution.py:168
  37.7 4.7 %collective-permute-start.4 = (bf16[2,256,128]{2,1,0:T(8,128)(2,1)S(1)}, bf16[2,256,128]{2,1,0:T(8,128)(2,1)S(1)}, u32[]{:S(2)}, u32[]{:S(2)}) collective-permute-start(bf16[2,256,128]{2,1,0:T(8,128)(2,1)S(1)} %get-tuple-element.91), channel_id=1, source_target_pairs={{0,1},{1,0},{2,3},{3,2},{4,5},{5,4},{6,7},{7,6},{8,9},{9,8},{10,11... | collective-permute-start | bytes 393224 | tf_op jit(solution)/shard_map/ppermute | solution.py:168
  39.1 13.2 %collective-permute-start.8 = (bf16[2,256,128]{2,1,0:T(8,128)(2,1)S(1)}, bf16[2,256,128]{2,1,0:T(8,128)(2,1)S(1)}, u32[]{:S(2)}, u32[]{:S(2)}) collective-permute-start(bf16[2,256,128]{2,1,0:T(8,128)(2,1)S(1)} %pad_maximum_fusion.2), channel_id=1, source_target_pairs={{0,6},{1,7},{2,4},{3,5},{4,2},{5,3},{6,0},{7,1},{8,14},{9,15},{10,... | collective-permute-start | bytes 393224 | tf_op jit(solution)/shard_map/ppermute | solution.py:184
  42.4 18.2 %collective-permute-start.7 = (bf16[2,256,128]{2,1,0:T(8,128)(2,1)S(1)}, bf16[2,256,128]{2,1,0:T(8,128)(2,1)S(1)}, u32[]{:S(2)}, u32[]{:S(2)}) collective-permute-start(bf16[2,256,128]{2,1,0:T(8,128)(2,1)S(1)} %pad_maximum_fusion.1), channel_id=1, source_target_pairs={{0,4},{1,5},{2,6},{3,7},{4,0},{5,1},{6,2},{7,3},{8,12},{9,13},{10,... | collective-permute-start | bytes 393224 | tf_op jit(solution)/shard_map/ppermute | solution.py:184
  43.1 17.5 %collective-permute-start.5 = (bf16[2,256,128]{2,1,0:T(8,128)(2,1)S(1)}, bf16[2,256,128]{2,1,0:T(8,128)(2,1)S(1)}, u32[]{:S(2)}, u32[]{:S(2)}) collective-permute-start(bf16[2,256,128]{2,1,0:T(8,128)(2,1)S(1)} %pad_maximum_fusion), channel_id=1, source_target_pairs={{0,2},{1,3},{2,0},{3,1},{4,6},{5,7},{6,4},{7,5},{8,10},{9,11},{10,... | collective-permute-start | bytes 393224 | tf_op jit(solution)/shard_map/ppermute | solution.py:184
  46.8 1.4 %collective-permute-start.13 = (bf16[2,256,128]{2,1,0:T(8,128)(2,1)S(1)}, bf16[2,256,128]{2,1,0:T(8,128)(2,1)S(1)}, u32[]{:S(2)}, u32[]{:S(2)}) collective-permute-start(bf16[2,256,128]{2,1,0:T(8,128)(2,1)S(1)} %get-tuple-element.85), channel_id=1, source_target_pairs={{0,1},{1,0},{2,3},{3,2},{4,5},{5,4},{6,7},{7,6},{8,9},{9,8},{10,11... | collective-permute-start | bytes 393224 | tf_op jit(solution)/shard_map/ppermute | solution.py:168
  46.9 5.3 %collective-permute-start.12 = (bf16[2,256,128]{2,1,0:T(8,128)(2,1)S(1)}, bf16[2,256,128]{2,1,0:T(8,128)(2,1)S(1)}, u32[]{:S(2)}, u32[]{:S(2)}) collective-permute-start(bf16[2,256,128]{2,1,0:T(8,128)(2,1)S(1)} %get-tuple-element.86), channel_id=1, source_target_pairs={{0,1},{1,0},{2,3},{3,2},{4,5},{5,4},{6,7},{7,6},{8,9},{9,8},{10,11... | collective-permute-start | bytes 393224 | tf_op jit(solution)/shard_map/ppermute | solution.py:168
  48.2 16.7 %collective-permute-start.16 = (bf16[2,256,128]{2,1,0:T(8,128)(2,1)S(1)}, bf16[2,256,128]{2,1,0:T(8,128)(2,1)S(1)}, u32[]{:S(2)}, u32[]{:S(2)}) collective-permute-start(bf16[2,256,128]{2,1,0:T(8,128)(2,1)S(1)} %pad_maximum_fusion.5), channel_id=1, source_target_pairs={{0,6},{1,7},{2,4},{3,5},{4,2},{5,3},{6,0},{7,1},{8,14},{9,15},{10,... | collective-permute-start | bytes 393224 | tf_op jit(solution)/shard_map/ppermute | solution.py:184
  52.2 14.0 %collective-permute-start.15 = (bf16[2,256,128]{2,1,0:T(8,128)(2,1)S(1)}, bf16[2,256,128]{2,1,0:T(8,128)(2,1)S(1)}, u32[]{:S(2)}, u32[]{:S(2)}) collective-permute-start(bf16[2,256,128]{2,1,0:T(8,128)(2,1)S(1)} %pad_maximum_fusion.4), channel_id=1, source_target_pairs={{0,4},{1,5},{2,6},{3,7},{4,0},{5,1},{6,2},{7,3},{8,12},{9,13},{10,... | collective-permute-start | bytes 393224 | tf_op jit(solution)/shard_map/ppermute | solution.py:184
  52.3 13.8 %collective-permute-start.14 = (bf16[2,256,128]{2,1,0:T(8,128)(2,1)S(1)}, bf16[2,256,128]{2,1,0:T(8,128)(2,1)S(1)}, u32[]{:S(2)}, u32[]{:S(2)}) collective-permute-start(bf16[2,256,128]{2,1,0:T(8,128)(2,1)S(1)} %pad_maximum_fusion.3), channel_id=1, source_target_pairs={{0,2},{1,3},{2,0},{3,1},{4,6},{5,7},{6,4},{7,5},{8,10},{9,11},{10,... | collective-permute-start | bytes 393224 | tf_op jit(solution)/shard_map/ppermute | solution.py:184
  71.9 5.1 %collective-permute-start.17 = (f32[2,3,16,128]{3,2,1,0:T(8,128)S(1)}, f32[2,3,16,128]{3,2,1,0:T(8,128)S(1)}, u32[]{:S(2)}, u32[]{:S(2)}) collective-permute-start(f32[2,3,16,128]{3,2,1,0:T(8,128)S(1)} %get-tuple-element.79.refs_2_), channel_id=1, source_target_pairs={{0,8},{8,16},{16,24},{24,0},{1,9},{9,17},{17,25},{25,1},{2,10},{10... | collective-permute-start | bytes 147464 | tf_op jit(solution)/shard_map/ppermute | solution.py:530
  73.4 4.1 %collective-permute-start.18 = (f32[2,3,16,128]{3,2,1,0:T(8,128)S(1)}, f32[2,3,16,128]{3,2,1,0:T(8,128)S(1)}, u32[]{:S(2)}, u32[]{:S(2)}) collective-permute-start(f32[2,3,16,128]{3,2,1,0:T(8,128)S(1)} %get-tuple-element.79.refs_2_), channel_id=1, source_target_pairs={{0,16},{8,24},{16,0},{24,8},{1,17},{9,25},{17,1},{25,9},{2,18},{10... | collective-permute-start | bytes 147464 | tf_op jit(solution)/shard_map/ppermute | solution.py:530
  74.9 4.1 %collective-permute-start.19 = (f32[2,3,16,128]{3,2,1,0:T(8,128)S(1)}, f32[2,3,16,128]{3,2,1,0:T(8,128)S(1)}, u32[]{:S(2)}, u32[]{:S(2)}) collective-permute-start(f32[2,3,16,128]{3,2,1,0:T(8,128)S(1)} %get-tuple-element.79.refs_2_), channel_id=1, source_target_pairs={{0,24},{8,0},{16,8},{24,16},{1,25},{9,1},{17,9},{25,17},{2,26},{10... | collective-permute-start | bytes 147464 | tf_op jit(solution)/shard_map/ppermute | solution.py:530
  (11 other events, 74.7 us)

commit v4 on v3

v4 whole, which is shorter than its diff:
```python
import functools

import jax
import jax.numpy as jnp
from jax import lax
from jax.experimental import pallas as pl
from jax.experimental.pallas import tpu as pltpu
from jax.sharding import PartitionSpec as P

CLS = 1000
LANES = 128
GROUP = 16
blend = 0.8

SMEM = pl.BlockSpec(memory_space=pltpu.SMEM)
VMEM = pl.BlockSpec(memory_space=pltpu.VMEM)
HBM = pl.BlockSpec(memory_space=pltpu.HBM)
T_SHIFT, B_SHIFT = 20, 8


COST = pl.CostEstimate(flops=1, bytes_accessed=1, transcendentals=0)


PARAMS = pltpu.CompilerParams(vmem_limit_bytes=8 << 20)


def held(shape, dtype):
    return pltpu.VMEM(shape, dtype)


def sds(shape, dtype):
    return jax.ShapeDtypeStruct(shape, dtype)


def put_chunk(out, value, chunk):
    start = chunk * LANES
    live = min(LANES, value.shape[-1] - start)
    out[..., :live] = value[..., start : start + live]
    if live < LANES:
        out[..., live:] = jnp.zeros(value.shape[:-1] + (LANES - live,), out.dtype)


def fill_lists(room, index, links_ref, counts_ref, fetch_ref, items_ref, sizes_ref):
    own, slots = links_ref.shape
    n = fetch_ref.shape[0]
    mine = fetch_ref[index]

    def tile(t, sizes):
        def slot(j, sizes):
            v = links_ref[t, j]
            x = (v - own) ^ index
            is_own = jnp.logical_or(v < own, x == 0)
            is_near = jnp.logical_and(jnp.logical_not(is_own), x < n // 2)
            field = jnp.where(is_own, jnp.where(v < own, v, mine), x)
            place = jnp.where(
                is_own, sizes[0], jnp.where(is_near, 2 * room + sizes[1], 2 * room - 1 - sizes[2])
            )
            items_ref[place] = (t << T_SHIFT) + ((t * slots + j) << B_SHIFT) + field
            is_far = jnp.logical_not(jnp.logical_or(is_own, is_near))
            return tuple(
                size + kind.astype(jnp.int32) for size, kind in zip(sizes, (is_own, is_near, is_far))
            )

        return lax.fori_loop(0, counts_ref[t], slot, sizes)

    sizes = lax.fori_loop(0, own, tile, (jnp.int32(0),) * 3)
    for kind in range(3):
        sizes_ref[kind] = sizes[kind]
    sizes_ref[3] = fetch_ref[index ^ 1]

    def fill(i, carry):
        items_ref[sizes[0] + i] = own << T_SHIFT
        items_ref[2 * room + sizes[1] + i] = own << T_SHIFT
        items_ref[2 * room - sizes[2] - 1 - i] = own << T_SHIFT
        return carry

    lax.fori_loop(0, GROUP, fill, 0)


def groups_of(count):
    return (count + GROUP - 1) // GROUP


def own_list(room, sizes_ref):
    return 0, groups_of(sizes_ref[0])


def near_list(room, sizes_ref):
    return 2 * room, groups_of(sizes_ref[1])


def far_list(room, sizes_ref):
    groups = groups_of(sizes_ref[2])
    return 2 * room - groups * GROUP, groups


def both_lists(room, sizes_ref):
    return 2 * room - sizes_ref[2], groups_of(sizes_ref[1] + sizes_ref[2])


def near_bound(n):
    return max(1, n // 4)


def split_kernel(prior_ref, *outs):
    for c, out in enumerate(outs):
        put_chunk(out, prior_ref[...], c)


def split(prior, chunks):
    return pl.pallas_call(
        split_kernel,
        out_shape=[held(prior.shape[:2] + (LANES,), prior.dtype)] * chunks,
        in_specs=[VMEM],
        out_specs=[VMEM] * chunks,
        compiler_params=PARAMS,
        name="split",
    )(prior)


def pick_kernel(chunks, me_ref, fetch_ref, *refs):
    n = fetch_ref.shape[0]
    count = n // 2 - 1
    lists = (fetch_ref,) + refs[:count]
    tabs, neighbours = refs[count : count + chunks], refs[count + chunks : count + 2 * chunks]
    asked_ref, *outs = refs[count + 2 * chunks :]
    besides, outs = outs[:chunks], outs[chunks:]
    index = me_ref[0]
    first = near_bound(n)
    for c in range(chunks):
        besides[c][...] = neighbours[c][fetch_ref[index ^ 1]]
    for k in range(1, n // 2):
        mine, other = lists[k][index], lists[k][index ^ 1]
        for c in range(chunks):
            if k < first:
                out, at = outs[k - 1], 2 * c
            else:
                out, at = outs[first - 1 + c * (n // 2 - first) + k - first], 0
            out[at] = tabs[c][mine]
            out[at + 1] = neighbours[c][other]
    for k, one in enumerate(lists):
        for j in range(n):
            asked_ref[k, j] = one[j]


def pick(me, fetch, lists, tabs, neighbours):
    n = fetch.shape[0]
    chunks = len(tabs)
    first = near_bound(n)
    tile, dtype = tabs[0].shape[1:], tabs[0].dtype
    near, far = first - 1, n // 2 - first
    outs = pl.pallas_call(
        functools.partial(pick_kernel, chunks),
        out_shape=[sds((n // 2, n), fetch.dtype)]
        + [held(tile, dtype)] * chunks
        + [held((2 * chunks,) + tile, dtype)] * near
        + [held((2,) + tile, dtype)] * (chunks * far),
        in_specs=[SMEM] * (2 + len(lists)) + [VMEM] * (2 * chunks),
        out_specs=[SMEM] + [VMEM] * (chunks + near + chunks * far),
        compiler_params=PARAMS,
        name="pick",
    )(me, fetch, *lists, *tabs, *neighbours)
    far_parts = outs[1 + chunks + near :]
    return (
        outs[0],
        outs[1 : 1 + chunks],
        outs[1 + chunks : 1 + chunks + near],
        [far_parts[c * far : (c + 1) * far] for c in range(chunks)],
    )


def after(value, *others):
    return lax.optimization_barrier((value, others))[0]


def swap(value, n):
    return lax.ppermute(value, "rows", [(i, i ^ 1) for i in range(n)])


def send(parts, ks, n):
    return [
        lax.ppermute(part, "rows", [(i, i ^ (2 * k)) for i in range(n)])
        for part, k in zip(parts, ks)
    ]


def run_list(which, items_ref, blocks, rhs, totals, ready=None):
    first, groups = which
    own = totals[0].shape[0] - 1
    low, high = (1 << B_SHIFT) - 1, (1 << (T_SHIFT - B_SHIFT)) - 1

    def step(g, waited):
        at = first + g * GROUP
        if ready is not None:
            last = jnp.minimum(items_ref[at + GROUP - 1] >> T_SHIFT, own - 1) + 1
            lax.fori_loop(waited, last, ready, 0)
            waited = jnp.maximum(waited, last)
        for i in range(GROUP):
            word = items_ref[at + i]
            t = word >> T_SHIFT
            value = jnp.dot(
                blocks[(word >> B_SHIFT) & high],
                rhs(word & low),
                preferred_element_type=jnp.float32,
            )
            for c, total in enumerate(totals):
                total[t] += value[:, c * LANES : (c + 1) * LANES]
        return waited

    waited = lax.fori_loop(0, groups, step, jnp.int32(0))
    if ready is not None:
        lax.fori_loop(waited, own, ready, 0)


def column(ref, t, tile_rows):
    parts = tile_rows // LANES
    rows = [ref[pl.ds(t * parts + i, 1), :] for i in range(parts)]
    return jnp.concatenate(
        [jnp.broadcast_to(row, (LANES, LANES)).T for row in rows], axis=0
    )


def start_totals(me_ref, seeds_ref, totals):
    own, tile_rows = totals[0].shape[0] - 1, totals[0].shape[1]
    share = (1.0 - blend) / blend
    lane = lax.broadcasted_iota(jnp.int32, totals[0].shape[1:], 1)
    for t in range(own):
        seeds = column(seeds_ref, t, tile_rows) - me_ref[1]
        for c, total in enumerate(totals):
            total[t] = jnp.where(seeds == lane + c * LANES, share, 0.0)


def side_by_side(tabs):
    return lambda f: jnp.concatenate([tab[f] for tab in tabs], axis=1)


def prepare_kernel(room, me_ref, links_ref, counts_ref, fetch_ref, items_ref, sizes_ref):
    fill_lists(room, me_ref[0], links_ref, counts_ref, fetch_ref, items_ref, sizes_ref)


def prepare(me, links, counts, fetch):
    room = links.size + GROUP
    return pl.pallas_call(
        functools.partial(prepare_kernel, room),
        out_shape=[sds((3 * room,), jnp.int32), sds((4,), jnp.int32)],
        in_specs=[SMEM] * 4,
        out_specs=[SMEM] * 2,
        compiler_params=PARAMS,
        cost_estimate=COST,
        name="prepare",
    )(me, links, counts, fetch)


def begin_kernel(
    room, me_ref, items_ref, sizes_ref, counts_ref, blocks_hbm, prior, seeds_ref, blocks, *refs
):
    *totals, stage, tab, sems, prior_sem = refs
    own, groups = sems.shape
    slots = blocks.shape[0] // own
    size = slots // groups
    load = pltpu.make_async_copy(prior, stage, prior_sem)
    load.start()

    def copy(t, g):
        span = pl.ds(t * slots + g * size, size)
        return pltpu.make_async_copy(blocks_hbm.at[span], blocks.at[span], sems.at[t, g])

    def used(t):
        return (counts_ref[t] + size - 1) // size

    def begin(t, carry):
        return lax.fori_loop(0, used(t), lambda g, c: (copy(t, g).start(), c)[1], carry)

    def ready(t, carry):
        return lax.fori_loop(0, used(t), lambda g, c: (copy(t, g).wait(), c)[1], carry)

    lax.fori_loop(0, own, begin, 0)
    start_totals(me_ref, seeds_ref, totals)
    load.wait()
    for c in range(len(totals)):
        put_chunk(tab.at[:, :, pl.ds(c * LANES, LANES)], stage[...], c)
    run_list(own_list(room, sizes_ref), items_ref, blocks, lambda f: tab[f], totals, ready)


def begin(me, items, sizes, counts, blocks, prior, seeds, chunks):
    own, tile_rows = prior.shape[:2]
    slots = blocks.shape[0] // own
    size = next(g for g in (4, 3, 2, 1) if slots % g == 0)
    out = pl.pallas_call(
        functools.partial(begin_kernel, items.shape[0] // 3),
        out_shape=[held(blocks.shape, blocks.dtype)]
        + [held((own + 1, tile_rows, LANES), jnp.float32)] * chunks,
        in_specs=[SMEM] * 4 + [HBM] * 2 + [VMEM],
        out_specs=[VMEM] * (1 + chunks),
        scratch_shapes=[
            pltpu.VMEM(prior.shape, prior.dtype),
            pltpu.VMEM((own, tile_rows, chunks * LANES), prior.dtype),
            pltpu.SemaphoreType.DMA((own, slots // size)),
            pltpu.SemaphoreType.DMA,
        ],
        compiler_params=PARAMS,
        cost_estimate=COST,
        name="begin",
    )(me, items, sizes, counts, blocks, prior, seeds)
    return out[0], out[1:]


def own_kernel(chunks, room, me_ref, items_ref, sizes_ref, blocks, seeds_ref, temp_ref, *refs):
    tabs, wide_ref, totals = refs[:chunks], refs[chunks], refs[chunks + 1 :]
    start_totals(me_ref, seeds_ref, totals)
    own, tile_rows = wide_ref.shape[:2]
    for t in range(own):
        wide_ref[t] = blend * column(temp_ref, t, tile_rows)
    run_list(own_list(room, sizes_ref), items_ref, blocks, side_by_side(tabs), totals)


def own_part(me, items, sizes, blocks, seeds, temp, tabs):
    own, tile_rows = tabs[0].shape[:2]
    chunks = len(tabs)
    out = pl.pallas_call(
        functools.partial(own_kernel, chunks, items.shape[0] // 3),
        out_shape=[held((own, tile_rows, LANES), jnp.float32)]
        + [held((own + 1, tile_rows, LANES), jnp.float32)] * chunks,
        in_specs=[SMEM] * 3 + [VMEM] * (3 + chunks),
        out_specs=[VMEM] * (1 + chunks),
        compiler_params=PARAMS,
        cost_estimate=COST,
        name="own_part",
    )(me, items, sizes, blocks, seeds, temp, *tabs)
    return out[0], out[1:]


def put_near(chunk, near, field):
    for k, one in enumerate(near):
        for j in range(2):
            field[2 * (k + 1) + j] = one[2 * chunk + j]


def put_far(first, far, field):
    for k, one in enumerate(far):
        for j in range(2):
            field[2 * (first + k) + j] = one[j]


def put_pairs(first, arrived, got, field):
    for i, (one, other) in enumerate(zip(arrived, got)):
        field[2 * (first + i)] = one[0]
        field[2 * (first + i) + 1] = other[0]


def step1_kernel(
    nears, fars, chunk, room, me_ref, items_ref, sizes_ref, asked_ref, beside_ref, blocks, *refs
):
    tile, near, far = refs[0], refs[1 : 1 + nears], refs[1 + nears : 1 + nears + fars]
    begun, out, beside_tile, *messages, field, total = refs[1 + nears + fars :]
    own = out.shape[0]
    field[1] = tile[...]
    put_near(chunk, near, field)
    put_far(nears + 1, far, field)
    total[...] = begun[...]
    run_list(both_lists(room, sizes_ref), items_ref, blocks, lambda f: field[f], [total])
    for t in range(own):
        out[t] = (blend * total[t]).astype(out.dtype)
    index = me_ref[0]
    beside_tile[0] = out[beside_ref[0, index]]
    for k, message in enumerate(messages):
        message[0] = out[asked_ref[k + 1, index]]
        message[1] = out[beside_ref[k + 1, index]]


def step1(chunk, me, items, sizes, asked, beside, blocks, tile, near, far, begun):
    own, tile_rows = begun.shape[0] - 1, begun.shape[1]
    n = asked.shape[1]
    dtype = tile.dtype
    count = n // 2 - 1
    out = pl.pallas_call(
        functools.partial(step1_kernel, len(near), len(far), chunk, items.shape[0] // 3),
        out_shape=[
            held((own, tile_rows, LANES), dtype),
            held((1, tile_rows, LANES), dtype),
        ]
        + [held((2, tile_rows, LANES), dtype)] * count,
        in_specs=[SMEM] * 5 + [VMEM] * (3 + len(near) + len(far)),
        out_specs=[VMEM] * (2 + count),
        scratch_shapes=[
            pltpu.VMEM((n, tile_rows, LANES), dtype),
            pltpu.VMEM(begun.shape, begun.dtype),
        ],
        compiler_params=PARAMS,
        cost_estimate=COST,
        name="step1",
    )(me, items, sizes, asked, beside, blocks, tile, *near, *far, begun)
    return out[0], out[1], out[2:]


def near_kernel(nears, room, items_ref, sizes_ref, blocks, *refs):
    got, near, (_, total, field) = refs[: nears + 1], refs[nears + 1 : -3], refs[-3:]
    field[1] = got[0][0]
    put_pairs(1, near, got[1:], field)
    run_list(near_list(room, sizes_ref), items_ref, blocks, lambda f: field[f], [total])


def near_part(items, sizes, blocks, got, near, begun):
    tile_rows = begun.shape[1]
    return pl.pallas_call(
        functools.partial(near_kernel, len(near), items.shape[0] // 3),
        out_shape=held(begun.shape, begun.dtype),
        in_specs=[SMEM] * 2 + [VMEM] * (3 + 2 * len(near)),
        out_specs=VMEM,
        input_output_aliases={4 + 2 * len(near): 0},
        scratch_shapes=[pltpu.VMEM((2 * (len(near) + 1), tile_rows, LANES), got[0].dtype)],
        compiler_params=PARAMS,
        cost_estimate=COST,
        name="near_part",
    )(items, sizes, blocks, *got, *near, begun)


def step2_kernel(gots, count, live, whole, room, items_ref, sizes_ref, blocks, *refs):
    got, arrived = refs[:gots], refs[gots : gots + count]
    begun, wide_ref = refs[gots + count : gots + count + 2]
    *earlier, expo_ref, stats_ref, field, total = refs[gots + count + 2 :]
    own, tile_rows = expo_ref.shape[:2]
    if whole:
        field[1] = got[0][0]
        put_far(1, arrived, field)
    else:
        put_pairs(field.shape[0] // 2 - count, arrived, got, field)
    total[...] = begun[...]
    which = (both_lists if whole else far_list)(room, sizes_ref)
    run_list(which, items_ref, blocks, lambda f: field[f], [total])
    parts = tile_rows // LANES
    last = stats_ref.shape[0] - 1
    if earlier:
        stats_ref[:last] = earlier[0][...]
    for t in range(own):
        logits = wide_ref[t] * total[t]
        lane = lax.broadcasted_iota(jnp.int32, logits.shape, 1)
        if live < LANES:
            top = jnp.max(jnp.where(lane < live, logits, -jnp.inf), axis=1, keepdims=True)
            shifted = jnp.where(lane < live, logits - top, 0.0)
            expo = jnp.where(lane < live, jnp.exp(shifted), 0.0)
        else:
            top = jnp.max(logits, axis=1, keepdims=True)
            shifted = logits - top
            expo = jnp.exp(shifted)
        sums = jnp.sum(expo, axis=1, keepdims=True)
        moments = jnp.sum(expo * shifted, axis=1, keepdims=True)
        expo_ref[t] = expo
        summary = jnp.where(lane == 0, top, jnp.where(lane == 1, sums, moments))
        for i in range(parts):
            flat = summary[i * LANES : (i + 1) * LANES, :].T
            for q in range(3):
                stats_ref[last, q, t * parts + i : t * parts + i + 1, :] = flat[q : q + 1]


def step2(live, whole, n, items, sizes, blocks, got, arrived, begun, wide, earlier):
    own, tile_rows = begun.shape[0] - 1, begun.shape[1]
    before = () if earlier is None else (earlier,)
    count = 1 + (earlier.shape[0] if before else 0)
    return pl.pallas_call(
        functools.partial(
            step2_kernel, len(got), len(arrived), live, whole, items.shape[0] // 3
        ),
        out_shape=[
            held((own, tile_rows, LANES), jnp.float32),
            held((count, 3, own * tile_rows // LANES, LANES), jnp.float32),
        ],
        in_specs=[SMEM] * 2 + [VMEM] * (3 + len(got) + len(arrived) + len(before)),
        out_specs=[VMEM] * 2,
        scratch_shapes=[
            pltpu.VMEM((n, tile_rows, LANES), got[0].dtype),
            pltpu.VMEM(begun.shape, begun.dtype),
        ],
        compiler_params=PARAMS,
        cost_estimate=COST,
        name="step2",
    )(items, sizes, blocks, *got, *arrived, begun, wide, *before)


def finish_kernel(chunks, parts, *refs):
    expos, stats = refs[:chunks], refs[chunks : chunks + parts]
    pseudo_ref, certainty_ref, scale_ref = refs[chunks + parts :]
    own, tile_rows = expos[0].shape[:2]
    width = pseudo_ref.shape[1]
    every = [(s, c) for s in stats for c in range(chunks)]
    top = functools.reduce(jnp.maximum, [s[c, 0] for s, c in every])
    totals, moments, scales = 0.0, 0.0, []
    for s, c in every:
        delta = s[c, 0] - top
        scale = jnp.exp(delta)
        scales.append(scale)
        totals += scale * s[c, 1]
        moments += scale * (s[c, 2] + delta * s[c, 1])
    certainty_ref[...] = 1.0 - (jnp.log(totals) - moments / totals) / jnp.log(jnp.float32(CLS))
    inverse = 1.0 / totals
    for c in range(chunks):
        scale_ref[c] = scales[c] * inverse
    for t in range(own):
        span = slice(t * tile_rows, (t + 1) * tile_rows)
        for c in range(chunks):
            start = c * LANES
            live = min(LANES, width - start)
            value = expos[c][t] * column(scale_ref.at[c], t, tile_rows)
            pseudo_ref[span, start : start + live] = value[:, :live].astype(pseudo_ref.dtype)


def finish(expos, stats, width):
    own, tile_rows = expos[0].shape[:2]
    rows = own * tile_rows
    chunks, parts = len(expos), len(stats)
    return pl.pallas_call(
        functools.partial(finish_kernel, chunks, parts),
        out_shape=[sds((rows, width), jnp.bfloat16), sds((rows // LANES, LANES), jnp.float32)],
        in_specs=[VMEM] * (chunks + parts),
        out_specs=[VMEM] * 2,
        scratch_shapes=[pltpu.VMEM((chunks, rows // LANES, LANES), jnp.float32)],
        compiler_params=PARAMS,
        name="finish",
    )(*expos, *stats)


def local(prior, blocks, links, counts, fetch, seeds, inv_temp):
    width = prior.shape[1]
    tile_rows = blocks.shape[2]
    n = lax.axis_size("rows")
    parts = lax.axis_size("cls")
    chunks = pl.cdiv(width, LANES)
    me = jnp.stack([lax.axis_index("rows"), lax.axis_index("cls") * width]).astype(jnp.int32)
    fetch = fetch.reshape(n)
    first = near_bound(n)
    near_ks, far_ks = range(1, first), range(first, n // 2)
    neighbour = swap(prior, n).reshape(-1, tile_rows, width)
    prior = prior.reshape(-1, tile_rows, width)
    lists = send([fetch] * (n // 2 - 1), range(1, n // 2), n)
    tabs, neighbours = split(prior, chunks), split(neighbour, chunks)
    blocks = blocks.reshape((-1,) + blocks.shape[2:])
    seeds = seeds.reshape(-1, LANES)
    temp = inv_temp.reshape(-1, LANES)

    asked, tiles, near_sent, far_sent = pick(me, fetch, lists, tabs, neighbours)
    beside = swap(asked, n)
    near = send(near_sent, near_ks, n)
    far = [send(far_sent[0], far_ks, n)]
    items, sizes = prepare(me, links, counts, after(fetch, near_sent, far_sent))
    parcels = []
    for c in range(1, chunks):
        parcels = [after(part, sizes, beside) for part in far_sent[c]]
        far.append(send(parcels, far_ks, n))
    blocks, begun = begin(
        me, items, sizes, counts, after(blocks, parcels), prior, seeds, chunks
    )
    firsts, there = [], []
    ks = range(1, n // 2)
    for c in range(chunks):
        out, tile, parcels = step1(
            c, me, items, sizes, asked, beside, blocks, tiles[c], near, far[c],
            after(begun[c], parcels),
        )
        firsts.append(out)
        if c < chunks - 1:
            seconds = [swap(part[1:], n) for part in parcels]
            parcels = [jnp.concatenate([p[:1], q]) for p, q in zip(parcels, seconds)]
            tile = swap(after(tile, parcels), n)
        elif there:
            parcels = [after(part, there[-1][1][: first - 1]) for part in parcels]
        there.append((tile, send(parcels[::-1], ks[::-1], n)[::-1]))
    wide, begun = own_part(me, items, sizes, blocks, after(seeds, parcels), temp, firsts)
    expos, stats = [], None
    for c in range(chunks):
        live = min(LANES, width - c * LANES)
        (tile, here), total = there[c], begun[c]
        if c < chunks - 1:
            got = [tile]
        else:
            near, here = here[: first - 1], here[first - 1 :]
            tile = after(tile, near)
            got = [swap(part, n) for part in [tile] + [part[1:] for part in near]]
            total = near_part(items, sizes, blocks, got, near, total)
            if stats is not None:
                here = [after(part, stats) for part in here]
            got = [swap(part[1:], n) for part in here]
        expo, stats = step2(
            live, c < chunks - 1, n, items, sizes, blocks, got, here, total, wide, stats
        )
        expos.append(expo)
    stats = [stats] + [
        lax.ppermute(stats, "cls", [(i, (i + k) % parts) for i in range(parts)])
        for k in range(1, parts)
    ]
    pseudo, certainty = finish(expos, stats, width)
    return pseudo, certainty.reshape(-1)


def solution(mesh):
    return jax.shard_map(
        local,
        mesh=mesh,
        in_specs=(
            P("rows", "cls"),
            P("rows", None, None, None),
            P("rows", None),
            P("rows"),
            P("rows", None, None),
            P("rows"),
            P("rows"),
        ),
        out_specs=(P("rows", "cls"), P("rows")),
        check_vma=False,
    )
```

time: 80.5 us -> 79.8 us (level)
  Pallas kernels: 36.6 us -> 33.4 us
  waiting for transfers between devices: 12 us -> 14.2 us
    ppermute x12 -> x14, waiting for transfers between devices: 4.17 us -> 10.6 us  [send(): lax.ppermute(part, 'rows', [(i, i ^ 2 * k) for i in range(n)])]
    all_to_all x1 -> x0, starting transfers between devices: 6 us -> none  [local(): lax.all_to_all(ask(fetch), 'rows', split_axis=0, concat_axis=0, tiled=True)]
    pallas_call x2 -> x1, Pallas kernels: 9.14 us -> 4.1 us  [own_part(): pl.pallas_call(functools.partial(own_kernel, chunks, items.shape[0] // 3)...]
    ppermute x12 -> x14, starting transfers between devices: 17.3 us -> 21.8 us  [send(): lax.ppermute(part, 'rows', [(i, i ^ 2 * k) for i in range(n)])]
    all_to_all x1 -> x0, waiting for transfers between devices: 3.57 us -> none  [local(): lax.all_to_all(ask(fetch), 'rows', split_axis=0, concat_axis=0, tiled=True)]
    pallas_call x10, Pallas kernels: 25.8 us -> 27.7 us  [the longest x2 8.08 us: step2(): pl.pallas_call(functools.partial(step2_kernel, len(got), len(arrived), li...]
    ppermute x5 -> x10, starting transfers between devices: 1.66 us -> 3.21 us  [swap(): return lax.ppermute(value, 'rows', [(i, i ^ 1) for i in range(n)])]
    ppermute x5 -> x10, waiting for transfers between devices: 1.65 us -> 0.92 us  [swap(): return lax.ppermute(value, 'rows', [(i, i ^ 1) for i in range(n)])]
  transfers between devices with their start and end apart: 21 -> 27, of which waited for: 8 -> 11; matrix products, arithmetic and copies ran while one was open for 0% -> 0% of each run, Pallas kernels for 35% -> 34%
where the time goes in v4:
time: 79.8 us; the launch traced here: 79.4 us
  Pallas kernels  33.4 us (42%)
  starting transfers between devices  29.4 us (37%)
  waiting for transfers between devices  14.2 us (18%)
  local copies, waits for them, and re-layouts  1.3 us (2%)
  between operations  0.88 us (1%)
    ppermute x14, starting transfers between devices, send(): lax.ppermute(part, 'rows', [(i, i ^ 2 * k) for i in range(n)])  21.8 us
    ppermute x14, waiting for transfers between devices, send(): lax.ppermute(part, 'rows', [(i, i ^ 2 * k) for i in range(n)])  10.6 us
    pallas_call x2, Pallas kernels, step2(): pl.pallas_call(functools.partial(step2_kernel, len(got), len(arrived), li...  8.08 us
    pallas_call x1, Pallas kernels, begin(): pl.pallas_call(functools.partial(begin_kernel, items.shape[0] // 3), out_...  6.8 us
    pallas_call x2, Pallas kernels, step1(): pl.pallas_call(functools.partial(step1_kernel, len(near), len(far), chunk...  6.14 us
    ppermute x3, starting transfers between devices, local(): lax.ppermute(stats, 'cls', [(i, (i + k) % parts) for i in range(parts)])  4.48 us
    pallas_call x1, Pallas kernels, own_part(): pl.pallas_call(functools.partial(own_kernel, chunks, items.shape[0] // 3)...  4.1 us
    ppermute x10, starting transfers between devices, swap(): return lax.ppermute(value, 'rows', [(i, i ^ 1) for i in range(n)])  3.21 us
  transfers between devices with their start and end apart: 27, of which 11 were waited for; matrix products, arithmetic and copies ran while one was open for 0% of the time, Pallas kernels for 34%

profile of v4, /device:TPU:0, one launch (start us, length us, event | category | flops | bytes accessed | tf_op | source)
XLA Modules:
  0.0 79.4 jit_solution(9209330617353995926)
XLA Ops:
  1.2 2.7 %collective-permute-start = (s32[8]{0:T(128)}, s32[8]{0:T(128)S(1)}, u32[]{:S(2)}, u32[]{:S(2)}) collective-permute-start(s32[8]{0:T(128)} %bitcast.15), channel_id=1, source_target_pairs={{0,2},{1,3},{2,0},{3,1},{4,6},{5,7},{6,4},{7,5},{8,10},{9,11},{10,... | collective-permute-start | bytes 104 | tf_op jit(solution)/shard_map/ppermute | solution.py:182
  3.8 2.6 %collective-permute-start.1 = (s32[8]{0:T(128)}, s32[8]{0:T(128)S(1)}, u32[]{:S(2)}, u32[]{:S(2)}) collective-permute-start(s32[8]{0:T(128)} %bitcast.16), channel_id=1, source_target_pairs={{0,4},{1,5},{2,6},{3,7},{4,0},{5,1},{6,2},{7,3},{8,12},{9,13},{10,... | collective-permute-start | bytes 104 | tf_op jit(solution)/shard_map/ppermute | solution.py:182
  6.4 1.2 %copy-done = bf16[2048,250]{1,0:T(8,128)(2,1)S(1)} copy-done((bf16[2048,250]{1,0:T(8,128)(2,1)S(1)}, bf16[2048,250]{1,0:T(8,128)(2,1)}, u32[]{:S(2)}) %copy-start) | copy-done | bytes 1024024
  8.4 3.5 %collective-permute-done.2.refs_2_ = s32[8]{0:T(128)S(1)} collective-permute-done((s32[8]{0:T(128)}, s32[8]{0:T(128)S(1)}, u32[]{:S(2)}, u32[]{:S(2)}) %collective-permute-start.2) | collective-permute-done | bytes 64 | tf_op jit(solution)/shard_map/ppermute | solution.py:182
  13.9 3.6 %collective-permute-start.7 = (bf16[2,256,128]{2,1,0:T(8,128)(2,1)S(1)}, bf16[2,256,128]{2,1,0:T(8,128)(2,1)S(1)}, u32[]{:S(2)}, u32[]{:S(2)}) collective-permute-start(bf16[2,256,128]{2,1,0:T(8,128)(2,1)S(1)} %get-tuple-element.58), channel_id=1, source_target_pairs={{0,6},{1,7},{2,4},{3,5},{4,2},{5,3},{6,0},{7,1},{8,14},{9,15},{10,... | collective-permute-start | bytes 393224 | tf_op jit(solution)/shard_map/ppermute | solution.py:182
  17.6 2.9 %prepare.1 = (s32[624]{0:T(1024)S(1)}, s32[4]{0:T(128)S(1)}) custom-call(s32[2]{0:T(128)S(1)} %pad_add_fusion.me_ref, s32[8,24]{1,0:T(8,128)S(1)} %copy-done.4, s32[8]{0:T(128)S(1)} %copy-done.5, s32[8]{0:T(128)S(1)} %bitcast.19), custom_call_target="tpu_custom_call" | custom-call | flops 1 | bytes 1 | tf_op jit(solution)/shard_map/prepare/pallas_call | solution.py:243
  20.6 1.5 %collective-permute-start.16 = (bf16[2,256,128]{2,1,0:T(8,128)(2,1)S(1)}, bf16[2,256,128]{2,1,0:T(8,128)(2,1)S(1)}, u32[]{:S(2)}, u32[]{:S(2)}) collective-permute-start(bf16[2,256,128]{2,1,0:T(8,128)(2,1)S(1)} %get-tuple-element.66), channel_id=1, source_target_pairs={{0,6},{1,7},{2,4},{3,5},{4,2},{5,3},{6,0},{7,1},{8,14},{9,15},{10,... | collective-permute-start | bytes 393224 | tf_op jit(solution)/shard_map/ppermute | solution.py:182
  22.1 6.8 %begin.1 = (bf16[192,256,256]{2,1,0:T(8,128)(2,1)S(1)}, f32[9,256,128]{2,1,0:T(8,128)S(1)}, f32[9,256,128]{2,1,0:T(8,128)S(1)}) custom-call(s32[2]{0:T(128)S(1)} %pad_add_fusion.me_ref, s32[624]{0:T(1024)S(1)} %get-tuple-element.62.items_ref, s32[4]{0:T(128)S(1)} %get-tuple-element.63.sizes_ref, s32[8]{0:T(128)S(1)} %copy-done.5, ...), custom_call_target="tpu_custom_call" | custom-call | flops 1 | bytes 1 | tf_op jit(solution)/shard_map/begin/pallas_call | solution.py:289
  29.0 2.1 %collective-permute-done.6.refs_2_ = bf16[2,256,128]{2,1,0:T(8,128)(2,1)S(1)} collective-permute-done((bf16[2,256,128]{2,1,0:T(8,128)(2,1)S(1)}, bf16[2,256,128]{2,1,0:T(8,128)(2,1)S(1)}, u32[]{:S(2)}, u32[]{:S(2)}) %collective-permute-start.6) | collective-permute-done | bytes 131104 | tf_op jit(solution)/shard_map/ppermute | solution.py:182
  31.1 3.1 %step1.2 = (bf16[8,256,128]{2,1,0:T(8,128)(2,1)S(1)}, bf16[1,256,128]{2,1,0:T(8,128)(2,1)S(1)}, bf16[2,256,128]{2,1,0:T(8,128)(2,1)S(1)}, bf16[2,256,128]{2,1,0:T(8,128)(2,1)S(1)}, bf16[2,256,128]{2,1,0:T(8,128)(2,1)S(1)}) custom-call(s32[2]{0:T(128)S(1)} %pad_add_fusion.me_ref, s32[624]{0:T(1024)S(1)} %get-tuple-element.62.items_ref, ...), custom_call_target="tpu_custom_call" | custom-call | flops 1 | bytes 1 | tf_op jit(solution)/shard_map/step1/pallas_call | solution.py:376
  36.0 3.0 %collective-permute-start.12 = (bf16[2,256,128]{2,1,0:T(8,128)(2,1)S(1)}, bf16[2,256,128]{2,1,0:T(8,128)(2,1)S(1)}, u32[]{:S(2)}, u32[]{:S(2)}) collective-permute-start(bf16[2,256,128]{2,1,0:T(8,128)(2,1)S(1)} %pad_maximum_fusion), channel_id=1, source_target_pairs={{0,2},{1,3},{2,0},{3,1},{4,6},{5,7},{6,4},{7,5},{8,10},{9,11},{10,... | collective-permute-start | bytes 393224 | tf_op jit(solution)/shard_map/ppermute | solution.py:182
  39.5 2.6 %collective-permute-start.14 = (bf16[2,256,128]{2,1,0:T(8,128)(2,1)S(1)}, bf16[2,256,128]{2,1,0:T(8,128)(2,1)S(1)}, u32[]{:S(2)}, u32[]{:S(2)}) collective-permute-start(bf16[2,256,128]{2,1,0:T(8,128)(2,1)S(1)} %pad_maximum_fusion.2), channel_id=1, source_target_pairs={{0,6},{1,7},{2,4},{3,5},{4,2},{5,3},{6,0},{7,1},{8,14},{9,15},{10,... | collective-permute-start | bytes 393224 | tf_op jit(solution)/shard_map/ppermute | solution.py:182
  42.1 3.1 %step1.3 = (bf16[8,256,128]{2,1,0:T(8,128)(2,1)S(1)}, bf16[1,256,128]{2,1,0:T(8,128)(2,1)S(1)}, bf16[2,256,128]{2,1,0:T(8,128)(2,1)S(1)}, bf16[2,256,128]{2,1,0:T(8,128)(2,1)S(1)}, bf16[2,256,128]{2,1,0:T(8,128)(2,1)S(1)}) custom-call(s32[2]{0:T(128)S(1)} %pad_add_fusion.me_ref, s32[624]{0:T(1024)S(1)} %get-tuple-element.62.items_ref, ...), custom_call_target="tpu_custom_call" | custom-call | flops 1 | bytes 1 | tf_op jit(solution)/shard_map/step1/pallas_call | solution.py:376
  46.3 3.4 %collective-permute-start.19 = (bf16[2,256,128]{2,1,0:T(8,128)(2,1)S(1)}, bf16[2,256,128]{2,1,0:T(8,128)(2,1)S(1)}, u32[]{:S(2)}, u32[]{:S(2)}) collective-permute-start(bf16[2,256,128]{2,1,0:T(8,128)(2,1)S(1)} %get-tuple-element.85), channel_id=1, source_target_pairs={{0,6},{1,7},{2,4},{3,5},{4,2},{5,3},{6,0},{7,1},{8,14},{9,15},{10,... | collective-permute-start | bytes 393224 | tf_op jit(solution)/shard_map/ppermute | solution.py:182
  49.7 4.1 %own_part.1 = (f32[8,256,128]{2,1,0:T(8,128)S(1)}, f32[9,256,128]{2,1,0:T(8,128)S(1)}, f32[9,256,128]{2,1,0:T(8,128)S(1)}) custom-call(s32[2]{0:T(128)S(1)} %pad_add_fusion.me_ref, s32[624]{0:T(1024)S(1)} %get-tuple-element.62.items_ref, s32[4]{0:T(128)S(1)} %get-tuple-element.63.sizes_ref, bf16[192,256,256]{2,1,0:T(8,128)(2,1)S(1)} %get-tuple-element.68.blocks, ...), custom_call_target="tpu_custom_call" | custom-call | flops 1 | bytes 1 | tf_op jit(solution)/shard_map/own_part/pallas_call | solution.py:320
  54.6 4.4 %step2.2 = (f32[8,256,128]{2,1,0:T(8,128)S(1)}, f32[1,3,16,128]{3,2,1,0:T(8,128)S(1)}) custom-call(s32[624]{0:T(1024)S(1)} %get-tuple-element.62.items_ref, s32[4]{0:T(128)S(1)} %get-tuple-element.63.sizes_ref, bf16[192,256,256]{2,1,0:T(8,128)(2,1)S(1)} %get-tuple-element.68.blocks, bf16[1,256,128]{2,1,0:T(8,128)(2,1)S(1)} %collective-permute-done.11.refs_0_, ...), custom_call_target="tpu_custom_call" | custom-call | flops 1 | bytes 1 | tf_op jit(solution)/shard_map/step2/pallas_call | solution.py:460
  59.0 4.0 %collective-permute-done.17.refs_2_ = bf16[2,256,128]{2,1,0:T(8,128)(2,1)S(1)} collective-permute-done((bf16[2,256,128]{2,1,0:T(8,128)(2,1)S(1)}, bf16[2,256,128]{2,1,0:T(8,128)(2,1)S(1)}, u32[]{:S(2)}, u32[]{:S(2)}) %collective-permute-start.17) | collective-permute-done | bytes 131104 | tf_op jit(solution)/shard_map/ppermute | solution.py:182
  64.8 2.1 %near_part.1.refs_4_ = f32[9,256,128]{2,1,0:T(8,128)S(1)} custom-call(s32[624]{0:T(1024)S(1)} %get-tuple-element.62.items_ref, s32[4]{0:T(128)S(1)} %get-tuple-element.63.sizes_ref, bf16[192,256,256]{2,1,0:T(8,128)(2,1)S(1)} %get-tuple-element.68.blocks, bf16[1,256,128]{2,1,0:T(8,128)(2,1)S(1)} %collective-permute-done.22.refs_0_, ...), custom_call_target="tpu_custom_call", output_to_operand_aliasing={{}: (6, {})} | custom-call | flops 1 | bytes 1 | tf_op jit(solution)/shard_map/near_part/pallas_call | solution.py:405
  66.9 3.7 %step2.3 = (f32[8,256,128]{2,1,0:T(8,128)S(1)}, f32[2,3,16,128]{3,2,1,0:T(8,128)S(1)}) custom-call(s32[624]{0:T(1024)S(1)} %get-tuple-element.62.items_ref, s32[4]{0:T(128)S(1)} %get-tuple-element.63.sizes_ref, bf16[192,256,256]{2,1,0:T(8,128)(2,1)S(1)} %get-tuple-element.68.blocks, bf16[1,256,128]{2,1,0:T(8,128)(2,1)S(1)} %collective-permute-done.18.refs_0_, ...), custom_call_target="tpu_custom_call" | custom-call | flops 1 | bytes 1 | tf_op jit(solution)/shard_map/step2/pallas_call | solution.py:460
  70.6 1.5 %collective-permute-start.24 = (f32[2,3,16,128]{3,2,1,0:T(8,128)S(1)}, f32[2,3,16,128]{3,2,1,0:T(8,128)S(1)}, u32[]{:S(2)}, u32[]{:S(2)}) collective-permute-start(f32[2,3,16,128]{3,2,1,0:T(8,128)S(1)} %get-tuple-element.99.refs_2_), channel_id=1, source_target_pairs={{0,8},{8,16},{16,24},{24,0},{1,9},{9,17},{17,25},{25,1},{2,10},{10... | collective-permute-start | bytes 147464 | tf_op jit(solution)/shard_map/ppermute | solution.py:587
  72.1 1.5 %collective-permute-start.25 = (f32[2,3,16,128]{3,2,1,0:T(8,128)S(1)}, f32[2,3,16,128]{3,2,1,0:T(8,128)S(1)}, u32[]{:S(2)}, u32[]{:S(2)}) collective-permute-start(f32[2,3,16,128]{3,2,1,0:T(8,128)S(1)} %get-tuple-element.99.refs_2_), channel_id=1, source_target_pairs={{0,16},{8,24},{16,0},{24,8},{1,17},{9,25},{17,1},{25,9},{2,18},{10... | collective-permute-start | bytes 147464 | tf_op jit(solution)/shard_map/ppermute | solution.py:587
  73.6 1.4 %collective-permute-start.26 = (f32[2,3,16,128]{3,2,1,0:T(8,128)S(1)}, f32[2,3,16,128]{3,2,1,0:T(8,128)S(1)}, u32[]{:S(2)}, u32[]{:S(2)}) collective-permute-start(f32[2,3,16,128]{3,2,1,0:T(8,128)S(1)} %get-tuple-element.99.refs_2_), channel_id=1, source_target_pairs={{0,24},{8,0},{16,8},{24,16},{1,25},{9,1},{17,9},{25,17},{2,26},{10... | collective-permute-start | bytes 147464 | tf_op jit(solution)/shard_map/ppermute | solution.py:587
  76.4 1.3 %collective-permute-done.26.refs_5_ = f32[2,3,16,128]{3,2,1,0:T(8,128)S(1)} collective-permute-done((f32[2,3,16,128]{3,2,1,0:T(8,128)S(1)}, f32[2,3,16,128]{3,2,1,0:T(8,128)S(1)}, u32[]{:S(2)}, u32[]{:S(2)}) %collective-permute-start.26) | collective-permute-done | bytes 49184 | tf_op jit(solution)/shard_map/ppermute | solution.py:587
  77.7 1.6 %finish.1 = (bf16[2048,250]{1,0:T(8,128)(2,1)}, f32[16,128]{1,0:T(8,128)}) custom-call(f32[8,256,128]{2,1,0:T(8,128)S(1)} %get-tuple-element.91.refs_0_, f32[8,256,128]{2,1,0:T(8,128)S(1)} %get-tuple-element.98.refs_1_, f32[2,3,16,128]{3,2,1,0:T(8,128)S(1)} %get-tuple-element.99.refs_2_, f32[2,3,16,128]{3,2,1,0:T(8,128)S(1)} %collective-permute-done.24.refs_3_, ...), custom_call_target="tpu_custom_call" | custom-call | tf_op jit(solution)/shard_map/finish/pallas_call | solution.py:511
  (66 shorter events, 10.7 us)
Async XLA Ops:
  0.6 7.3 %collective-permute-start.3 = (bf16[2048,250]{1,0:T(8,128)(2,1)}, bf16[2048,250]{1,0:T(8,128)(2,1)S(1)}, u32[]{:S(2)}, u32[]{:S(2)}) collective-permute-start(bf16[2048,250]{1,0:T(8,128)(2,1)} %param.7), channel_id=1, source_target_pairs={{0,1},{1,0},{2,3},{3,2},{4,5},{5,4},{6,7},{7,6},{8,9},{9,8},{10,11... | collective-permute-start | bytes 3072008 | tf_op jit(solution)/shard_map/ppermute | solution.py:177
  1.2 7.1 %collective-permute-start = (s32[8]{0:T(128)}, s32[8]{0:T(128)S(1)}, u32[]{:S(2)}, u32[]{:S(2)}) collective-permute-start(s32[8]{0:T(128)} %bitcast.15), channel_id=1, source_target_pairs={{0,2},{1,3},{2,0},{3,1},{4,6},{5,7},{6,4},{7,5},{8,10},{9,11},{10,... | collective-permute-start | bytes 104 | tf_op jit(solution)/shard_map/ppermute | solution.py:182
  3.8 4.6 %collective-permute-start.1 = (s32[8]{0:T(128)}, s32[8]{0:T(128)S(1)}, u32[]{:S(2)}, u32[]{:S(2)}) collective-permute-start(s32[8]{0:T(128)} %bitcast.16), channel_id=1, source_target_pairs={{0,4},{1,5},{2,6},{3,7},{4,0},{5,1},{6,2},{7,3},{8,12},{9,13},{10,... | collective-permute-start | bytes 104 | tf_op jit(solution)/shard_map/ppermute | solution.py:182
  6.4 5.5 %collective-permute-start.2 = (s32[8]{0:T(128)}, s32[8]{0:T(128)S(1)}, u32[]{:S(2)}, u32[]{:S(2)}) collective-permute-start(s32[8]{0:T(128)} %bitcast.17), channel_id=1, source_target_pairs={{0,6},{1,7},{2,4},{3,5},{4,2},{5,3},{6,0},{7,1},{8,14},{9,15},{10,... | collective-permute-start | bytes 104 | tf_op jit(solution)/shard_map/ppermute | solution.py:182
  13.1 18.0 %collective-permute-start.5 = (bf16[4,256,128]{2,1,0:T(8,128)(2,1)S(1)}, bf16[4,256,128]{2,1,0:T(8,128)(2,1)S(1)}, u32[]{:S(2)}, u32[]{:S(2)}) collective-permute-start(bf16[4,256,128]{2,1,0:T(8,128)(2,1)S(1)} %get-tuple-element.56), channel_id=1, source_target_pairs={{0,2},{1,3},{2,0},{3,1},{4,6},{5,7},{6,4},{7,5},{8,10},{9,11},{10,... | collective-permute-start | bytes 786440 | tf_op jit(solution)/shard_map/ppermute | solution.py:182
  13.2 17.9 %collective-permute-start.6 = (bf16[2,256,128]{2,1,0:T(8,128)(2,1)S(1)}, bf16[2,256,128]{2,1,0:T(8,128)(2,1)S(1)}, u32[]{:S(2)}, u32[]{:S(2)}) collective-permute-start(bf16[2,256,128]{2,1,0:T(8,128)(2,1)S(1)} %get-tuple-element.57), channel_id=1, source_target_pairs={{0,4},{1,5},{2,6},{3,7},{4,0},{5,1},{6,2},{7,3},{8,12},{9,13},{10,... | collective-permute-start | bytes 393224 | tf_op jit(solution)/shard_map/ppermute | solution.py:182
  13.9 17.1 %collective-permute-start.7 = (bf16[2,256,128]{2,1,0:T(8,128)(2,1)S(1)}, bf16[2,256,128]{2,1,0:T(8,128)(2,1)S(1)}, u32[]{:S(2)}, u32[]{:S(2)}) collective-permute-start(bf16[2,256,128]{2,1,0:T(8,128)(2,1)S(1)} %get-tuple-element.58), channel_id=1, source_target_pairs={{0,6},{1,7},{2,4},{3,5},{4,2},{5,3},{6,0},{7,1},{8,14},{9,15},{10,... | collective-permute-start | bytes 393224 | tf_op jit(solution)/shard_map/ppermute | solution.py:182
  17.6 3.0 %collective-permute-start.4 = (s32[4,8]{1,0:T(4,128)S(1)}, s32[4,8]{1,0:T(4,128)S(1)}, u32[]{:S(2)}, u32[]{:S(2)}) collective-permute-start(s32[4,8]{1,0:T(4,128)S(1)} %get-tuple-element.64.asked_ref), channel_id=1, source_target_pairs={{0,1},{1,0},{2,3},{3,2},{4,5},{5,4},{6,7},{7,6},{8,9},{9,8},{10,11... | collective-permute-start | bytes 392 | tf_op jit(solution)/shard_map/ppermute | solution.py:177
  20.5 19.0 %collective-permute-start.15 = (bf16[2,256,128]{2,1,0:T(8,128)(2,1)S(1)}, bf16[2,256,128]{2,1,0:T(8,128)(2,1)S(1)}, u32[]{:S(2)}, u32[]{:S(2)}) collective-permute-start(bf16[2,256,128]{2,1,0:T(8,128)(2,1)S(1)} %get-tuple-element.65), channel_id=1, source_target_pairs={{0,4},{1,5},{2,6},{3,7},{4,0},{5,1},{6,2},{7,3},{8,12},{9,13},{10,... | collective-permute-start | bytes 393224 | tf_op jit(solution)/shard_map/ppermute | solution.py:182
  20.6 21.5 %collective-permute-start.16 = (bf16[2,256,128]{2,1,0:T(8,128)(2,1)S(1)}, bf16[2,256,128]{2,1,0:T(8,128)(2,1)S(1)}, u32[]{:S(2)}, u32[]{:S(2)}) collective-permute-start(bf16[2,256,128]{2,1,0:T(8,128)(2,1)S(1)} %get-tuple-element.66), channel_id=1, source_target_pairs={{0,6},{1,7},{2,4},{3,5},{4,2},{5,3},{6,0},{7,1},{8,14},{9,15},{10,... | collective-permute-start | bytes 393224 | tf_op jit(solution)/shard_map/ppermute | solution.py:182
  35.1 3.9 %collective-permute-start.9 = (bf16[1,256,128]{2,1,0:T(8,128)(2,1)S(1)}, bf16[1,256,128]{2,1,0:T(8,128)(2,1)S(1)}, u32[]{:S(2)}, u32[]{:S(2)}) collective-permute-start(bf16[1,256,128]{2,1,0:T(8,128)(2,1)S(1)} %get-tuple-element.105), channel_id=1, source_target_pairs={{0,1},{1,0},{2,3},{3,2},{4,5},{5,4},{6,7},{7,6},{8,9},{9,8},{10,11... | collective-permute-start | bytes 196616 | tf_op jit(solution)/shard_map/ppermute | solution.py:177
  35.2 3.8 %collective-permute-start.10 = (bf16[1,256,128]{2,1,0:T(8,128)(2,1)S(1)}, bf16[1,256,128]{2,1,0:T(8,128)(2,1)S(1)}, u32[]{:S(2)}, u32[]{:S(2)}) collective-permute-start(bf16[1,256,128]{2,1,0:T(8,128)(2,1)S(1)} %get-tuple-element.103), channel_id=1, source_target_pairs={{0,1},{1,0},{2,3},{3,2},{4,5},{5,4},{6,7},{7,6},{8,9},{9,8},{10,11... | collective-permute-start | bytes 196616 | tf_op jit(solution)/shard_map/ppermute | solution.py:177
  36.0 9.2 %collective-permute-start.12 = (bf16[2,256,128]{2,1,0:T(8,128)(2,1)S(1)}, bf16[2,256,128]{2,1,0:T(8,128)(2,1)S(1)}, u32[]{:S(2)}, u32[]{:S(2)}) collective-permute-start(bf16[2,256,128]{2,1,0:T(8,128)(2,1)S(1)} %pad_maximum_fusion), channel_id=1, source_target_pairs={{0,2},{1,3},{2,0},{3,1},{4,6},{5,7},{6,4},{7,5},{8,10},{9,11},{10,... | collective-permute-start | bytes 393224 | tf_op jit(solution)/shard_map/ppermute | solution.py:182
  39.0 7.3 %collective-permute-start.11 = (bf16[1,256,128]{2,1,0:T(8,128)(2,1)S(1)}, bf16[1,256,128]{2,1,0:T(8,128)(2,1)S(1)}, u32[]{:S(2)}, u32[]{:S(2)}) collective-permute-start(bf16[1,256,128]{2,1,0:T(8,128)(2,1)S(1)} %get-tuple-element.76), channel_id=1, source_target_pairs={{0,1},{1,0},{2,3},{3,2},{4,5},{5,4},{6,7},{7,6},{8,9},{9,8},{10,11... | collective-permute-start | bytes 196616 | tf_op jit(solution)/shard_map/ppermute | solution.py:177
  39.1 15.5 %collective-permute-start.13 = (bf16[2,256,128]{2,1,0:T(8,128)(2,1)S(1)}, bf16[2,256,128]{2,1,0:T(8,128)(2,1)S(1)}, u32[]{:S(2)}, u32[]{:S(2)}) collective-permute-start(bf16[2,256,128]{2,1,0:T(8,128)(2,1)S(1)} %pad_maximum_fusion.1), channel_id=1, source_target_pairs={{0,4},{1,5},{2,6},{3,7},{4,0},{5,1},{6,2},{7,3},{8,12},{9,13},{10,... | collective-permute-start | bytes 393224 | tf_op jit(solution)/shard_map/ppermute | solution.py:182
  39.5 15.1 %collective-permute-start.14 = (bf16[2,256,128]{2,1,0:T(8,128)(2,1)S(1)}, bf16[2,256,128]{2,1,0:T(8,128)(2,1)S(1)}, u32[]{:S(2)}, u32[]{:S(2)}) collective-permute-start(bf16[2,256,128]{2,1,0:T(8,128)(2,1)S(1)} %pad_maximum_fusion.2), channel_id=1, source_target_pairs={{0,6},{1,7},{2,4},{3,5},{4,2},{5,3},{6,0},{7,1},{8,14},{9,15},{10,... | collective-permute-start | bytes 393224 | tf_op jit(solution)/shard_map/ppermute | solution.py:182
  45.2 17.8 %collective-permute-start.17 = (bf16[2,256,128]{2,1,0:T(8,128)(2,1)S(1)}, bf16[2,256,128]{2,1,0:T(8,128)(2,1)S(1)}, u32[]{:S(2)}, u32[]{:S(2)}) collective-permute-start(bf16[2,256,128]{2,1,0:T(8,128)(2,1)S(1)} %get-tuple-element.83), channel_id=1, source_target_pairs={{0,4},{1,5},{2,6},{3,7},{4,0},{5,1},{6,2},{7,3},{8,12},{9,13},{10,... | collective-permute-start | bytes 393224 | tf_op jit(solution)/shard_map/ppermute | solution.py:182
  46.3 16.8 %collective-permute-start.21 = (bf16[2,256,128]{2,1,0:T(8,128)(2,1)S(1)}, bf16[2,256,128]{2,1,0:T(8,128)(2,1)S(1)}, u32[]{:S(2)}, u32[]{:S(2)}) collective-permute-start(bf16[2,256,128]{2,1,0:T(8,128)(2,1)S(1)} %get-tuple-element.81), channel_id=1, source_target_pairs={{0,2},{1,3},{2,0},{3,1},{4,6},{5,7},{6,4},{7,5},{8,10},{9,11},{10,... | collective-permute-start | bytes 393224 | tf_op jit(solution)/shard_map/ppermute | solution.py:182
  46.3 17.3 %collective-permute-start.19 = (bf16[2,256,128]{2,1,0:T(8,128)(2,1)S(1)}, bf16[2,256,128]{2,1,0:T(8,128)(2,1)S(1)}, u32[]{:S(2)}, u32[]{:S(2)}) collective-permute-start(bf16[2,256,128]{2,1,0:T(8,128)(2,1)S(1)} %get-tuple-element.85), channel_id=1, source_target_pairs={{0,6},{1,7},{2,4},{3,5},{4,2},{5,3},{6,0},{7,1},{8,14},{9,15},{10,... | collective-permute-start | bytes 393224 | tf_op jit(solution)/shard_map/ppermute | solution.py:182
  63.0 3.9 %collective-permute-start.18 = (bf16[1,256,128]{2,1,0:T(8,128)(2,1)S(1)}, bf16[1,256,128]{2,1,0:T(8,128)(2,1)S(1)}, u32[]{:S(2)}, u32[]{:S(2)}) collective-permute-start(bf16[1,256,128]{2,1,0:T(8,128)(2,1)S(1)} %slice.33), channel_id=1, source_target_pairs={{0,1},{1,0},{2,3},{3,2},{4,5},{5,4},{6,7},{7,6},{8,9},{9,8},{10,11... | collective-permute-start | bytes 196616 | tf_op jit(solution)/shard_map/ppermute | solution.py:177
  63.6 3.3 %collective-permute-start.20 = (bf16[1,256,128]{2,1,0:T(8,128)(2,1)S(1)}, bf16[1,256,128]{2,1,0:T(8,128)(2,1)S(1)}, u32[]{:S(2)}, u32[]{:S(2)}) collective-permute-start(bf16[1,256,128]{2,1,0:T(8,128)(2,1)S(1)} %slice.34), channel_id=1, source_target_pairs={{0,1},{1,0},{2,3},{3,2},{4,5},{5,4},{6,7},{7,6},{8,9},{9,8},{10,11... | collective-permute-start | bytes 196616 | tf_op jit(solution)/shard_map/ppermute | solution.py:177
  70.6 5.1 %collective-permute-start.24 = (f32[2,3,16,128]{3,2,1,0:T(8,128)S(1)}, f32[2,3,16,128]{3,2,1,0:T(8,128)S(1)}, u32[]{:S(2)}, u32[]{:S(2)}) collective-permute-start(f32[2,3,16,128]{3,2,1,0:T(8,128)S(1)} %get-tuple-element.99.refs_2_), channel_id=1, source_target_pairs={{0,8},{8,16},{16,24},{24,0},{1,9},{9,17},{17,25},{25,1},{2,10},{10... | collective-permute-start | bytes 147464 | tf_op jit(solution)/shard_map/ppermute | solution.py:587
  72.1 4.3 %collective-permute-start.25 = (f32[2,3,16,128]{3,2,1,0:T(8,128)S(1)}, f32[2,3,16,128]{3,2,1,0:T(8,128)S(1)}, u32[]{:S(2)}, u32[]{:S(2)}) collective-permute-start(f32[2,3,16,128]{3,2,1,0:T(8,128)S(1)} %get-tuple-element.99.refs_2_), channel_id=1, source_target_pairs={{0,16},{8,24},{16,0},{24,8},{1,17},{9,25},{17,1},{25,9},{2,18},{10... | collective-permute-start | bytes 147464 | tf_op jit(solution)/shard_map/ppermute | solution.py:587
  73.6 4.1 %collective-permute-start.26 = (f32[2,3,16,128]{3,2,1,0:T(8,128)S(1)}, f32[2,3,16,128]{3,2,1,0:T(8,128)S(1)}, u32[]{:S(2)}, u32[]{:S(2)}) collective-permute-start(f32[2,3,16,128]{3,2,1,0:T(8,128)S(1)} %get-tuple-element.99.refs_2_), channel_id=1, source_target_pairs={{0,24},{8,0},{16,8},{24,16},{1,25},{9,1},{17,9},{25,17},{2,26},{10... | collective-permute-start | bytes 147464 | tf_op jit(solution)/shard_map/ppermute | solution.py:587
  (10 other events, 71.1 us)

commit v5 on v4

--- a/solution.py
+++ b/solution.py
@@ -121,7 +121,7 @@
 def pick_kernel(chunks, me_ref, fetch_ref, *refs):
     n = fetch_ref.shape[0]
     count = n // 2 - 1
-    lists = (fetch_ref,) + refs[:count]
+    lists = (fetch_ref,) + refs[:count][::-1]
     tabs, neighbours = refs[count : count + chunks], refs[count + chunks : count + 2 * chunks]
     asked_ref, *outs = refs[count + 2 * chunks :]
     besides, outs = outs[:chunks], outs[chunks:]
@@ -159,7 +159,7 @@
         out_specs=[SMEM] + [VMEM] * (chunks + near + chunks * far),
         compiler_params=PARAMS,
         name="pick",
-    )(me, fetch, *lists, *tabs, *neighbours)
+    )(me, fetch, *lists[::-1], *tabs, *neighbours)
     far_parts = outs[1 + chunks + near :]
     return (
         outs[0],
@@ -413,6 +413,16 @@
         cost_estimate=COST,
         name="near_part",
     )(items, sizes, blocks, *got, *near, begun)
+
+
+def row_sums(value):
+    ones = jnp.ones((8, value.shape[1]), jnp.bfloat16)
+    high = value.astype(jnp.bfloat16)
+    low = (value - high.astype(jnp.float32)).astype(jnp.bfloat16)
+    add = lambda part: lax.dot_general(
+        ones, part, (((1,), (1,)), ((), ())), preferred_element_type=jnp.float32
+    )
+    return add(high) + add(low)
 
 
 def step2_kernel(gots, count, live, whole, room, items_ref, sizes_ref, blocks, *refs):
@@ -443,14 +453,14 @@
             top = jnp.max(logits, axis=1, keepdims=True)
             shifted = logits - top
             expo = jnp.exp(shifted)
-        sums = jnp.sum(expo, axis=1, keepdims=True)
-        moments = jnp.sum(expo * shifted, axis=1, keepdims=True)
         expo_ref[t] = expo
-        summary = jnp.where(lane == 0, top, jnp.where(lane == 1, sums, moments))
+        sums, moments = row_sums(expo), row_sums(expo * shifted)
         for i in range(parts):
-            flat = summary[i * LANES : (i + 1) * LANES, :].T
-            for q in range(3):
-                stats_ref[last, q, t * parts + i : t * parts + i + 1, :] = flat[q : q + 1]
+            span, at = slice(i * LANES, (i + 1) * LANES), slice(t * parts + i, t * parts + i + 1)
+            flat = jnp.broadcast_to(top[span], (LANES, LANES)).T
+            stats_ref[last, 0, at, :] = flat[:1]
+            stats_ref[last, 1, at, :] = sums[:1, span]
+            stats_ref[last, 2, at, :] = moments[:1, span]
 
 
 def step2(live, whole, n, items, sizes, blocks, got, arrived, begun, wide, earlier):
@@ -560,9 +570,10 @@
         if c < chunks - 1:
             seconds = [swap(part[1:], n) for part in parcels]
             parcels = [jnp.concatenate([p[:1], q]) for p, q in zip(parcels, seconds)]
-            tile = swap(after(tile, parcels), n)
         elif there:
             parcels = [after(part, there[-1][1][: first - 1]) for part in parcels]
+        if c < chunks - 1:
+            parcels = [after(p, parcels[first - 1 :]) for p in parcels[: first - 1]] + parcels[first - 1 :]
         there.append((tile, send(parcels[::-1], ks[::-1], n)[::-1]))
     wide, begun = own_part(me, items, sizes, blocks, after(seeds, parcels), temp, firsts)
     expos, stats = [], None
@@ -570,7 +581,7 @@
         live = min(LANES, width - c * LANES)
         (tile, here), total = there[c], begun[c]
         if c < chunks - 1:
-            got = [tile]
+            got = [swap(after(tile, begun), n)]
         else:
             near, here = here[: first - 1], here[first - 1 :]
             tile = after(tile, near)

time: 79.8 us -> 78.7 us (0.986)
  the two profiles are of different devices: /device:TPU:0 before, /device:TPU:16 now
where the time goes in v5:
time: 78.7 us; the launch traced here: 78.9 us
  Pallas kernels  37.7 us (48%)
  starting transfers between devices  24.3 us (31%)
  waiting for transfers between devices  14.5 us (18%)
  local copies, waits for them, and re-layouts  1.32 us (2%)
  between operations  0.91 us (1%)
    ppermute x14, starting transfers between devices, send(): lax.ppermute(part, 'rows', [(i, i ^ 2 * k) for i in range(n)])  18.4 us
    ppermute x14, waiting for transfers between devices, send(): lax.ppermute(part, 'rows', [(i, i ^ 2 * k) for i in range(n)])  9.84 us
    pallas_call x2, Pallas kernels, step2(): pl.pallas_call(functools.partial(step2_kernel, len(got), len(arrived), li...  8.17 us
    pallas_call x1, Pallas kernels, begin(): pl.pallas_call(functools.partial(begin_kernel, items.shape[0] // 3), out_...  8.11 us
    pallas_call x2, Pallas kernels, step1(): pl.pallas_call(functools.partial(step1_kernel, len(near), len(far), chunk...  7.61 us
    pallas_call x1, Pallas kernels, own_part(): pl.pallas_call(functools.partial(own_kernel, chunks, items.shape[0] // 3)...  5.07 us
    ppermute x3, starting transfers between devices, local(): lax.ppermute(stats, 'cls', [(i, (i + k) % parts) for i in range(parts)])  4.46 us
    pallas_call x1, Pallas kernels, prepare(): pl.pallas_call(functools.partial(prepare_kernel, room), out_shape=[sds((3...  3.41 us
  transfers between devices with their start and end apart: 27, of which 12 were waited for; matrix products, arithmetic and copies ran while one was open for 0% of the time, Pallas kernels for 40%

profile of v5, /device:TPU:16, one launch (start us, length us, event | category | flops | bytes accessed | tf_op | source)
XLA Modules:
  0.0 78.9 jit_solution(13600228076553545193)
XLA Ops:
  1.2 3.5 %collective-permute-start.1 = (s32[8]{0:T(128)}, s32[8]{0:T(128)S(1)}, u32[]{:S(2)}, u32[]{:S(2)}) collective-permute-start(s32[8]{0:T(128)} %bitcast.16), channel_id=1, source_target_pairs={{0,4},{1,5},{2,6},{3,7},{4,0},{5,1},{6,2},{7,3},{8,12},{9,13},{10,... | collective-permute-start | bytes 104 | tf_op jit(solution)/shard_map/ppermute | solution.py:182
  4.7 1.2 %copy-done = bf16[2048,250]{1,0:T(8,128)(2,1)S(1)} copy-done((bf16[2048,250]{1,0:T(8,128)(2,1)S(1)}, bf16[2048,250]{1,0:T(8,128)(2,1)}, u32[]{:S(2)}) %copy-start) | copy-done | bytes 1024024
  6.6 1.8 %collective-permute-done.2.refs_2_ = s32[8]{0:T(128)S(1)} collective-permute-done((s32[8]{0:T(128)}, s32[8]{0:T(128)S(1)}, u32[]{:S(2)}, u32[]{:S(2)}) %collective-permute-start.2) | collective-permute-done | bytes 64 | tf_op jit(solution)/shard_map/ppermute | solution.py:182
  8.4 1.2 %pick.1 = (s32[4,8]{1,0:T(4,128)S(1)}, bf16[256,128]{1,0:T(8,128)(2,1)S(1)}, bf16[256,128]{1,0:T(8,128)(2,1)S(1)}, bf16[4,256,128]{2,1,0:T(8,128)(2,1)S(1)}, bf1...) custom-call(s32[2]{0:T(128)S(1)} %pad_add_fusion.me_ref, ...), custom_call_target="tpu_custom_call" | custom-call | tf_op jit(solution)/shard_map/pick/pallas_call | solution.py:152
  10.7 2.5 %collective-permute-start.7 = (bf16[2,256,128]{2,1,0:T(8,128)(2,1)S(1)}, bf16[2,256,128]{2,1,0:T(8,128)(2,1)S(1)}, u32[]{:S(2)}, u32[]{:S(2)}) collective-permute-start(bf16[2,256,128]{2,1,0:T(8,128)(2,1)S(1)} %get-tuple-element.59), channel_id=1, source_target_pairs={{0,6},{1,7},{2,4},{3,5},{4,2},{5,3},{6,0},{7,1},{8,14},{9,15},{10,... | collective-permute-start | bytes 393224 | tf_op jit(solution)/shard_map/ppermute | solution.py:182
  13.2 3.4 %prepare.1 = (s32[624]{0:T(1024)S(1)}, s32[4]{0:T(128)S(1)}) custom-call(s32[2]{0:T(128)S(1)} %pad_add_fusion.me_ref, s32[8,24]{1,0:T(8,128)S(1)} %copy-done.4, s32[8]{0:T(128)S(1)} %copy-done.5, s32[8]{0:T(128)S(1)} %bitcast.19), custom_call_target="tpu_custom_call" | custom-call | flops 1 | bytes 1 | tf_op jit(solution)/shard_map/prepare/pallas_call | solution.py:243
  16.6 1.6 %collective-permute-start.8 = (bf16[2,256,128]{2,1,0:T(8,128)(2,1)S(1)}, bf16[2,256,128]{2,1,0:T(8,128)(2,1)S(1)}, u32[]{:S(2)}, u32[]{:S(2)}) collective-permute-start(bf16[2,256,128]{2,1,0:T(8,128)(2,1)S(1)} %get-tuple-element.66), channel_id=1, source_target_pairs={{0,4},{1,5},{2,6},{3,7},{4,0},{5,1},{6,2},{7,3},{8,12},{9,13},{10,... | collective-permute-start | bytes 393224 | tf_op jit(solution)/shard_map/ppermute | solution.py:182
  19.4 8.1 %begin.1 = (bf16[192,256,256]{2,1,0:T(8,128)(2,1)S(1)}, f32[9,256,128]{2,1,0:T(8,128)S(1)}, f32[9,256,128]{2,1,0:T(8,128)S(1)}) custom-call(s32[2]{0:T(128)S(1)} %pad_add_fusion.me_ref, s32[624]{0:T(1024)S(1)} %get-tuple-element.63.items_ref, s32[4]{0:T(128)S(1)} %get-tuple-element.64.sizes_ref, s32[8]{0:T(128)S(1)} %copy-done.5, ...), custom_call_target="tpu_custom_call" | custom-call | flops 1 | bytes 1 | tf_op jit(solution)/shard_map/begin/pallas_call | solution.py:289
  27.6 3.2 %collective-permute-done.7.refs_3_ = bf16[2,256,128]{2,1,0:T(8,128)(2,1)S(1)} collective-permute-done((bf16[2,256,128]{2,1,0:T(8,128)(2,1)S(1)}, bf16[2,256,128]{2,1,0:T(8,128)(2,1)S(1)}, u32[]{:S(2)}, u32[]{:S(2)}) %collective-permute-start.7) | collective-permute-done | bytes 131104 | tf_op jit(solution)/shard_map/ppermute | solution.py:182
  30.7 3.8 %step1.2 = (bf16[8,256,128]{2,1,0:T(8,128)(2,1)S(1)}, bf16[1,256,128]{2,1,0:T(8,128)(2,1)S(1)}, bf16[2,256,128]{2,1,0:T(8,128)(2,1)S(1)}, bf16[2,256,128]{2,1,0:T(8,128)(2,1)S(1)}, bf16[2,256,128]{2,1,0:T(8,128)(2,1)S(1)}) custom-call(s32[2]{0:T(128)S(1)} %pad_add_fusion.me_ref, s32[624]{0:T(1024)S(1)} %get-tuple-element.63.items_ref, ...), custom_call_target="tpu_custom_call" | custom-call | flops 1 | bytes 1 | tf_op jit(solution)/shard_map/step1/pallas_call | solution.py:376
  37.1 3.0 %collective-permute-start.16 = (bf16[2,256,128]{2,1,0:T(8,128)(2,1)S(1)}, bf16[2,256,128]{2,1,0:T(8,128)(2,1)S(1)}, u32[]{:S(2)}, u32[]{:S(2)}) collective-permute-start(bf16[2,256,128]{2,1,0:T(8,128)(2,1)S(1)} %pad_maximum_fusion.2), channel_id=1, source_target_pairs={{0,6},{1,7},{2,4},{3,5},{4,2},{5,3},{6,0},{7,1},{8,14},{9,15},{10,... | collective-permute-start | bytes 393224 | tf_op jit(solution)/shard_map/ppermute | solution.py:182
  40.1 3.8 %step1.3 = (bf16[8,256,128]{2,1,0:T(8,128)(2,1)S(1)}, bf16[1,256,128]{2,1,0:T(8,128)(2,1)S(1)}, bf16[2,256,128]{2,1,0:T(8,128)(2,1)S(1)}, bf16[2,256,128]{2,1,0:T(8,128)(2,1)S(1)}, bf16[2,256,128]{2,1,0:T(8,128)(2,1)S(1)}) custom-call(s32[2]{0:T(128)S(1)} %pad_add_fusion.me_ref, s32[624]{0:T(1024)S(1)} %get-tuple-element.63.items_ref, ...), custom_call_target="tpu_custom_call" | custom-call | flops 1 | bytes 1 | tf_op jit(solution)/shard_map/step1/pallas_call | solution.py:376
  44.2 2.3 %collective-permute-start.19 = (bf16[2,256,128]{2,1,0:T(8,128)(2,1)S(1)}, bf16[2,256,128]{2,1,0:T(8,128)(2,1)S(1)}, u32[]{:S(2)}, u32[]{:S(2)}) collective-permute-start(bf16[2,256,128]{2,1,0:T(8,128)(2,1)S(1)} %get-tuple-element.86), channel_id=1, source_target_pairs={{0,6},{1,7},{2,4},{3,5},{4,2},{5,3},{6,0},{7,1},{8,14},{9,15},{10,... | collective-permute-start | bytes 393224 | tf_op jit(solution)/shard_map/ppermute | solution.py:182
  46.5 1.9 %collective-permute-start.21 = (bf16[2,256,128]{2,1,0:T(8,128)(2,1)S(1)}, bf16[2,256,128]{2,1,0:T(8,128)(2,1)S(1)}, u32[]{:S(2)}, u32[]{:S(2)}) collective-permute-start(bf16[2,256,128]{2,1,0:T(8,128)(2,1)S(1)} %get-tuple-element.82), channel_id=1, source_target_pairs={{0,2},{1,3},{2,0},{3,1},{4,6},{5,7},{6,4},{7,5},{8,10},{9,11},{10,... | collective-permute-start | bytes 393224 | tf_op jit(solution)/shard_map/ppermute | solution.py:182
  48.4 5.1 %own_part.1 = (f32[8,256,128]{2,1,0:T(8,128)S(1)}, f32[9,256,128]{2,1,0:T(8,128)S(1)}, f32[9,256,128]{2,1,0:T(8,128)S(1)}) custom-call(s32[2]{0:T(128)S(1)} %pad_add_fusion.me_ref, s32[624]{0:T(1024)S(1)} %get-tuple-element.63.items_ref, s32[4]{0:T(128)S(1)} %get-tuple-element.64.sizes_ref, bf16[192,256,256]{2,1,0:T(8,128)(2,1)S(1)} %get-tuple-element.69.blocks, ...), custom_call_target="tpu_custom_call" | custom-call | flops 1 | bytes 1 | tf_op jit(solution)/shard_map/own_part/pallas_call | solution.py:320
  53.6 4.2 %collective-permute-done.16.refs_3_ = bf16[2,256,128]{2,1,0:T(8,128)(2,1)S(1)} collective-permute-done((bf16[2,256,128]{2,1,0:T(8,128)(2,1)S(1)}, bf16[2,256,128]{2,1,0:T(8,128)(2,1)S(1)}, u32[]{:S(2)}, u32[]{:S(2)}) %collective-permute-start.16) | collective-permute-done | bytes 131104 | tf_op jit(solution)/shard_map/ppermute | solution.py:182
  57.8 4.5 %step2.2 = (f32[8,256,128]{2,1,0:T(8,128)S(1)}, f32[1,3,16,128]{3,2,1,0:T(8,128)S(1)}) custom-call(s32[624]{0:T(1024)S(1)} %get-tuple-element.63.items_ref, s32[4]{0:T(128)S(1)} %get-tuple-element.64.sizes_ref, bf16[192,256,256]{2,1,0:T(8,128)(2,1)S(1)} %get-tuple-element.69.blocks, bf16[1,256,128]{2,1,0:T(8,128)(2,1)S(1)} %collective-permute-done.14.refs_0_, ...), custom_call_target="tpu_custom_call" | custom-call | flops 1 | bytes 1 | tf_op jit(solution)/shard_map/step2/pallas_call | solution.py:470
  64.4 2.1 %near_part.1.refs_4_ = f32[9,256,128]{2,1,0:T(8,128)S(1)} custom-call(s32[624]{0:T(1024)S(1)} %get-tuple-element.63.items_ref, s32[4]{0:T(128)S(1)} %get-tuple-element.64.sizes_ref, bf16[192,256,256]{2,1,0:T(8,128)(2,1)S(1)} %get-tuple-element.69.blocks, bf16[1,256,128]{2,1,0:T(8,128)(2,1)S(1)} %collective-permute-done.22.refs_0_, ...), custom_call_target="tpu_custom_call", output_to_operand_aliasing={{}: (6, {})} | custom-call | flops 1 | bytes 1 | tf_op jit(solution)/shard_map/near_part/pallas_call | solution.py:405
  66.5 3.7 %step2.3 = (f32[8,256,128]{2,1,0:T(8,128)S(1)}, f32[2,3,16,128]{3,2,1,0:T(8,128)S(1)}) custom-call(s32[624]{0:T(1024)S(1)} %get-tuple-element.63.items_ref, s32[4]{0:T(128)S(1)} %get-tuple-element.64.sizes_ref, bf16[192,256,256]{2,1,0:T(8,128)(2,1)S(1)} %get-tuple-element.69.blocks, bf16[1,256,128]{2,1,0:T(8,128)(2,1)S(1)} %collective-permute-done.18.refs_0_, ...), custom_call_target="tpu_custom_call" | custom-call | flops 1 | bytes 1 | tf_op jit(solution)/shard_map/step2/pallas_call | solution.py:470
  70.2 1.5 %collective-permute-start.24 = (f32[2,3,16,128]{3,2,1,0:T(8,128)S(1)}, f32[2,3,16,128]{3,2,1,0:T(8,128)S(1)}, u32[]{:S(2)}, u32[]{:S(2)}) collective-permute-start(f32[2,3,16,128]{3,2,1,0:T(8,128)S(1)} %get-tuple-element.101.refs_2_), channel_id=1, source_target_pairs={{0,8},{8,16},{16,24},{24,0},{1,9},{9,17},{17,25},{25,1},{2,10},{10... | collective-permute-start | bytes 147464 | tf_op jit(solution)/shard_map/ppermute | solution.py:598
  71.7 1.5 %collective-permute-start.25 = (f32[2,3,16,128]{3,2,1,0:T(8,128)S(1)}, f32[2,3,16,128]{3,2,1,0:T(8,128)S(1)}, u32[]{:S(2)}, u32[]{:S(2)}) collective-permute-start(f32[2,3,16,128]{3,2,1,0:T(8,128)S(1)} %get-tuple-element.101.refs_2_), channel_id=1, source_target_pairs={{0,16},{8,24},{16,0},{24,8},{1,17},{9,25},{17,1},{25,9},{2,18},{10... | collective-permute-start | bytes 147464 | tf_op jit(solution)/shard_map/ppermute | solution.py:598
  73.2 1.4 %collective-permute-start.26 = (f32[2,3,16,128]{3,2,1,0:T(8,128)S(1)}, f32[2,3,16,128]{3,2,1,0:T(8,128)S(1)}, u32[]{:S(2)}, u32[]{:S(2)}) collective-permute-start(f32[2,3,16,128]{3,2,1,0:T(8,128)S(1)} %get-tuple-element.101.refs_2_), channel_id=1, source_target_pairs={{0,24},{8,0},{16,8},{24,16},{1,25},{9,1},{17,9},{25,17},{2,26},{10... | collective-permute-start | bytes 147464 | tf_op jit(solution)/shard_map/ppermute | solution.py:598
  76.0 1.4 %collective-permute-done.26.refs_5_ = f32[2,3,16,128]{3,2,1,0:T(8,128)S(1)} collective-permute-done((f32[2,3,16,128]{3,2,1,0:T(8,128)S(1)}, f32[2,3,16,128]{3,2,1,0:T(8,128)S(1)}, u32[]{:S(2)}, u32[]{:S(2)}) %collective-permute-start.26) | collective-permute-done | bytes 49184 | tf_op jit(solution)/shard_map/ppermute | solution.py:598
  77.3 1.6 %finish.1 = (bf16[2048,250]{1,0:T(8,128)(2,1)}, f32[16,128]{1,0:T(8,128)}) custom-call(f32[8,256,128]{2,1,0:T(8,128)S(1)} %get-tuple-element.94.refs_0_, f32[8,256,128]{2,1,0:T(8,128)S(1)} %get-tuple-element.100.refs_1_, f32[2,3,16,128]{3,2,1,0:T(8,128)S(1)} %get-tuple-element.101.refs_2_, f32[2,3,16,128]{3,2,1,0:T(8,128)S(1)} %collective-permute-done.24.refs_3_, ...), custom_call_target="tpu_custom_call" | custom-call | tf_op jit(solution)/shard_map/finish/pallas_call | solution.py:521
  (66 shorter events, 9.7 us)
Async XLA Ops:
  0.6 5.6 %collective-permute-start.3 = (bf16[2048,250]{1,0:T(8,128)(2,1)}, bf16[2048,250]{1,0:T(8,128)(2,1)S(1)}, u32[]{:S(2)}, u32[]{:S(2)}) collective-permute-start(bf16[2048,250]{1,0:T(8,128)(2,1)} %param.7), channel_id=1, source_target_pairs={{0,1},{1,0},{2,3},{3,2},{4,5},{5,4},{6,7},{7,6},{8,9},{9,8},{10,11... | collective-permute-start | bytes 3072008 | tf_op jit(solution)/shard_map/ppermute | solution.py:177
  0.7 5.8 %collective-permute-start = (s32[8]{0:T(128)}, s32[8]{0:T(128)S(1)}, u32[]{:S(2)}, u32[]{:S(2)}) collective-permute-start(s32[8]{0:T(128)} %bitcast.15), channel_id=1, source_target_pairs={{0,6},{1,7},{2,4},{3,5},{4,2},{5,3},{6,0},{7,1},{8,14},{9,15},{10,... | collective-permute-start | bytes 104 | tf_op jit(solution)/shard_map/ppermute | solution.py:182
  1.2 5.3 %collective-permute-start.1 = (s32[8]{0:T(128)}, s32[8]{0:T(128)S(1)}, u32[]{:S(2)}, u32[]{:S(2)}) collective-permute-start(s32[8]{0:T(128)} %bitcast.16), channel_id=1, source_target_pairs={{0,4},{1,5},{2,6},{3,7},{4,0},{5,1},{6,2},{7,3},{8,12},{9,13},{10,... | collective-permute-start | bytes 104 | tf_op jit(solution)/shard_map/ppermute | solution.py:182
  4.7 3.7 %collective-permute-start.2 = (s32[8]{0:T(128)}, s32[8]{0:T(128)S(1)}, u32[]{:S(2)}, u32[]{:S(2)}) collective-permute-start(s32[8]{0:T(128)} %bitcast.17), channel_id=1, source_target_pairs={{0,2},{1,3},{2,0},{3,1},{4,6},{5,7},{6,4},{7,5},{8,10},{9,11},{10,... | collective-permute-start | bytes 104 | tf_op jit(solution)/shard_map/ppermute | solution.py:182
  9.6 21.1 %collective-permute-start.5 = (bf16[4,256,128]{2,1,0:T(8,128)(2,1)S(1)}, bf16[4,256,128]{2,1,0:T(8,128)(2,1)S(1)}, u32[]{:S(2)}, u32[]{:S(2)}) collective-permute-start(bf16[4,256,128]{2,1,0:T(8,128)(2,1)S(1)} %get-tuple-element.57), channel_id=1, source_target_pairs={{0,2},{1,3},{2,0},{3,1},{4,6},{5,7},{6,4},{7,5},{8,10},{9,11},{10,... | collective-permute-start | bytes 786440 | tf_op jit(solution)/shard_map/ppermute | solution.py:182
  9.9 17.6 %collective-permute-start.6 = (bf16[2,256,128]{2,1,0:T(8,128)(2,1)S(1)}, bf16[2,256,128]{2,1,0:T(8,128)(2,1)S(1)}, u32[]{:S(2)}, u32[]{:S(2)}) collective-permute-start(bf16[2,256,128]{2,1,0:T(8,128)(2,1)S(1)} %get-tuple-element.58), channel_id=1, source_target_pairs={{0,4},{1,5},{2,6},{3,7},{4,0},{5,1},{6,2},{7,3},{8,12},{9,13},{10,... | collective-permute-start | bytes 393224 | tf_op jit(solution)/shard_map/ppermute | solution.py:182
  10.7 20.0 %collective-permute-start.7 = (bf16[2,256,128]{2,1,0:T(8,128)(2,1)S(1)}, bf16[2,256,128]{2,1,0:T(8,128)(2,1)S(1)}, u32[]{:S(2)}, u32[]{:S(2)}) collective-permute-start(bf16[2,256,128]{2,1,0:T(8,128)(2,1)S(1)} %get-tuple-element.59), channel_id=1, source_target_pairs={{0,6},{1,7},{2,4},{3,5},{4,2},{5,3},{6,0},{7,1},{8,14},{9,15},{10,... | collective-permute-start | bytes 393224 | tf_op jit(solution)/shard_map/ppermute | solution.py:182
  13.2 3.4 %collective-permute-start.4 = (s32[4,8]{1,0:T(4,128)S(1)}, s32[4,8]{1,0:T(4,128)S(1)}, u32[]{:S(2)}, u32[]{:S(2)}) collective-permute-start(s32[4,8]{1,0:T(4,128)S(1)} %get-tuple-element.65.asked_ref), channel_id=1, source_target_pairs={{0,1},{1,0},{2,3},{3,2},{4,5},{5,4},{6,7},{7,6},{8,9},{9,8},{10,11... | collective-permute-start | bytes 392 | tf_op jit(solution)/shard_map/ppermute | solution.py:177
  16.6 23.5 %collective-permute-start.8 = (bf16[2,256,128]{2,1,0:T(8,128)(2,1)S(1)}, bf16[2,256,128]{2,1,0:T(8,128)(2,1)S(1)}, u32[]{:S(2)}, u32[]{:S(2)}) collective-permute-start(bf16[2,256,128]{2,1,0:T(8,128)(2,1)S(1)} %get-tuple-element.66), channel_id=1, source_target_pairs={{0,4},{1,5},{2,6},{3,7},{4,0},{5,1},{6,2},{7,3},{8,12},{9,13},{10,... | collective-permute-start | bytes 393224 | tf_op jit(solution)/shard_map/ppermute | solution.py:182
  18.2 21.9 %collective-permute-start.9 = (bf16[2,256,128]{2,1,0:T(8,128)(2,1)S(1)}, bf16[2,256,128]{2,1,0:T(8,128)(2,1)S(1)}, u32[]{:S(2)}, u32[]{:S(2)}) collective-permute-start(bf16[2,256,128]{2,1,0:T(8,128)(2,1)S(1)} %get-tuple-element.67), channel_id=1, source_target_pairs={{0,6},{1,7},{2,4},{3,5},{4,2},{5,3},{6,0},{7,1},{8,14},{9,15},{10,... | collective-permute-start | bytes 393224 | tf_op jit(solution)/shard_map/ppermute | solution.py:182
  34.6 1.5 %collective-permute-start.11 = (bf16[1,256,128]{2,1,0:T(8,128)(2,1)S(1)}, bf16[1,256,128]{2,1,0:T(8,128)(2,1)S(1)}, u32[]{:S(2)}, u32[]{:S(2)}) collective-permute-start(bf16[1,256,128]{2,1,0:T(8,128)(2,1)S(1)} %get-tuple-element.107), channel_id=1, source_target_pairs={{0,1},{1,0},{2,3},{3,2},{4,5},{5,4},{6,7},{7,6},{8,9},{9,8},{10,11... | collective-permute-start | bytes 196616 | tf_op jit(solution)/shard_map/ppermute | solution.py:177
  36.6 7.4 %collective-permute-start.13 = (bf16[2,256,128]{2,1,0:T(8,128)(2,1)S(1)}, bf16[2,256,128]{2,1,0:T(8,128)(2,1)S(1)}, u32[]{:S(2)}, u32[]{:S(2)}) collective-permute-start(bf16[2,256,128]{2,1,0:T(8,128)(2,1)S(1)} %pad_maximum_fusion), channel_id=1, source_target_pairs={{0,2},{1,3},{2,0},{3,1},{4,6},{5,7},{6,4},{7,5},{8,10},{9,11},{10,... | collective-permute-start | bytes 393224 | tf_op jit(solution)/shard_map/ppermute | solution.py:182
  36.6 16.8 %collective-permute-start.15 = (bf16[2,256,128]{2,1,0:T(8,128)(2,1)S(1)}, bf16[2,256,128]{2,1,0:T(8,128)(2,1)S(1)}, u32[]{:S(2)}, u32[]{:S(2)}) collective-permute-start(bf16[2,256,128]{2,1,0:T(8,128)(2,1)S(1)} %pad_maximum_fusion.1), channel_id=1, source_target_pairs={{0,4},{1,5},{2,6},{3,7},{4,0},{5,1},{6,2},{7,3},{8,12},{9,13},{10,... | collective-permute-start | bytes 393224 | tf_op jit(solution)/shard_map/ppermute | solution.py:182
  37.1 20.7 %collective-permute-start.16 = (bf16[2,256,128]{2,1,0:T(8,128)(2,1)S(1)}, bf16[2,256,128]{2,1,0:T(8,128)(2,1)S(1)}, u32[]{:S(2)}, u32[]{:S(2)}) collective-permute-start(bf16[2,256,128]{2,1,0:T(8,128)(2,1)S(1)} %pad_maximum_fusion.2), channel_id=1, source_target_pairs={{0,6},{1,7},{2,4},{3,5},{4,2},{5,3},{6,0},{7,1},{8,14},{9,15},{10,... | collective-permute-start | bytes 393224 | tf_op jit(solution)/shard_map/ppermute | solution.py:182
  43.9 18.3 %collective-permute-start.17 = (bf16[2,256,128]{2,1,0:T(8,128)(2,1)S(1)}, bf16[2,256,128]{2,1,0:T(8,128)(2,1)S(1)}, u32[]{:S(2)}, u32[]{:S(2)}) collective-permute-start(bf16[2,256,128]{2,1,0:T(8,128)(2,1)S(1)} %get-tuple-element.84), channel_id=1, source_target_pairs={{0,4},{1,5},{2,6},{3,7},{4,0},{5,1},{6,2},{7,3},{8,12},{9,13},{10,... | collective-permute-start | bytes 393224 | tf_op jit(solution)/shard_map/ppermute | solution.py:182
  44.2 18.8 %collective-permute-start.19 = (bf16[2,256,128]{2,1,0:T(8,128)(2,1)S(1)}, bf16[2,256,128]{2,1,0:T(8,128)(2,1)S(1)}, u32[]{:S(2)}, u32[]{:S(2)}) collective-permute-start(bf16[2,256,128]{2,1,0:T(8,128)(2,1)S(1)} %get-tuple-element.86), channel_id=1, source_target_pairs={{0,6},{1,7},{2,4},{3,5},{4,2},{5,3},{6,0},{7,1},{8,14},{9,15},{10,... | collective-permute-start | bytes 393224 | tf_op jit(solution)/shard_map/ppermute | solution.py:182
  46.5 16.5 %collective-permute-start.21 = (bf16[2,256,128]{2,1,0:T(8,128)(2,1)S(1)}, bf16[2,256,128]{2,1,0:T(8,128)(2,1)S(1)}, u32[]{:S(2)}, u32[]{:S(2)}) collective-permute-start(bf16[2,256,128]{2,1,0:T(8,128)(2,1)S(1)} %get-tuple-element.82), channel_id=1, source_target_pairs={{0,2},{1,3},{2,0},{3,1},{4,6},{5,7},{6,4},{7,5},{8,10},{9,11},{10,... | collective-permute-start | bytes 393224 | tf_op jit(solution)/shard_map/ppermute | solution.py:182
  53.5 4.3 %collective-permute-start.14 = (bf16[1,256,128]{2,1,0:T(8,128)(2,1)S(1)}, bf16[1,256,128]{2,1,0:T(8,128)(2,1)S(1)}, u32[]{:S(2)}, u32[]{:S(2)}) collective-permute-start(bf16[1,256,128]{2,1,0:T(8,128)(2,1)S(1)} %get-tuple-element.92), channel_id=1, source_target_pairs={{0,1},{1,0},{2,3},{3,2},{4,5},{5,4},{6,7},{7,6},{8,9},{9,8},{10,11... | collective-permute-start | bytes 196616 | tf_op jit(solution)/shard_map/ppermute | solution.py:177
  62.3 4.2 %collective-permute-start.18 = (bf16[1,256,128]{2,1,0:T(8,128)(2,1)S(1)}, bf16[1,256,128]{2,1,0:T(8,128)(2,1)S(1)}, u32[]{:S(2)}, u32[]{:S(2)}) collective-permute-start(bf16[1,256,128]{2,1,0:T(8,128)(2,1)S(1)} %slice.33), channel_id=1, source_target_pairs={{0,1},{1,0},{2,3},{3,2},{4,5},{5,4},{6,7},{7,6},{8,9},{9,8},{10,11... | collective-permute-start | bytes 196616 | tf_op jit(solution)/shard_map/ppermute | solution.py:177
  63.0 1.4 %collective-permute-start.23 = (bf16[1,256,128]{2,1,0:T(8,128)(2,1)S(1)}, bf16[1,256,128]{2,1,0:T(8,128)(2,1)S(1)}, u32[]{:S(2)}, u32[]{:S(2)}) collective-permute-start(bf16[1,256,128]{2,1,0:T(8,128)(2,1)S(1)} %slice.36), channel_id=1, source_target_pairs={{0,1},{1,0},{2,3},{3,2},{4,5},{5,4},{6,7},{7,6},{8,9},{9,8},{10,11... | collective-permute-start | bytes 196616 | tf_op jit(solution)/shard_map/ppermute | solution.py:177
  63.5 3.0 %collective-permute-start.20 = (bf16[1,256,128]{2,1,0:T(8,128)(2,1)S(1)}, bf16[1,256,128]{2,1,0:T(8,128)(2,1)S(1)}, u32[]{:S(2)}, u32[]{:S(2)}) collective-permute-start(bf16[1,256,128]{2,1,0:T(8,128)(2,1)S(1)} %slice.34), channel_id=1, source_target_pairs={{0,1},{1,0},{2,3},{3,2},{4,5},{5,4},{6,7},{7,6},{8,9},{9,8},{10,11... | collective-permute-start | bytes 196616 | tf_op jit(solution)/shard_map/ppermute | solution.py:177
  70.2 5.4 %collective-permute-start.24 = (f32[2,3,16,128]{3,2,1,0:T(8,128)S(1)}, f32[2,3,16,128]{3,2,1,0:T(8,128)S(1)}, u32[]{:S(2)}, u32[]{:S(2)}) collective-permute-start(f32[2,3,16,128]{3,2,1,0:T(8,128)S(1)} %get-tuple-element.101.refs_2_), channel_id=1, source_target_pairs={{0,8},{8,16},{16,24},{24,0},{1,9},{9,17},{17,25},{25,1},{2,10},{10... | collective-permute-start | bytes 147464 | tf_op jit(solution)/shard_map/ppermute | solution.py:598
  71.7 4.2 %collective-permute-start.25 = (f32[2,3,16,128]{3,2,1,0:T(8,128)S(1)}, f32[2,3,16,128]{3,2,1,0:T(8,128)S(1)}, u32[]{:S(2)}, u32[]{:S(2)}) collective-permute-start(f32[2,3,16,128]{3,2,1,0:T(8,128)S(1)} %get-tuple-element.101.refs_2_), channel_id=1, source_target_pairs={{0,16},{8,24},{16,0},{24,8},{1,17},{9,25},{17,1},{25,9},{2,18},{10... | collective-permute-start | bytes 147464 | tf_op jit(solution)/shard_map/ppermute | solution.py:598
  73.2 4.1 %collective-permute-start.26 = (f32[2,3,16,128]{3,2,1,0:T(8,128)S(1)}, f32[2,3,16,128]{3,2,1,0:T(8,128)S(1)}, u32[]{:S(2)}, u32[]{:S(2)}) collective-permute-start(f32[2,3,16,128]{3,2,1,0:T(8,128)S(1)} %get-tuple-element.101.refs_2_), channel_id=1, source_target_pairs={{0,24},{8,0},{16,8},{24,16},{1,25},{9,1},{17,9},{25,17},{2,26},{10... | collective-permute-start | bytes 147464 | tf_op jit(solution)/shard_map/ppermute | solution.py:598
  (10 other events, 60.4 us)

commit v6 on v5

--- a/solution.py
+++ b/solution.py
@@ -352,12 +352,11 @@
     nears, fars, chunk, room, me_ref, items_ref, sizes_ref, asked_ref, beside_ref, blocks, *refs
 ):
     tile, near, far = refs[0], refs[1 : 1 + nears], refs[1 + nears : 1 + nears + fars]
-    begun, out, beside_tile, *messages, field, total = refs[1 + nears + fars :]
+    _, total, out, beside_tile, *messages, field = refs[1 + nears + fars :]
     own = out.shape[0]
     field[1] = tile[...]
     put_near(chunk, near, field)
     put_far(nears + 1, far, field)
-    total[...] = begun[...]
     run_list(both_lists(room, sizes_ref), items_ref, blocks, lambda f: field[f], [total])
     for t in range(own):
         out[t] = (blend * total[t]).astype(out.dtype)
@@ -376,21 +375,20 @@
     out = pl.pallas_call(
         functools.partial(step1_kernel, len(near), len(far), chunk, items.shape[0] // 3),
         out_shape=[
+            held(begun.shape, begun.dtype),
             held((own, tile_rows, LANES), dtype),
             held((1, tile_rows, LANES), dtype),
         ]
         + [held((2, tile_rows, LANES), dtype)] * count,
         in_specs=[SMEM] * 5 + [VMEM] * (3 + len(near) + len(far)),
-        out_specs=[VMEM] * (2 + count),
-        scratch_shapes=[
-            pltpu.VMEM((n, tile_rows, LANES), dtype),
-            pltpu.VMEM(begun.shape, begun.dtype),
-        ],
+        out_specs=[VMEM] * (3 + count),
+        input_output_aliases={7 + len(near) + len(far): 0},
+        scratch_shapes=[pltpu.VMEM((n, tile_rows, LANES), dtype)],
         compiler_params=PARAMS,
         cost_estimate=COST,
         name="step1",
     )(me, items, sizes, asked, beside, blocks, tile, *near, *far, begun)
-    return out[0], out[1], out[2:]
+    return out[1], out[2], out[3:]
 
 
 def near_kernel(nears, room, items_ref, sizes_ref, blocks, *refs):
@@ -427,15 +425,14 @@
 
 def step2_kernel(gots, count, live, whole, room, items_ref, sizes_ref, blocks, *refs):
     got, arrived = refs[:gots], refs[gots : gots + count]
-    begun, wide_ref = refs[gots + count : gots + count + 2]
-    *earlier, expo_ref, stats_ref, field, total = refs[gots + count + 2 :]
+    _, wide_ref = refs[gots + count : gots + count + 2]
+    *earlier, total, expo_ref, stats_ref, field = refs[gots + count + 2 :]
     own, tile_rows = expo_ref.shape[:2]
     if whole:
         field[1] = got[0][0]
         put_far(1, arrived, field)
     else:
         put_pairs(field.shape[0] // 2 - count, arrived, got, field)
-    total[...] = begun[...]
     which = (both_lists if whole else far_list)(room, sizes_ref)
     run_list(which, items_ref, blocks, lambda f: field[f], [total])
     parts = tile_rows // LANES
@@ -467,24 +464,24 @@
     own, tile_rows = begun.shape[0] - 1, begun.shape[1]
     before = () if earlier is None else (earlier,)
     count = 1 + (earlier.shape[0] if before else 0)
-    return pl.pallas_call(
+    out = pl.pallas_call(
         functools.partial(
             step2_kernel, len(got), len(arrived), live, whole, items.shape[0] // 3
         ),
         out_shape=[
+            held(begun.shape, begun.dtype),
             held((own, tile_rows, LANES), jnp.float32),
             held((count, 3, own * tile_rows // LANES, LANES), jnp.float32),
         ],
         in_specs=[SMEM] * 2 + [VMEM] * (3 + len(got) + len(arrived) + len(before)),
-        out_specs=[VMEM] * 2,
-        scratch_shapes=[
-            pltpu.VMEM((n, tile_rows, LANES), got[0].dtype),
-            pltpu.VMEM(begun.shape, begun.dtype),
-        ],
+        out_specs=[VMEM] * 3,
+        input_output_aliases={3 + len(got) + len(arrived): 0},
+        scratch_shapes=[pltpu.VMEM((n, tile_rows, LANES), got[0].dtype)],
         compiler_params=PARAMS,
         cost_estimate=COST,
         name="step2",
     )(items, sizes, blocks, *got, *arrived, begun, wide, *before)
+    return out[1:]
 
 
 def finish_kernel(chunks, parts, *refs):

time: 78.7 us -> 79.1 us (level)
  the two profiles are of different devices: /device:TPU:16 before, /device:TPU:0 now
where the time goes in v6:
time: 79.1 us; the launch traced here: 78.8 us
  Pallas kernels  33.9 us (43%)
  starting transfers between devices  32.3 us (41%)
  waiting for transfers between devices  10.3 us (13%)
  local copies, waits for them, and re-layouts  1.31 us (2%)
  between operations  0.92 us (1%)
    ppermute x14, starting transfers between devices, send(): lax.ppermute(part, 'rows', [(i, i ^ 2 * k) for i in range(n)])  25.8 us
    pallas_call x1, Pallas kernels, begin(): pl.pallas_call(functools.partial(begin_kernel, items.shape[0] // 3), out_...  8.31 us
    pallas_call x2, Pallas kernels, step2(): pl.pallas_call(functools.partial(step2_kernel, len(got), len(arrived), li...  6.61 us
    ppermute x14, waiting for transfers between devices, send(): lax.ppermute(part, 'rows', [(i, i ^ 2 * k) for i in range(n)])  6.11 us
    pallas_call x2, Pallas kernels, step1(): pl.pallas_call(functools.partial(step1_kernel, len(near), len(far), chunk...  6.05 us
    pallas_call x1, Pallas kernels, own_part(): pl.pallas_call(functools.partial(own_kernel, chunks, items.shape[0] // 3)...  5.06 us
    ppermute x3, starting transfers between devices, local(): lax.ppermute(stats, 'cls', [(i, (i + k) % parts) for i in range(parts)])  4.46 us
    pallas_call x1, Pallas kernels, prepare(): pl.pallas_call(functools.partial(prepare_kernel, room), out_shape=[sds((3...  3.2 us
  transfers between devices with their start and end apart: 27, of which 11 were waited for; matrix products, arithmetic and copies ran while one was open for 0% of the time, Pallas kernels for 36%

profile of v6, /device:TPU:0, one launch (start us, length us, event | category | flops | bytes accessed | tf_op | source)
XLA Modules:
  0.0 78.8 jit_solution(155206367137576586)
XLA Ops:
  1.2 4.7 %collective-permute-start = (s32[8]{0:T(128)}, s32[8]{0:T(128)S(1)}, u32[]{:S(2)}, u32[]{:S(2)}) collective-permute-start(s32[8]{0:T(128)} %bitcast.15), channel_id=1, source_target_pairs={{0,6},{1,7},{2,4},{3,5},{4,2},{5,3},{6,0},{7,1},{8,14},{9,15},{10,... | collective-permute-start | bytes 104 | tf_op jit(solution)/shard_map/ppermute | solution.py:182
  6.5 1.2 %copy-done = bf16[2048,250]{1,0:T(8,128)(2,1)S(1)} copy-done((bf16[2048,250]{1,0:T(8,128)(2,1)S(1)}, bf16[2048,250]{1,0:T(8,128)(2,1)}, u32[]{:S(2)}) %copy-start) | copy-done | bytes 1024024
  8.3 2.1 %collective-permute-done.1.refs_1_ = s32[8]{0:T(128)S(1)} collective-permute-done((s32[8]{0:T(128)}, s32[8]{0:T(128)S(1)}, u32[]{:S(2)}, u32[]{:S(2)}) %collective-permute-start.1) | collective-permute-done | bytes 64 | tf_op jit(solution)/shard_map/ppermute | solution.py:182
  10.4 1.2 %pick.1 = (s32[4,8]{1,0:T(4,128)S(1)}, bf16[256,128]{1,0:T(8,128)(2,1)S(1)}, bf16[256,128]{1,0:T(8,128)(2,1)S(1)}, bf16[4,256,128]{2,1,0:T(8,128)(2,1)S(1)}, bf1...) custom-call(s32[2]{0:T(128)S(1)} %pad_add_fusion.me_ref, ...), custom_call_target="tpu_custom_call" | custom-call | tf_op jit(solution)/shard_map/pick/pallas_call | solution.py:152
  11.7 2.2 %collective-permute-start.6 = (bf16[2,256,128]{2,1,0:T(8,128)(2,1)S(1)}, bf16[2,256,128]{2,1,0:T(8,128)(2,1)S(1)}, u32[]{:S(2)}, u32[]{:S(2)}) collective-permute-start(bf16[2,256,128]{2,1,0:T(8,128)(2,1)S(1)} %get-tuple-element.58), channel_id=1, source_target_pairs={{0,4},{1,5},{2,6},{3,7},{4,0},{5,1},{6,2},{7,3},{8,12},{9,13},{10,... | collective-permute-start | bytes 393224 | tf_op jit(solution)/shard_map/ppermute | solution.py:182
  13.9 2.1 %collective-permute-start.7 = (bf16[2,256,128]{2,1,0:T(8,128)(2,1)S(1)}, bf16[2,256,128]{2,1,0:T(8,128)(2,1)S(1)}, u32[]{:S(2)}, u32[]{:S(2)}) collective-permute-start(bf16[2,256,128]{2,1,0:T(8,128)(2,1)S(1)} %get-tuple-element.59), channel_id=1, source_target_pairs={{0,6},{1,7},{2,4},{3,5},{4,2},{5,3},{6,0},{7,1},{8,14},{9,15},{10,... | collective-permute-start | bytes 393224 | tf_op jit(solution)/shard_map/ppermute | solution.py:182
  16.1 3.2 %prepare.1 = (s32[624]{0:T(1024)S(1)}, s32[4]{0:T(128)S(1)}) custom-call(s32[2]{0:T(128)S(1)} %pad_add_fusion.me_ref, s32[8,24]{1,0:T(8,128)S(1)} %copy-done.4, s32[8]{0:T(128)S(1)} %copy-done.5, s32[8]{0:T(128)S(1)} %bitcast.19), custom_call_target="tpu_custom_call" | custom-call | flops 1 | bytes 1 | tf_op jit(solution)/shard_map/prepare/pallas_call | solution.py:243
  19.3 2.1 %collective-permute-start.9 = (bf16[2,256,128]{2,1,0:T(8,128)(2,1)S(1)}, bf16[2,256,128]{2,1,0:T(8,128)(2,1)S(1)}, u32[]{:S(2)}, u32[]{:S(2)}) collective-permute-start(bf16[2,256,128]{2,1,0:T(8,128)(2,1)S(1)} %get-tuple-element.67), channel_id=1, source_target_pairs={{0,6},{1,7},{2,4},{3,5},{4,2},{5,3},{6,0},{7,1},{8,14},{9,15},{10,... | collective-permute-start | bytes 393224 | tf_op jit(solution)/shard_map/ppermute | solution.py:182
  21.5 8.3 %begin.1 = (bf16[192,256,256]{2,1,0:T(8,128)(2,1)S(1)}, f32[9,256,128]{2,1,0:T(8,128)S(1)}, f32[9,256,128]{2,1,0:T(8,128)S(1)}) custom-call(s32[2]{0:T(128)S(1)} %pad_add_fusion.me_ref, s32[624]{0:T(1024)S(1)} %get-tuple-element.63.items_ref, s32[4]{0:T(128)S(1)} %get-tuple-element.64.sizes_ref, s32[8]{0:T(128)S(1)} %copy-done.5, ...), custom_call_target="tpu_custom_call" | custom-call | flops 1 | bytes 1 | tf_op jit(solution)/shard_map/begin/pallas_call | solution.py:289
  29.9 3.0 %step1.2 = (f32[9,256,128]{2,1,0:T(8,128)S(1)}, bf16[8,256,128]{2,1,0:T(8,128)(2,1)S(1)}, bf16[1,256,128]{2,1,0:T(8,128)(2,1)S(1)}, bf16[2,256,128]{2,1,0:T(8,12...) custom-call(s32[2]{0:T(128)S(1)} %pad_add_fusion.me_ref, ...), custom_call_target="tpu_custom_call", output_to_operand_aliasing={{0}: (10, {})} | custom-call | flops 1 | bytes 1 | tf_op jit(solution)/shard_map/step1/pallas_call | solution.py:375
  34.9 3.2 %collective-permute-start.13 = (bf16[2,256,128]{2,1,0:T(8,128)(2,1)S(1)}, bf16[2,256,128]{2,1,0:T(8,128)(2,1)S(1)}, u32[]{:S(2)}, u32[]{:S(2)}) collective-permute-start(bf16[2,256,128]{2,1,0:T(8,128)(2,1)S(1)} %pad_maximum_fusion), channel_id=1, source_target_pairs={{0,2},{1,3},{2,0},{3,1},{4,6},{5,7},{6,4},{7,5},{8,10},{9,11},{10,... | collective-permute-start | bytes 393224 | tf_op jit(solution)/shard_map/ppermute | solution.py:182
  38.2 4.6 %collective-permute-start.16 = (bf16[2,256,128]{2,1,0:T(8,128)(2,1)S(1)}, bf16[2,256,128]{2,1,0:T(8,128)(2,1)S(1)}, u32[]{:S(2)}, u32[]{:S(2)}) collective-permute-start(bf16[2,256,128]{2,1,0:T(8,128)(2,1)S(1)} %pad_maximum_fusion.2), channel_id=1, source_target_pairs={{0,6},{1,7},{2,4},{3,5},{4,2},{5,3},{6,0},{7,1},{8,14},{9,15},{10,... | collective-permute-start | bytes 393224 | tf_op jit(solution)/shard_map/ppermute | solution.py:182
  42.8 3.0 %step1.3 = (f32[9,256,128]{2,1,0:T(8,128)S(1)}, bf16[8,256,128]{2,1,0:T(8,128)(2,1)S(1)}, bf16[1,256,128]{2,1,0:T(8,128)(2,1)S(1)}, bf16[2,256,128]{2,1,0:T(8,12...) custom-call(s32[2]{0:T(128)S(1)} %pad_add_fusion.me_ref, ...), custom_call_target="tpu_custom_call", output_to_operand_aliasing={{0}: (10, {})} | custom-call | flops 1 | bytes 1 | tf_op jit(solution)/shard_map/step1/pallas_call | solution.py:375
  46.5 5.3 %collective-permute-start.19 = (bf16[2,256,128]{2,1,0:T(8,128)(2,1)S(1)}, bf16[2,256,128]{2,1,0:T(8,128)(2,1)S(1)}, u32[]{:S(2)}, u32[]{:S(2)}) collective-permute-start(bf16[2,256,128]{2,1,0:T(8,128)(2,1)S(1)} %get-tuple-element.86), channel_id=1, source_target_pairs={{0,6},{1,7},{2,4},{3,5},{4,2},{5,3},{6,0},{7,1},{8,14},{9,15},{10,... | collective-permute-start | bytes 393224 | tf_op jit(solution)/shard_map/ppermute | solution.py:182
  51.8 5.1 %own_part.1 = (f32[8,256,128]{2,1,0:T(8,128)S(1)}, f32[9,256,128]{2,1,0:T(8,128)S(1)}, f32[9,256,128]{2,1,0:T(8,128)S(1)}) custom-call(s32[2]{0:T(128)S(1)} %pad_add_fusion.me_ref, s32[624]{0:T(1024)S(1)} %get-tuple-element.63.items_ref, s32[4]{0:T(128)S(1)} %get-tuple-element.64.sizes_ref, bf16[192,256,256]{2,1,0:T(8,128)(2,1)S(1)} %get-tuple-element.69.blocks, ...), custom_call_target="tpu_custom_call" | custom-call | flops 1 | bytes 1 | tf_op jit(solution)/shard_map/own_part/pallas_call | solution.py:320
  57.0 3.5 %collective-permute-done.15.refs_2_ = bf16[2,256,128]{2,1,0:T(8,128)(2,1)S(1)} collective-permute-done((bf16[2,256,128]{2,1,0:T(8,128)(2,1)S(1)}, bf16[2,256,128]{2,1,0:T(8,128)(2,1)S(1)}, u32[]{:S(2)}, u32[]{:S(2)}) %collective-permute-start.15) | collective-permute-done | bytes 131104 | tf_op jit(solution)/shard_map/ppermute | solution.py:182
  60.5 3.7 %step2.2 = (f32[9,256,128]{2,1,0:T(8,128)S(1)}, f32[8,256,128]{2,1,0:T(8,128)S(1)}, f32[1,3,16,128]{3,2,1,0:T(8,128)S(1)}) custom-call(s32[624]{0:T(1024)S(1)} %get-tuple-element.63.items_ref, s32[4]{0:T(128)S(1)} %get-tuple-element.64.sizes_ref, bf16[192,256,256]{2,1,0:T(8,128)(2,1)S(1)} %get-tuple-element.69.blocks, ...), custom_call_target="tpu_custom_call", output_to_operand_aliasing={{0}: (7, {})} | custom-call | flops 1 | bytes 1 | tf_op jit(solution)/shard_map/step2/pallas_call | solution.py:467
  65.7 1.3 %near_part.1.refs_4_ = f32[9,256,128]{2,1,0:T(8,128)S(1)} custom-call(s32[624]{0:T(1024)S(1)} %get-tuple-element.63.items_ref, s32[4]{0:T(128)S(1)} %get-tuple-element.64.sizes_ref, bf16[192,256,256]{2,1,0:T(8,128)(2,1)S(1)} %get-tuple-element.69.blocks, bf16[1,256,128]{2,1,0:T(8,128)(2,1)S(1)} %collective-permute-done.22.refs_0_, ...), custom_call_target="tpu_custom_call", output_to_operand_aliasing={{}: (6, {})} | custom-call | flops 1 | bytes 1 | tf_op jit(solution)/shard_map/near_part/pallas_call | solution.py:403
  67.0 2.9 %step2.3 = (f32[9,256,128]{2,1,0:T(8,128)S(1)}, f32[8,256,128]{2,1,0:T(8,128)S(1)}, f32[2,3,16,128]{3,2,1,0:T(8,128)S(1)}) custom-call(s32[624]{0:T(1024)S(1)} %get-tuple-element.63.items_ref, s32[4]{0:T(128)S(1)} %get-tuple-element.64.sizes_ref, bf16[192,256,256]{2,1,0:T(8,128)(2,1)S(1)} %get-tuple-element.69.blocks, ...), custom_call_target="tpu_custom_call", output_to_operand_aliasing={{0}: (7, {})} | custom-call | flops 1 | bytes 1 | tf_op jit(solution)/shard_map/step2/pallas_call | solution.py:467
  70.0 1.5 %collective-permute-start.24 = (f32[2,3,16,128]{3,2,1,0:T(8,128)S(1)}, f32[2,3,16,128]{3,2,1,0:T(8,128)S(1)}, u32[]{:S(2)}, u32[]{:S(2)}) collective-permute-start(f32[2,3,16,128]{3,2,1,0:T(8,128)S(1)} %get-tuple-element.101.refs_2_), channel_id=1, source_target_pairs={{0,8},{8,16},{16,24},{24,0},{1,9},{9,17},{17,25},{25,1},{2,10},{10... | collective-permute-start | bytes 147464 | tf_op jit(solution)/shard_map/ppermute | solution.py:595
  71.5 1.5 %collective-permute-start.25 = (f32[2,3,16,128]{3,2,1,0:T(8,128)S(1)}, f32[2,3,16,128]{3,2,1,0:T(8,128)S(1)}, u32[]{:S(2)}, u32[]{:S(2)}) collective-permute-start(f32[2,3,16,128]{3,2,1,0:T(8,128)S(1)} %get-tuple-element.101.refs_2_), channel_id=1, source_target_pairs={{0,16},{8,24},{16,0},{24,8},{1,17},{9,25},{17,1},{25,9},{2,18},{10... | collective-permute-start | bytes 147464 | tf_op jit(solution)/shard_map/ppermute | solution.py:595
  73.0 1.4 %collective-permute-start.26 = (f32[2,3,16,128]{3,2,1,0:T(8,128)S(1)}, f32[2,3,16,128]{3,2,1,0:T(8,128)S(1)}, u32[]{:S(2)}, u32[]{:S(2)}) collective-permute-start(f32[2,3,16,128]{3,2,1,0:T(8,128)S(1)} %get-tuple-element.101.refs_2_), channel_id=1, source_target_pairs={{0,24},{8,0},{16,8},{24,16},{1,25},{9,1},{17,9},{25,17},{2,26},{10... | collective-permute-start | bytes 147464 | tf_op jit(solution)/shard_map/ppermute | solution.py:595
  75.4 1.1 %collective-permute-done.25.refs_4_ = f32[2,3,16,128]{3,2,1,0:T(8,128)S(1)} collective-permute-done((f32[2,3,16,128]{3,2,1,0:T(8,128)S(1)}, f32[2,3,16,128]{3,2,1,0:T(8,128)S(1)}, u32[]{:S(2)}, u32[]{:S(2)}) %collective-permute-start.25) | collective-permute-done | bytes 49184 | tf_op jit(solution)/shard_map/ppermute | solution.py:595
  77.2 1.6 %finish.1 = (bf16[2048,250]{1,0:T(8,128)(2,1)}, f32[16,128]{1,0:T(8,128)}) custom-call(f32[8,256,128]{2,1,0:T(8,128)S(1)} %get-tuple-element.94.refs_0_, f32[8,256,128]{2,1,0:T(8,128)S(1)} %get-tuple-element.100.refs_1_, f32[2,3,16,128]{3,2,1,0:T(8,128)S(1)} %get-tuple-element.101.refs_2_, f32[2,3,16,128]{3,2,1,0:T(8,128)S(1)} %collective-permute-done.24.refs_3_, ...), custom_call_target="tpu_custom_call" | custom-call | tf_op jit(solution)/shard_map/finish/pallas_call | solution.py:518
  (66 shorter events, 7.7 us)
Async XLA Ops:
  0.6 7.4 %collective-permute-start.3 = (bf16[2048,250]{1,0:T(8,128)(2,1)}, bf16[2048,250]{1,0:T(8,128)(2,1)S(1)}, u32[]{:S(2)}, u32[]{:S(2)}) collective-permute-start(bf16[2048,250]{1,0:T(8,128)(2,1)} %param.7), channel_id=1, source_target_pairs={{0,1},{1,0},{2,3},{3,2},{4,5},{5,4},{6,7},{7,6},{8,9},{9,8},{10,11... | collective-permute-start | bytes 3072008 | tf_op jit(solution)/shard_map/ppermute | solution.py:177
  1.2 7.1 %collective-permute-start = (s32[8]{0:T(128)}, s32[8]{0:T(128)S(1)}, u32[]{:S(2)}, u32[]{:S(2)}) collective-permute-start(s32[8]{0:T(128)} %bitcast.15), channel_id=1, source_target_pairs={{0,6},{1,7},{2,4},{3,5},{4,2},{5,3},{6,0},{7,1},{8,14},{9,15},{10,... | collective-permute-start | bytes 104 | tf_op jit(solution)/shard_map/ppermute | solution.py:182
  5.8 4.6 %collective-permute-start.1 = (s32[8]{0:T(128)}, s32[8]{0:T(128)S(1)}, u32[]{:S(2)}, u32[]{:S(2)}) collective-permute-start(s32[8]{0:T(128)} %bitcast.16), channel_id=1, source_target_pairs={{0,4},{1,5},{2,6},{3,7},{4,0},{5,1},{6,2},{7,3},{8,12},{9,13},{10,... | collective-permute-start | bytes 104 | tf_op jit(solution)/shard_map/ppermute | solution.py:182
  5.8 4.6 %collective-permute-start.2 = (s32[8]{0:T(128)}, s32[8]{0:T(128)S(1)}, u32[]{:S(2)}, u32[]{:S(2)}) collective-permute-start(s32[8]{0:T(128)} %bitcast.17), channel_id=1, source_target_pairs={{0,2},{1,3},{2,0},{3,1},{4,6},{5,7},{6,4},{7,5},{8,10},{9,11},{10,... | collective-permute-start | bytes 104 | tf_op jit(solution)/shard_map/ppermute | solution.py:182
  11.6 18.2 %collective-permute-start.5 = (bf16[4,256,128]{2,1,0:T(8,128)(2,1)S(1)}, bf16[4,256,128]{2,1,0:T(8,128)(2,1)S(1)}, u32[]{:S(2)}, u32[]{:S(2)}) collective-permute-start(bf16[4,256,128]{2,1,0:T(8,128)(2,1)S(1)} %get-tuple-element.57), channel_id=1, source_target_pairs={{0,2},{1,3},{2,0},{3,1},{4,6},{5,7},{6,4},{7,5},{8,10},{9,11},{10,... | collective-permute-start | bytes 786440 | tf_op jit(solution)/shard_map/ppermute | solution.py:182
  11.7 18.1 %collective-permute-start.6 = (bf16[2,256,128]{2,1,0:T(8,128)(2,1)S(1)}, bf16[2,256,128]{2,1,0:T(8,128)(2,1)S(1)}, u32[]{:S(2)}, u32[]{:S(2)}) collective-permute-start(bf16[2,256,128]{2,1,0:T(8,128)(2,1)S(1)} %get-tuple-element.58), channel_id=1, source_target_pairs={{0,4},{1,5},{2,6},{3,7},{4,0},{5,1},{6,2},{7,3},{8,12},{9,13},{10,... | collective-permute-start | bytes 393224 | tf_op jit(solution)/shard_map/ppermute | solution.py:182
  13.9 15.9 %collective-permute-start.7 = (bf16[2,256,128]{2,1,0:T(8,128)(2,1)S(1)}, bf16[2,256,128]{2,1,0:T(8,128)(2,1)S(1)}, u32[]{:S(2)}, u32[]{:S(2)}) collective-permute-start(bf16[2,256,128]{2,1,0:T(8,128)(2,1)S(1)} %get-tuple-element.59), channel_id=1, source_target_pairs={{0,6},{1,7},{2,4},{3,5},{4,2},{5,3},{6,0},{7,1},{8,14},{9,15},{10,... | collective-permute-start | bytes 393224 | tf_op jit(solution)/shard_map/ppermute | solution.py:182
  16.1 3.2 %collective-permute-start.4 = (s32[4,8]{1,0:T(4,128)S(1)}, s32[4,8]{1,0:T(4,128)S(1)}, u32[]{:S(2)}, u32[]{:S(2)}) collective-permute-start(s32[4,8]{1,0:T(4,128)S(1)} %get-tuple-element.65.asked_ref), channel_id=1, source_target_pairs={{0,1},{1,0},{2,3},{3,2},{4,5},{5,4},{6,7},{7,6},{8,9},{9,8},{10,11... | collective-permute-start | bytes 392 | tf_op jit(solution)/shard_map/ppermute | solution.py:177
  19.3 23.5 %collective-permute-start.9 = (bf16[2,256,128]{2,1,0:T(8,128)(2,1)S(1)}, bf16[2,256,128]{2,1,0:T(8,128)(2,1)S(1)}, u32[]{:S(2)}, u32[]{:S(2)}) collective-permute-start(bf16[2,256,128]{2,1,0:T(8,128)(2,1)S(1)} %get-tuple-element.67), channel_id=1, source_target_pairs={{0,6},{1,7},{2,4},{3,5},{4,2},{5,3},{6,0},{7,1},{8,14},{9,15},{10,... | collective-permute-start | bytes 393224 | tf_op jit(solution)/shard_map/ppermute | solution.py:182
  21.4 21.4 %collective-permute-start.8 = (bf16[2,256,128]{2,1,0:T(8,128)(2,1)S(1)}, bf16[2,256,128]{2,1,0:T(8,128)(2,1)S(1)}, u32[]{:S(2)}, u32[]{:S(2)}) collective-permute-start(bf16[2,256,128]{2,1,0:T(8,128)(2,1)S(1)} %get-tuple-element.66), channel_id=1, source_target_pairs={{0,4},{1,5},{2,6},{3,7},{4,0},{5,1},{6,2},{7,3},{8,12},{9,13},{10,... | collective-permute-start | bytes 393224 | tf_op jit(solution)/shard_map/ppermute | solution.py:182
  33.0 1.5 %collective-permute-start.11 = (bf16[1,256,128]{2,1,0:T(8,128)(2,1)S(1)}, bf16[1,256,128]{2,1,0:T(8,128)(2,1)S(1)}, u32[]{:S(2)}, u32[]{:S(2)}) collective-permute-start(bf16[1,256,128]{2,1,0:T(8,128)(2,1)S(1)} %get-tuple-element.107), channel_id=1, source_target_pairs={{0,1},{1,0},{2,3},{3,2},{4,5},{5,4},{6,7},{7,6},{8,9},{9,8},{10,11... | collective-permute-start | bytes 196616 | tf_op jit(solution)/shard_map/ppermute | solution.py:177
  34.9 11.0 %collective-permute-start.13 = (bf16[2,256,128]{2,1,0:T(8,128)(2,1)S(1)}, bf16[2,256,128]{2,1,0:T(8,128)(2,1)S(1)}, u32[]{:S(2)}, u32[]{:S(2)}) collective-permute-start(bf16[2,256,128]{2,1,0:T(8,128)(2,1)S(1)} %pad_maximum_fusion), channel_id=1, source_target_pairs={{0,2},{1,3},{2,0},{3,1},{4,6},{5,7},{6,4},{7,5},{8,10},{9,11},{10,... | collective-permute-start | bytes 393224 | tf_op jit(solution)/shard_map/ppermute | solution.py:182
  38.2 18.7 %collective-permute-start.16 = (bf16[2,256,128]{2,1,0:T(8,128)(2,1)S(1)}, bf16[2,256,128]{2,1,0:T(8,128)(2,1)S(1)}, u32[]{:S(2)}, u32[]{:S(2)}) collective-permute-start(bf16[2,256,128]{2,1,0:T(8,128)(2,1)S(1)} %pad_maximum_fusion.2), channel_id=1, source_target_pairs={{0,6},{1,7},{2,4},{3,5},{4,2},{5,3},{6,0},{7,1},{8,14},{9,15},{10,... | collective-permute-start | bytes 393224 | tf_op jit(solution)/shard_map/ppermute | solution.py:182
  42.8 17.7 %collective-permute-start.15 = (bf16[2,256,128]{2,1,0:T(8,128)(2,1)S(1)}, bf16[2,256,128]{2,1,0:T(8,128)(2,1)S(1)}, u32[]{:S(2)}, u32[]{:S(2)}) collective-permute-start(bf16[2,256,128]{2,1,0:T(8,128)(2,1)S(1)} %pad_maximum_fusion.1), channel_id=1, source_target_pairs={{0,4},{1,5},{2,6},{3,7},{4,0},{5,1},{6,2},{7,3},{8,12},{9,13},{10,... | collective-permute-start | bytes 393224 | tf_op jit(solution)/shard_map/ppermute | solution.py:182
  45.9 18.3 %collective-permute-start.21 = (bf16[2,256,128]{2,1,0:T(8,128)(2,1)S(1)}, bf16[2,256,128]{2,1,0:T(8,128)(2,1)S(1)}, u32[]{:S(2)}, u32[]{:S(2)}) collective-permute-start(bf16[2,256,128]{2,1,0:T(8,128)(2,1)S(1)} %get-tuple-element.82), channel_id=1, source_target_pairs={{0,2},{1,3},{2,0},{3,1},{4,6},{5,7},{6,4},{7,5},{8,10},{9,11},{10,... | collective-permute-start | bytes 393224 | tf_op jit(solution)/shard_map/ppermute | solution.py:182
  46.5 18.2 %collective-permute-start.19 = (bf16[2,256,128]{2,1,0:T(8,128)(2,1)S(1)}, bf16[2,256,128]{2,1,0:T(8,128)(2,1)S(1)}, u32[]{:S(2)}, u32[]{:S(2)}) collective-permute-start(bf16[2,256,128]{2,1,0:T(8,128)(2,1)S(1)} %get-tuple-element.86), channel_id=1, source_target_pairs={{0,6},{1,7},{2,4},{3,5},{4,2},{5,3},{6,0},{7,1},{8,14},{9,15},{10,... | collective-permute-start | bytes 393224 | tf_op jit(solution)/shard_map/ppermute | solution.py:182
  51.8 13.6 %collective-permute-start.17 = (bf16[2,256,128]{2,1,0:T(8,128)(2,1)S(1)}, bf16[2,256,128]{2,1,0:T(8,128)(2,1)S(1)}, u32[]{:S(2)}, u32[]{:S(2)}) collective-permute-start(bf16[2,256,128]{2,1,0:T(8,128)(2,1)S(1)} %get-tuple-element.84), channel_id=1, source_target_pairs={{0,4},{1,5},{2,6},{3,7},{4,0},{5,1},{6,2},{7,3},{8,12},{9,13},{10,... | collective-permute-start | bytes 393224 | tf_op jit(solution)/shard_map/ppermute | solution.py:182
  56.9 3.6 %collective-permute-start.14 = (bf16[1,256,128]{2,1,0:T(8,128)(2,1)S(1)}, bf16[1,256,128]{2,1,0:T(8,128)(2,1)S(1)}, u32[]{:S(2)}, u32[]{:S(2)}) collective-permute-start(bf16[1,256,128]{2,1,0:T(8,128)(2,1)S(1)} %get-tuple-element.92), channel_id=1, source_target_pairs={{0,1},{1,0},{2,3},{3,2},{4,5},{5,4},{6,7},{7,6},{8,9},{9,8},{10,11... | collective-permute-start | bytes 196616 | tf_op jit(solution)/shard_map/ppermute | solution.py:177
  64.3 1.4 %collective-permute-start.23 = (bf16[1,256,128]{2,1,0:T(8,128)(2,1)S(1)}, bf16[1,256,128]{2,1,0:T(8,128)(2,1)S(1)}, u32[]{:S(2)}, u32[]{:S(2)}) collective-permute-start(bf16[1,256,128]{2,1,0:T(8,128)(2,1)S(1)} %slice.36), channel_id=1, source_target_pairs={{0,1},{1,0},{2,3},{3,2},{4,5},{5,4},{6,7},{7,6},{8,9},{9,8},{10,11... | collective-permute-start | bytes 196616 | tf_op jit(solution)/shard_map/ppermute | solution.py:177
  64.8 2.2 %collective-permute-start.20 = (bf16[1,256,128]{2,1,0:T(8,128)(2,1)S(1)}, bf16[1,256,128]{2,1,0:T(8,128)(2,1)S(1)}, u32[]{:S(2)}, u32[]{:S(2)}) collective-permute-start(bf16[1,256,128]{2,1,0:T(8,128)(2,1)S(1)} %slice.34), channel_id=1, source_target_pairs={{0,1},{1,0},{2,3},{3,2},{4,5},{5,4},{6,7},{7,6},{8,9},{9,8},{10,11... | collective-permute-start | bytes 196616 | tf_op jit(solution)/shard_map/ppermute | solution.py:177
  65.4 1.6 %collective-permute-start.18 = (bf16[1,256,128]{2,1,0:T(8,128)(2,1)S(1)}, bf16[1,256,128]{2,1,0:T(8,128)(2,1)S(1)}, u32[]{:S(2)}, u32[]{:S(2)}) collective-permute-start(bf16[1,256,128]{2,1,0:T(8,128)(2,1)S(1)} %slice.33), channel_id=1, source_target_pairs={{0,1},{1,0},{2,3},{3,2},{4,5},{5,4},{6,7},{7,6},{8,9},{9,8},{10,11... | collective-permute-start | bytes 196616 | tf_op jit(solution)/shard_map/ppermute | solution.py:177
  70.0 5.5 %collective-permute-start.24 = (f32[2,3,16,128]{3,2,1,0:T(8,128)S(1)}, f32[2,3,16,128]{3,2,1,0:T(8,128)S(1)}, u32[]{:S(2)}, u32[]{:S(2)}) collective-permute-start(f32[2,3,16,128]{3,2,1,0:T(8,128)S(1)} %get-tuple-element.101.refs_2_), channel_id=1, source_target_pairs={{0,8},{8,16},{16,24},{24,0},{1,9},{9,17},{17,25},{25,1},{2,10},{10... | collective-permute-start | bytes 147464 | tf_op jit(solution)/shard_map/ppermute | solution.py:595
  71.5 5.1 %collective-permute-start.25 = (f32[2,3,16,128]{3,2,1,0:T(8,128)S(1)}, f32[2,3,16,128]{3,2,1,0:T(8,128)S(1)}, u32[]{:S(2)}, u32[]{:S(2)}) collective-permute-start(f32[2,3,16,128]{3,2,1,0:T(8,128)S(1)} %get-tuple-element.101.refs_2_), channel_id=1, source_target_pairs={{0,16},{8,24},{16,0},{24,8},{1,17},{9,25},{17,1},{25,9},{2,18},{10... | collective-permute-start | bytes 147464 | tf_op jit(solution)/shard_map/ppermute | solution.py:595
  73.0 4.2 %collective-permute-start.26 = (f32[2,3,16,128]{3,2,1,0:T(8,128)S(1)}, f32[2,3,16,128]{3,2,1,0:T(8,128)S(1)}, u32[]{:S(2)}, u32[]{:S(2)}) collective-permute-start(f32[2,3,16,128]{3,2,1,0:T(8,128)S(1)} %get-tuple-element.101.refs_2_), channel_id=1, source_target_pairs={{0,24},{8,0},{16,8},{24,16},{1,25},{9,1},{17,9},{25,17},{2,26},{10... | collective-permute-start | bytes 147464 | tf_op jit(solution)/shard_map/ppermute | solution.py:595
  (10 other events, 66.2 us)
